TPU v7x, 256 devices: a whole 4x4x8 slice. The times are simulated.
256 devices in a mesh: gx: 16 (over y, z_lo), gy: 16 (over x, z_hi, core).
Axes of the slice: x: 4, y: 4, z: 8 (z_hi: 2, z_lo: 4; z = z_hi * 4 + z_lo), core: 2. Of those that a mesh axis runs over, the one named last changes fastest.
Arguments:
- water_depth: float32 [2048, 8192], P('gx', 'gy'), may hold values from 0.5 to 2
- momentum_x: float32 [2048, 8192], P('gx', 'gy'), may hold values from -1.5 to 1.5
- momentum_y: float32 [2048, 8192], P('gx', 'gy'), may hold values from -1.5 to 1.5
- wet_mask: int32 [2048, 8192], P('gx', 'gy'), may hold values from 0 to 1, as said below
- damage_class: int32 [2048, 8192], P('gx', 'gy'), may hold values from 0 to 7
- damage_rates: float32 [8], replicated, may hold values from 0.2 to 2
- dam_cell: int32 [64], replicated, may hold values from 0 to 16777215, as said below
- releases: float32 [64, 2], replicated, may hold values from 0.5 to 4
Outputs:
- final_depth: float32 [2048, 8192], P('gx', 'gy')
- depth_adjoint: float32 [2048, 8192], P('gx', 'gy')
- release_grad: float32 [64, 2], replicated
Inputs may be any that keep to these rules, and one draw needn't show every extreme that they name: Every dam's inflow cell has wet_mask 1. `dam_cell`: a cell index row * 8192 + column.
All inputs are finite; a program needn't handle non-finite values.
Results may differ from a plain program's by a relative error of at most 0.0003.
Values sent between devices are 32-bit elements; how exact they have to be, the bound alone decides.
No kernel may reach another device: no remote copies, remote signals or barrier semaphores. Data moves between devices by JAX's collectives and lax.ppermute only.
A program may use at most 64 MiB of HBM per device.

v0:
```python
import jax
import jax.numpy as jnp
from jax import lax
from jax.experimental import pallas as pl
from jax.experimental.pallas import tpu as pltpu
from jax.sharding import PartitionSpec as P

GRAVITY = 9.81
TIME_RATIO = 0.05
INFLOW_GAIN = 0.25

LANES = 128
REACH = 4
EDGE = 8
FIELDS = 4
STRIP = FIELDS * REACH


def class_rate(classes, rates_ref):
    rate = jnp.full(classes.shape, rates_ref[0], jnp.float32)
    for index in range(1, rates_ref.shape[0]):
        rate = jnp.where(classes == index, rates_ref[index], rate)
    return rate


def edge_columns_kernel(h_ref, x_ref, y_ref, wet_ref, class_ref, rates_ref, low_ref, high_ref):
    rows, cols = h_ref.shape
    lane = lax.broadcasted_iota(jnp.int32, (rows, LANES), 1)
    mixed = jnp.zeros((rows, LANES), jnp.float32)
    for side, start in ((0, 0), (1, cols - LANES)):
        part = slice(start, start + LANES)
        wet = wet_ref[:, part] > 0
        fields = (
            jnp.where(wet, h_ref[:, part], 0.0),
            x_ref[:, part],
            y_ref[:, part],
            jnp.where(wet, class_rate(class_ref[:, part], rates_ref), 0.0),
        )
        for index, field in enumerate(fields):
            first = side * STRIP + index * REACH
            moved = first if side == 0 else first + REACH
            shifted = pltpu.roll(field, moved, 1) if moved else field
            mixed = jnp.where((lane >= first) & (lane < first + REACH), shifted, mixed)
    turned = mixed.T
    low_ref[...] = turned[:STRIP]
    high_ref[...] = turned[STRIP : 2 * STRIP]


def edge_rows_kernel(
    h_ref, x_ref, y_ref, wet_ref, class_ref, rates_ref, left_ref, right_ref, side_ref, low_ref, high_ref
):
    rows, cols = h_ref.shape
    blank = jnp.zeros((LANES - 2 * STRIP, rows), jnp.float32)
    turned = jnp.concatenate((right_ref[...], left_ref[...], blank), axis=0).T
    lane = lax.broadcasted_iota(jnp.int32, (rows, LANES), 1)
    for index in range(FIELDS):
        first = index * REACH
        upper = pltpu.roll(turned, (LANES - first) % LANES, 1) if first else turned
        lower = pltpu.roll(turned, LANES - REACH - STRIP - first, 1)
        tile = jnp.where(lane < REACH, upper, jnp.where(lane >= LANES - REACH, lower, 0.0))
        side_ref[index] = tile
        low_ref[first : first + REACH, cols:] = tile[:REACH]
        high_ref[first : first + REACH, cols:] = tile[rows - REACH :]
    for ref, start, kept in ((low_ref, 0, 0), (high_ref, rows - 8, 8 - REACH)):
        part = slice(start, start + 8)
        wet = wet_ref[part, :] > 0
        fields = (
            jnp.where(wet, h_ref[part, :], 0.0),
            x_ref[part, :],
            y_ref[part, :],
            jnp.where(wet, class_rate(class_ref[part, :], rates_ref), 0.0),
        )
        for index, field in enumerate(fields):
            ref[index * REACH : (index + 1) * REACH, :cols] = field[kept : kept + REACH]


def cell_terms(height, flow_x, flow_y):
    scaled = GRAVITY * height
    inverse = 1.0 / height
    return flow_x * inverse, flow_y * inverse, jnp.sqrt(scaled), inverse


def waves(u_low, c_low, u_high, c_high, both):
    slow_low, slow_high = u_low - c_low, u_high - c_high
    fast_low, fast_high = u_low + c_low, u_high + c_high
    slowest = jnp.minimum(jnp.minimum(slow_low, slow_high), 0.0)
    fastest = jnp.maximum(jnp.maximum(fast_low, fast_high), 0.0)
    inverse = both * (1.0 / (fastest - slowest))
    share_low = fastest * inverse
    share_high = -(slowest * inverse)
    spread = slowest * share_low
    return slowest, fastest, inverse, share_low, share_high, spread, slow_low <= slow_high, fast_low >= fast_high


def speed_terms(slowest, fastest, of_slowest, of_fastest, slow_is_low, fast_is_low):
    of_slowest = jnp.where(slowest < 0.0, of_slowest, 0.0)
    of_fastest = jnp.where(fastest > 0.0, of_fastest, 0.0)
    slow_to_low = jnp.where(slow_is_low, of_slowest, 0.0)
    fast_to_low = jnp.where(fast_is_low, of_fastest, 0.0)
    slow_to_high = of_slowest - slow_to_low
    fast_to_high = of_fastest - fast_to_low
    return (
        fast_to_low + slow_to_low,
        fast_to_low - slow_to_low,
        fast_to_high + slow_to_high,
        fast_to_high - slow_to_high,
    )


def window_kernel(
    h_ref, x_ref, y_ref, wet_ref, class_ref, rates_ref, side_ref, top_ref, bottom_ref, dam_ref, release_ref,
    depth_ref, adjoint_ref, grad_ref,
    state0, state1, mask, faces, walls, weight, last, lam, back, listed,
):
    rows, cols = h_ref.shape
    tiles = cols // LANES + 1
    chunks = rows // 8 + 2
    inner = range(tiles - 1)
    every = range(tiles)
    lane = lax.broadcasted_iota(jnp.int32, (8, LANES), 1)

    def at(ref, k, j, start):
        return ref[k, j, pl.ds(start, 8), :]

    def next_col(values):
        rolled = [pltpu.roll(v, LANES - 1, 1) for v in values]
        return [jnp.where(lane == LANES - 1, rolled[(j + 1) % tiles], rolled[j]) for j in every]

    def previous_col(values):
        rolled = [pltpu.roll(v, 1, 1) for v in values]
        return [jnp.where(lane == 0, rolled[(j - 1) % tiles], rolled[j]) for j in every]

    def previous_row(slot, j, start, value):
        back[slot, j, pl.ds(start + 8, 8), :] = value
        return back[slot, j, pl.ds(start + 7, 8), :]

    def put_cell(ref, j, start, height, flow_x, flow_y):
        u, v, c, inverse = cell_terms(height, flow_x, flow_y)
        for k, value in enumerate((height, flow_x, flow_y, u, v, c, inverse)):
            ref[k, j, pl.ds(start, 8), :] = value

    def put_start(j, start, wet, height, flow_x, flow_y, rate):
        put_cell(
            state0, j, start,
            jnp.where(wet, height, 1.0), jnp.where(wet, flow_x, 0.0), jnp.where(wet, flow_y, 0.0),
        )
        mask[j, pl.ds(start, 8), :] = jnp.where(wet, 1.0, 0.0)
        weight[j, pl.ds(start, 8), :] = rate

    row_first = lax.axis_index("gx") * rows
    col_first = lax.axis_index("gy") * cols
    total_cols = cols * lax.axis_size("gy")

    def list_dam(d, count):
        cell = dam_ref[d]
        row = cell // total_cols
        col = cell - row * total_cols - col_first
        row = row - row_first
        near = (row >= -REACH) & (row < rows + REACH) & (col >= -REACH) & (col < cols + REACH)

        @pl.when(near)
        def _():
            place = jnp.where(col < 0, col + tiles * LANES, col)
            listed[0, count] = d
            listed[1, count] = row + EDGE
            listed[2, count] = place // LANES
            listed[3, count] = place % LANES
            inside = (row >= 0) & (row < rows) & (col >= 0) & (col < cols)
            listed[4, count] = jnp.where(inside, 1, 0)

        return count + jnp.where(near, 1, 0)

    dams = lax.fori_loop(0, dam_ref.shape[0], list_dam, 0)

    zero = jnp.zeros((8, LANES), jnp.float32)
    for j in every:
        for slot in range(back.shape[0]):
            back[slot, j, 0:8, :] = zero
        for ref in (state0, state1):
            for k in range(7):
                ref[k, j, pl.ds(chunks * 8, 8), :] = zero + (1.0 if k in (0, 5, 6) else 0.0)
        mask[j, pl.ds(chunks * 8, 8), :] = zero
        for k in range(3):
            lam[k, j, pl.ds(chunks * 8, 8), :] = zero

    def start_rows(i, carry):
        start = pl.multiple_of(i * 8, 8)
        for j in inner:
            part = pl.ds(j * LANES, LANES)
            wet = wet_ref[pl.ds(start, 8), part] > 0
            rate = jnp.where(wet, class_rate(class_ref[pl.ds(start, 8), part], rates_ref), 0.0)
            put_start(
                j, start + EDGE, wet,
                h_ref[pl.ds(start, 8), part], x_ref[pl.ds(start, 8), part], y_ref[pl.ds(start, 8), part], rate,
            )
        h, x, y, rate = (side_ref[k, pl.ds(start, 8), :] for k in range(FIELDS))
        put_start(tiles - 1, start + EDGE, h > 0.0, h, x, y, rate)
        return carry

    lax.fori_loop(0, rows // 8, start_rows, 0)
    blank = jnp.zeros((8 - REACH, LANES), jnp.float32)
    for j in every:
        part = slice(j * LANES, (j + 1) * LANES)
        above = [jnp.concatenate((blank, top_ref[k * REACH : (k + 1) * REACH, part]), axis=0) for k in range(FIELDS)]
        below = [jnp.concatenate((bottom_ref[k * REACH : (k + 1) * REACH, part], blank), axis=0) for k in range(FIELDS)]
        for start, (h, x, y, rate) in ((0, above), (rows + EDGE, below)):
            put_start(j, start, h > 0.0, h, x, y, rate)

    def add_inflow(step, ref, refresh):
        def one(index, carry):
            d, row, j, col = (listed[k, index] for k in range(4))
            if refresh:
                old = [ref[k, j, pl.ds(row, 1), :] for k in range(3)]
            else:
                old = [ref[j, pl.ds(row, 1), :]]
            here = lax.broadcasted_iota(jnp.int32, (1, LANES), 1) == col
            height = old[0] + jnp.where(here, INFLOW_GAIN * release_ref[d, step], 0.0)
            if refresh:
                terms = (height, old[1], old[2]) + cell_terms(height, old[1], old[2])
                for k, value in enumerate(terms):
                    ref[k, j, pl.ds(row, 1), :] = value
            else:
                ref[j, pl.ds(row, 1), :] = height
            return carry

        lax.fori_loop(0, dams, one, 0)

    def pick(step, gradient):
        lane_row = lax.broadcasted_iota(jnp.int32, (1, LANES), 1)

        def one(index, total):
            d, row, j, col, inside = (listed[k, index] for k in range(5))
            values = lam[0, j, pl.ds(row, 1), :]
            value = jnp.sum(jnp.where(lane_row == col, values, 0.0), axis=1, keepdims=True)
            spot = (lane_row == d + step * dam_ref.shape[0]) & (inside > 0)
            return total + jnp.where(spot, (INFLOW_GAIN / TIME_RATIO) * value, 0.0)

        return lax.fori_loop(0, dams, one, gradient)

    def first_step(i, carry):
        start = pl.multiple_of(i * 8, 8)
        low = [[at(state0, k, j, start) for j in every] for k in range(6)]
        h, x, y, u, v, c = low
        m = [mask[j, pl.ds(start, 8), :] for j in every]
        half = [(0.5 * GRAVITY) * h[j] * h[j] for j in every]
        cross = [x[j] * v[j] for j in every]
        press_x = [x[j] * u[j] + half[j] for j in every]
        press_y = [y[j] * v[j] + half[j] for j in every]
        gain = []
        for j in every:
            hn, xn, yn, un, cn = (at(state0, k, j, start + 1) for k in (0, 1, 2, 3, 5))
            both = m[j] * mask[j, pl.ds(start + 1, 8), :]
            faces[0, j, pl.ds(start, 8), :] = both
            _, _, _, wl, wh, sp, _, _ = waves(u[j], c[j], un, cn, both)
            fh = wl * x[j] + wh * xn + sp * (hn - h[j])
            fn = wl * press_x[j] + wh * (xn * un + (0.5 * GRAVITY) * hn * hn) + sp * (xn - x[j])
            ft = wl * cross[j] + wh * (yn * un) + sp * (yn - y[j])
            both_low = previous_row(0, j, start, both)
            tilt = both_low - both
            shut = 2.0 * m[j] - both - both_low
            walls[0, j, pl.ds(start, 8), :] = tilt
            walls[1, j, pl.ds(start, 8), :] = shut
            gain.append(
                [
                    fh - previous_row(1, j, start, fh),
                    fn - previous_row(2, j, start, fn) + tilt * press_x[j] + shut * ((jnp.abs(u[j]) + c[j]) * x[j]),
                    ft - previous_row(3, j, start, ft),
                ]
            )
        hn, xn, yn, vn, cn, pn, tn, mn = (next_col(q) for q in (h, x, y, v, c, press_y, cross, m))
        flux = [[], [], []]
        both_up = []
        for j in every:
            both = m[j] * mn[j]
            faces[1, j, pl.ds(start, 8), :] = both
            both_up.append(both)
            _, _, _, wl, wh, sp, _, _ = waves(v[j], c[j], vn[j], cn[j], both)
            flux[0].append(wl * y[j] + wh * yn[j] + sp * (hn[j] - h[j]))
            flux[1].append(wl * press_y[j] + wh * pn[j] + sp * (yn[j] - y[j]))
            flux[2].append(wl * cross[j] + wh * tn[j] + sp * (xn[j] - x[j]))
        flux_low = [previous_col(q) for q in flux]
        both_low = previous_col(both_up)
        for j in every:
            tilt = both_low[j] - both_up[j]
            shut = 2.0 * m[j] - both_up[j] - both_low[j]
            walls[2, j, pl.ds(start, 8), :] = tilt
            walls[3, j, pl.ds(start, 8), :] = shut
            change_h = gain[j][0] + (flux[0][j] - flux_low[0][j])
            change_x = gain[j][1] + (flux[2][j] - flux_low[2][j])
            change_y = gain[j][2] + (flux[1][j] - flux_low[1][j])
            change_y = change_y + tilt * press_y[j] + shut * ((jnp.abs(v[j]) + c[j]) * y[j])
            put_cell(
                state1, j, start,
                h[j] - TIME_RATIO * change_h, x[j] - TIME_RATIO * change_x, y[j] - TIME_RATIO * change_y,
            )
        return carry

    lax.fori_loop(0, chunks, first_step, 0)
    add_inflow(0, state1, True)

    def second_step(i, carry):
        start = pl.multiple_of(i * 8, 8)
        h, x, y, u, v, c = [[at(state1, k, j, start) for j in every] for k in range(6)]
        gain = []
        for j in every:
            hn, xn, un, cn = (at(state1, k, j, start + 1) for k in (0, 1, 3, 5))
            _, _, _, wl, wh, sp, _, _ = waves(u[j], c[j], un, cn, at(faces, 0, j, start))
            fh = wl * x[j] + wh * xn + sp * (hn - h[j])
            gain.append(fh - previous_row(0, j, start, fh))
        hn, yn, vn, cn = (next_col(q) for q in (h, y, v, c))
        flux = []
        for j in every:
            _, _, _, wl, wh, sp, _, _ = waves(v[j], c[j], vn[j], cn[j], at(faces, 1, j, start))
            flux.append(wl * y[j] + wh * yn[j] + sp * (hn[j] - h[j]))
        flux_low = previous_col(flux)
        for j in every:
            last[j, pl.ds(start, 8), :] = h[j] - TIME_RATIO * (gain[j] + (flux[j] - flux_low[j]))
        return carry

    lax.fori_loop(0, chunks, second_step, 0)
    add_inflow(1, last, False)

    def finish_depth(i, carry):
        start = pl.multiple_of(i * 8, 8)
        for j in every:
            height = last[j, pl.ds(start, 8), :]
            lam[0, j, pl.ds(start, 8), :] = TIME_RATIO * (weight[j, pl.ds(start, 8), :] * height)
        return carry

    lax.fori_loop(0, chunks, finish_depth, 0)

    def store_depth(i, carry):
        start = pl.multiple_of(i * 8, 8)
        for j in inner:
            part = pl.ds(j * LANES, LANES)
            height = last[j, pl.ds(start + EDGE, 8), :]
            depth_ref[pl.ds(start, 8), part] = jnp.where(
                wet_ref[pl.ds(start, 8), part] > 0, height, h_ref[pl.ds(start, 8), part]
            )
        return carry

    lax.fori_loop(0, rows // 8, store_depth, 0)
    gradient = pick(1, jnp.zeros((1, LANES), jnp.float32))

    def second_back(i, carry):
        start = pl.multiple_of(i * 8, 8)
        h, x, y, u, v, c, r = [[at(state1, k, j, start) for j in every] for k in range(7)]
        lh = [at(lam, 0, j, start) for j in every]

        def face(hl, nl, ul, cl, hh, nh, uh, ch, gl, gh, both):
            slow, fast, inv, wl, wh, sp, slow_low, fast_low = waves(ul, cl, uh, ch, both)
            g = gh - gl
            dn, dh = nh - nl, hh - hl
            to_low, to_high = wl * g, wh * g
            of_slow = -(to_low * inv) * (dn - fast * dh)
            of_fast = -(to_high * inv) * (dn - slow * dh)
            return (to_low, to_high, sp * g) + speed_terms(slow, fast, of_slow, of_fast, slow_low, fast_low)

        partial_h, partial_u, partial_c, flow = [], [], [], []
        for j in every:
            hn, xn, un, cn = (at(state1, k, j, start + 1) for k in (0, 1, 3, 5))
            to_low, to_high, jump, u_low, c_low, u_high, c_high = face(
                h[j], x[j], u[j], c[j], hn, xn, un, cn, lh[j], at(lam, 0, j, start + 1), at(faces, 0, j, start)
            )
            of_u = u_low + previous_row(2, j, start, u_high)
            partial_h.append(previous_row(0, j, start, jump) - jump)
            partial_c.append(c_low + previous_row(3, j, start, c_high))
            partial_u.append(of_u * u[j])
            flow.append(to_low + previous_row(1, j, start, to_high) + of_u * r[j])
        hn, yn, vn, cn, ln = (next_col(q) for q in (h, y, v, c, lh))
        terms = [
            face(h[j], y[j], v[j], c[j], hn[j], yn[j], vn[j], cn[j], lh[j], ln[j], at(faces, 1, j, start))
            for j in every
        ]
        high, jump, u_high, c_high = (previous_col([t[k] for t in terms]) for k in (1, 2, 5, 6))
        for j in every:
            to_low, _, own_jump, u_low, c_low, _, _ = terms[j]
            of_v = u_low + u_high[j]
            of_c = partial_c[j] + c_low + c_high[j]
            of_h = partial_h[j] + (jump[j] - own_jump)
            of_h = of_h + r[j] * (0.5 * (of_c * c[j]) - partial_u[j] - of_v * v[j])
            back[4, j, pl.ds(start + 8, 8), :] = lh[j] + TIME_RATIO * of_h
            lam[1, j, pl.ds(start, 8), :] = TIME_RATIO * flow[j]
            lam[2, j, pl.ds(start, 8), :] = TIME_RATIO * (to_low + high[j] + of_v * r[j])
        return carry

    lax.fori_loop(0, chunks, second_back, 0)

    def move_back(i, carry):
        start = pl.multiple_of(i * 8, 8)
        for j in every:
            lam[0, j, pl.ds(start, 8), :] = back[4, j, pl.ds(start + 8, 8), :]
        return carry

    lax.fori_loop(0, chunks, move_back, 0)
    gradient = pick(0, gradient)
    grad_ref[...] = jnp.broadcast_to(gradient, grad_ref.shape)

    def first_back(i, carry):
        start = pl.multiple_of(i * 8, 8)
        h, x, y, u, v, c, r = [[at(state0, k, j, start) for j in every] for k in range(7)]
        lh, lx, ly = [[at(lam, k, j, start) for j in every] for k in range(3)]
        half = [(0.5 * GRAVITY) * h[j] * h[j] for j in every]
        cross = [x[j] * v[j] for j in every]

        def face(hl, nl, tl, ul, cl, pl_, kl, hh, nh, th, uh, ch, ph, kh, gl, gh, both):
            slow, fast, inv, wl, wh, sp, slow_low, fast_low = waves(ul, cl, uh, ch, both)
            g_h, g_n, g_t = (b - a for a, b in zip(gl, gh))
            dn = nh - nl
            of_flux = g_h * dn + g_n * (ph - pl_) + g_t * (kh - kl)
            of_jump = g_h * (hh - hl) + g_n * dn + g_t * (th - tl)
            of_slow = -(wl * inv) * (of_flux - fast * of_jump)
            of_fast = -(wh * inv) * (of_flux - slow * of_jump)
            return (wl * g_n, wl * g_t, wh * g_n, wh * g_t, sp * g_h) + speed_terms(
                slow, fast, of_slow, of_fast, slow_low, fast_low
            )

        kept = []
        for j in every:
            hn, xn, yn, un, cn = (at(state0, k, j, start + 1) for k in (0, 1, 2, 3, 5))
            nl, tl, nh, th, jump, u_low, c_low, u_high, c_high = face(
                h[j], x[j], y[j], u[j], c[j], x[j] * u[j] + half[j], cross[j],
                hn, xn, yn, un, cn, xn * un + (0.5 * GRAVITY) * hn * hn, yn * un,
                (lh[j], lx[j], ly[j]), tuple(at(lam, k, j, start + 1) for k in range(3)), at(faces, 0, j, start),
            )
            shut = lx[j] * at(walls, 1, j, start)
            normal = nl + previous_row(0, j, start, nh) - lx[j] * at(walls, 0, j, start)
            across = tl + previous_row(1, j, start, th)
            of_u = normal * x[j] + across * y[j] + u_low + previous_row(3, j, start, u_high) - shut * jnp.abs(x[j])
            of_c = c_low + previous_row(4, j, start, c_high) - shut * x[j]
            kept.append((normal, previous_row(2, j, start, jump) - jump, of_u * u[j], of_c))
        press = [y[j] * v[j] + half[j] for j in every]
        hn, xn, yn, vn, cn, pn, kn = (next_col(q) for q in (h, x, y, v, c, press, cross))
        lhn, lxn, lyn = (next_col(q) for q in (lh, lx, ly))
        terms = [
            face(
                h[j], y[j], x[j], v[j], c[j], press[j], cross[j],
                hn[j], yn[j], xn[j], vn[j], cn[j], pn[j], kn[j],
                (lh[j], ly[j], lx[j]), (lhn[j], lyn[j], lxn[j]), at(faces, 1, j, start),
            )
            for j in every
        ]
        nh, th, jump, u_high, c_high = (previous_col([t[k] for t in terms]) for k in (2, 3, 4, 7, 8))
        for j in inner:
            shut = ly[j] * at(walls, 3, j, start)
            normal = terms[j][0] + nh[j] - ly[j] * at(walls, 2, j, start)
            across = terms[j][1] + th[j]
            of_v = normal * y[j] + across * x[j] + terms[j][5] + u_high[j] - shut * jnp.abs(y[j])
            of_c = kept[j][3] + terms[j][6] + c_high[j] - shut * y[j]
            of_h = kept[j][1] + (jump[j] - terms[j][4]) + GRAVITY * h[j] * (kept[j][0] + normal)
            of_h = of_h + r[j] * (0.5 * (of_c * c[j]) - kept[j][2] - of_v * v[j])
            result = (1.0 / TIME_RATIO) * lh[j] + of_h

            @pl.when(i > 0)
            def _():
                adjoint_ref[pl.ds(pl.multiple_of(jnp.maximum(start - EDGE, 0), 8), 8), pl.ds(j * LANES, LANES)] = result

        return carry

    lax.fori_loop(0, chunks - 1, first_back, 0)


def on_device(
    water_depth, momentum_x, momentum_y, wet_mask, damage_class, damage_rates, dam_cell, releases
):
    rows, cols = water_depth.shape
    wide = cols + LANES
    rows_count = lax.axis_size("gx")
    cols_count = lax.axis_size("gy")
    tiles = wide // LANES
    tall = rows + 2 * EDGE + 8
    vmem = pl.BlockSpec(memory_space=pltpu.VMEM)
    smem = pl.BlockSpec(memory_space=pltpu.SMEM)
    f32 = jnp.float32
    params = pltpu.CompilerParams(vmem_limit_bytes=48 * 1024 * 1024)
    local = (water_depth, momentum_x, momentum_y, wet_mask, damage_class, damage_rates)

    def shift(value, axis, count, step):
        pairs = [(i, i + step) for i in range(count) if 0 <= i + step < count]
        return lax.ppermute(value, axis, pairs)

    low, high = pl.pallas_call(
        edge_columns_kernel,
        out_shape=[jax.ShapeDtypeStruct((STRIP, rows), f32)] * 2,
        in_specs=[vmem] * 5 + [smem],
        out_specs=[vmem] * 2,
        compiler_params=params,
        name="edge_columns",
    )(*local)
    right = shift(low, "gy", cols_count, -1)
    left = shift(high, "gy", cols_count, 1)
    side, low, high = pl.pallas_call(
        edge_rows_kernel,
        out_shape=[
            jax.ShapeDtypeStruct((FIELDS, rows, LANES), f32),
            jax.ShapeDtypeStruct((STRIP, wide), f32),
            jax.ShapeDtypeStruct((STRIP, wide), f32),
        ],
        in_specs=[vmem] * 5 + [smem] + [vmem] * 2,
        out_specs=[vmem] * 3,
        compiler_params=params,
        name="edge_rows",
    )(*local, left, right)
    bottom = shift(low, "gx", rows_count, -1)
    top = shift(high, "gx", rows_count, 1)

    def cells(*lead):
        return pltpu.VMEM(lead + (tiles, tall, LANES), f32)

    devices = rows_count * cols_count
    depth, adjoint, parts = pl.pallas_call(
        window_kernel,
        out_shape=[
            jax.ShapeDtypeStruct((rows, cols), f32),
            jax.ShapeDtypeStruct((rows, cols), f32),
            jax.ShapeDtypeStruct((devices, LANES), f32),
        ],
        in_specs=[vmem] * 5 + [smem] + [vmem] * 3 + [smem] * 2,
        out_specs=[vmem] * 3,
        scratch_shapes=[
            cells(7), cells(7), cells(), cells(2), cells(4), cells(), cells(), cells(3), cells(5),
            pltpu.SMEM((5, dam_cell.shape[0]), jnp.int32),
        ],
        compiler_params=params,
        name="window",
    )(*local, side, top, bottom, dam_cell, releases)
    gathered = lax.all_to_all(parts, ("gx", "gy"), 0, 0)
    release_grad = jnp.sum(gathered, axis=0).reshape(releases.shape[1], releases.shape[0]).T
    return (depth, adjoint, release_grad)


def solution(mesh):
    in_specs = (P("gx", "gy"),) * 5 + (P(), P(), P())
    out_specs = (P("gx", "gy"), P("gx", "gy"), P())
    return jax.shard_map(
        on_device, mesh=mesh, in_specs=in_specs, out_specs=out_specs, check_vma=False
    )
```

profile of v0, /device:TPU:1, one launch (start us, length us, event | category | flops | bytes accessed | tf_op | source)
XLA Modules:
  0.0 81.0 jit_solution(630813270518956042)
XLA Ops:
  0.6 0.0 copy-start
  0.6 0.9 %copy-done = f32[128,512]{1,0:T(8,128)S(1)} copy-done((f32[128,512]{1,0:T(8,128)S(1)}, f32[128,512]{1,0:T(8,128)}, u32[]{:S(2)}) %copy-start) | copy-done | bytes 262168
  1.6 0.9 %copy-done.2 = f32[128,512]{1,0:T(8,128)S(1)} copy-done((f32[128,512]{1,0:T(8,128)S(1)}, f32[128,512]{1,0:T(8,128)}, u32[]{:S(2)}) %copy-start.2) | copy-done | bytes 262168
  2.5 0.9 %copy-done.4 = f32[128,512]{1,0:T(8,128)S(1)} copy-done((f32[128,512]{1,0:T(8,128)S(1)}, f32[128,512]{1,0:T(8,128)}, u32[]{:S(2)}) %copy-start.4) | copy-done | bytes 262168
  3.5 0.9 %copy-done.6 = s32[128,512]{1,0:T(8,128)S(1)} copy-done((s32[128,512]{1,0:T(8,128)S(1)}, s32[128,512]{1,0:T(8,128)}, u32[]{:S(2)}) %copy-start.6) | copy-done | bytes 262168
  4.4 0.9 %copy-done.8 = s32[128,512]{1,0:T(8,128)S(1)} copy-done((s32[128,512]{1,0:T(8,128)S(1)}, s32[128,512]{1,0:T(8,128)}, u32[]{:S(2)}) %copy-start.8) | copy-done | bytes 262168
  5.4 0.7 copy-done.10
  6.0 0.8 edge_columns.1
  6.8 10.2 %collective-permute-start = (f32[16,128]{1,0:T(8,128)S(1)}, f32[16,128]{1,0:T(8,128)S(1)}, u32[]{:S(2)}, u32[]{:S(2)}) collective-permute-start(f32[16,128]{1,0:T(8,128)S(1)} %get-tuple-element.11), channel_id=1, source_target_pairs={{0,1},{1,2},{2,3},{3,4},{4,5},{5,6},{6,7},{7,8},{8,9},{9,10},{10,1... | collective-permute-start | bytes 24584 | tf_op jit(solution)/shard_map/ppermute | solution.py:480
  17.0 0.0 copy-start.1
  17.0 0.0 copy-start.3
  17.1 0.0 copy-start.9
  17.1 2.1 %collective-permute-start.1 = (f32[16,128]{1,0:T(8,128)S(1)}, f32[16,128]{1,0:T(8,128)S(1)}, u32[]{:S(2)}, u32[]{:S(2)}) collective-permute-start(f32[16,128]{1,0:T(8,128)S(1)} %get-tuple-element.12), channel_id=1, source_target_pairs={{1,0},{2,1},{3,2},{4,3},{5,4},{6,5},{7,6},{8,7},{9,8},{10,9},{11,1... | collective-permute-start | bytes 24584 | tf_op jit(solution)/shard_map/ppermute | solution.py:480
  19.1 6.9 %collective-permute-done.1.right_ref = f32[16,128]{1,0:T(8,128)S(1)} collective-permute-done((f32[16,128]{1,0:T(8,128)S(1)}, f32[16,128]{1,0:T(8,128)S(1)}, u32[]{:S(2)}, u32[]{:S(2)}) %collective-permute-start.1) | collective-permute-done | bytes 8224 | tf_op jit(solution)/shard_map/ppermute | solution.py:480
  26.1 0.8 %edge_rows.1 = (f32[4,128,128]{2,1,0:T(8,128)S(1)}, f32[16,640]{1,0:T(8,128)S(1)}, f32[16,640]{1,0:T(8,128)S(1)}) custom-call(f32[128,512]{1,0:T(8,128)S(1)} %copy-done, f32[128,512]{1,0:T(8,128)S(1)} %copy-done.2, f32[128,512]{1,0:T(8,128)S(1)} %copy-done.4, s32[128,512]{1,0:T(8,128)S(1)} %copy-done.6, s32[128,512]{1,0:T(8,128)S(1)} %copy-done.8, ...), custom_call_target="tpu_custom_call" | custom-call | tf_op jit(solution)/shard_map/edge_rows/pallas_call | solution.py:492
  26.9 0.0 copy-start.13
  26.9 2.6 %collective-permute-start.2 = (f32[16,640]{1,0:T(8,128)S(1)}, f32[16,640]{1,0:T(8,128)S(1)}, u32[]{:S(2)}, u32[]{:S(2)}) collective-permute-start(f32[16,640]{1,0:T(8,128)S(1)} %get-tuple-element.14), channel_id=1, source_target_pairs={{0,16},{16,32},{32,48},{48,64},{64,80},{80,96},{96,112},{112,128},... | collective-permute-start | bytes 122888 | tf_op jit(solution)/shard_map/ppermute | solution.py:480
  29.6 1.3 %collective-permute-start.3 = (f32[16,640]{1,0:T(8,128)S(1)}, f32[16,640]{1,0:T(8,128)S(1)}, u32[]{:S(2)}, u32[]{:S(2)}) collective-permute-start(f32[16,640]{1,0:T(8,128)S(1)} %get-tuple-element.15), channel_id=1, source_target_pairs={{16,0},{32,16},{48,32},{64,48},{80,64},{96,80},{112,96},{128,112},... | collective-permute-start | bytes 122888 | tf_op jit(solution)/shard_map/ppermute | solution.py:480
  30.9 0.1 copy.12.release_ref
  31.0 3.8 %collective-permute-done.3.bottom_ref = f32[16,640]{1,0:T(8,128)S(1)} collective-permute-done((f32[16,640]{1,0:T(8,128)S(1)}, f32[16,640]{1,0:T(8,128)S(1)}, u32[]{:S(2)}, u32[]{:S(2)}) %collective-permute-start.3) | collective-permute-done | bytes 40992 | tf_op jit(solution)/shard_map/ppermute | solution.py:480
  34.8 19.3 %window.1 = (f32[128,512]{1,0:T(8,128)}, f32[128,512]{1,0:T(8,128)}, f32[256,128]{1,0:T(8,128)S(1)}) custom-call(f32[128,512]{1,0:T(8,128)S(1)} %copy-done.1, f32[128,512]{1,0:T(8,128)S(1)} %copy-done.3, f32[128,512]{1,0:T(8,128)S(1)} %copy-done.5, s32[128,512]{1,0:T(8,128)S(1)} %copy-done.7, s32[128,512]{1,0:T(8,128)S(1)} %copy-done.9, f32[8]{0:T(128)S(1)} %copy-done.11, ...), custom_call_target="tpu_custom_call" | custom-call | tf_op jit(solution)/shard_map/window/pallas_call | solution.py:511
  54.1 25.9 %all_to_all.9 = f32[256,1,128]{2,1,0:T(1,128)S(1)} all-to-all(f32[256,1,128]{2,1,0:T(1,128)S(1)} %bitcast.4), channel_id=1, replica_groups=mesh['gx'=16,'gy'=16] {'gx','gy'}, dimensions={0} | all-to-all | bytes 262144 | tf_op jit(solution)/shard_map/all_to_all | solution.py:527
  80.0 0.3 reduce_sum.9
  80.3 0.6 reshape.11
  (19 shorter events, 0.0 us)
Async XLA Ops:
  0.6 1.0 %copy-start = (f32[128,512]{1,0:T(8,128)S(1)}, f32[128,512]{1,0:T(8,128)}, u32[]{:S(2)}) copy-start(f32[128,512]{1,0:T(8,128)} %h_ref.5) | copy-start | bytes 786436
  1.6 0.9 %copy-start.2 = (f32[128,512]{1,0:T(8,128)S(1)}, f32[128,512]{1,0:T(8,128)}, u32[]{:S(2)}) copy-start(f32[128,512]{1,0:T(8,128)} %x_ref.5) | copy-start | bytes 786436
  2.5 0.9 %copy-start.4 = (f32[128,512]{1,0:T(8,128)S(1)}, f32[128,512]{1,0:T(8,128)}, u32[]{:S(2)}) copy-start(f32[128,512]{1,0:T(8,128)} %y_ref.5) | copy-start | bytes 786436
  3.5 0.9 %copy-start.6 = (s32[128,512]{1,0:T(8,128)S(1)}, s32[128,512]{1,0:T(8,128)}, u32[]{:S(2)}) copy-start(s32[128,512]{1,0:T(8,128)} %wet_ref.5) | copy-start | bytes 786436
  4.4 0.9 %copy-start.8 = (s32[128,512]{1,0:T(8,128)S(1)}, s32[128,512]{1,0:T(8,128)}, u32[]{:S(2)}) copy-start(s32[128,512]{1,0:T(8,128)} %class_ref.5) | copy-start | bytes 786436
  5.4 0.7 copy-start.10
  6.8 12.3 %collective-permute-start = (f32[16,128]{1,0:T(8,128)S(1)}, f32[16,128]{1,0:T(8,128)S(1)}, u32[]{:S(2)}, u32[]{:S(2)}) collective-permute-start(f32[16,128]{1,0:T(8,128)S(1)} %get-tuple-element.11), channel_id=1, source_target_pairs={{0,1},{1,2},{2,3},{3,4},{4,5},{5,6},{6,7},{7,8},{8,9},{9,10},{10,1... | collective-permute-start | bytes 24584 | tf_op jit(solution)/shard_map/ppermute | solution.py:480
  17.0 17.7 %copy-start.1 = (f32[128,512]{1,0:T(8,128)S(1)}, f32[128,512]{1,0:T(8,128)}, u32[]{:S(2)}) copy-start(f32[128,512]{1,0:T(8,128)} %h_ref.5) | copy-start | bytes 786436
  17.0 17.7 %copy-start.3 = (f32[128,512]{1,0:T(8,128)S(1)}, f32[128,512]{1,0:T(8,128)}, u32[]{:S(2)}) copy-start(f32[128,512]{1,0:T(8,128)} %x_ref.5) | copy-start | bytes 786436
  17.0 17.7 %copy-start.5 = (f32[128,512]{1,0:T(8,128)S(1)}, f32[128,512]{1,0:T(8,128)}, u32[]{:S(2)}) copy-start(f32[128,512]{1,0:T(8,128)} %y_ref.5) | copy-start | bytes 786436
  17.0 17.7 %copy-start.7 = (s32[128,512]{1,0:T(8,128)S(1)}, s32[128,512]{1,0:T(8,128)}, u32[]{:S(2)}) copy-start(s32[128,512]{1,0:T(8,128)} %wet_ref.5) | copy-start | bytes 786436
  17.1 17.7 %copy-start.9 = (s32[128,512]{1,0:T(8,128)S(1)}, s32[128,512]{1,0:T(8,128)}, u32[]{:S(2)}) copy-start(s32[128,512]{1,0:T(8,128)} %class_ref.5) | copy-start | bytes 786436
  17.1 9.0 %collective-permute-start.1 = (f32[16,128]{1,0:T(8,128)S(1)}, f32[16,128]{1,0:T(8,128)S(1)}, u32[]{:S(2)}, u32[]{:S(2)}) collective-permute-start(f32[16,128]{1,0:T(8,128)S(1)} %get-tuple-element.12), channel_id=1, source_target_pairs={{1,0},{2,1},{3,2},{4,3},{5,4},{6,5},{7,6},{8,7},{9,8},{10,9},{11,1... | collective-permute-start | bytes 24584 | tf_op jit(solution)/shard_map/ppermute | solution.py:480
  26.9 4.0 %copy-start.13 = (f32[64,2]{0,1:T(2,128)S(1)}, f32[64,2]{0,1:T(2,128)}, u32[]{:S(2)}) copy-start(f32[64,2]{0,1:T(2,128)} %param.15) | copy-start | bytes 1540
  26.9 4.1 %collective-permute-start.2 = (f32[16,640]{1,0:T(8,128)S(1)}, f32[16,640]{1,0:T(8,128)S(1)}, u32[]{:S(2)}, u32[]{:S(2)}) collective-permute-start(f32[16,640]{1,0:T(8,128)S(1)} %get-tuple-element.14), channel_id=1, source_target_pairs={{0,16},{16,32},{32,48},{48,64},{64,80},{80,96},{96,112},{112,128},... | collective-permute-start | bytes 122888 | tf_op jit(solution)/shard_map/ppermute | solution.py:480
  29.6 5.2 %collective-permute-start.3 = (f32[16,640]{1,0:T(8,128)S(1)}, f32[16,640]{1,0:T(8,128)S(1)}, u32[]{:S(2)}, u32[]{:S(2)}) collective-permute-start(f32[16,640]{1,0:T(8,128)S(1)} %get-tuple-element.15), channel_id=1, source_target_pairs={{16,0},{32,16},{48,32},{64,48},{80,64},{96,80},{112,96},{128,112},... | collective-permute-start | bytes 122888 | tf_op jit(solution)/shard_map/ppermute | solution.py:480
  31.0 3.8 %copy-start.11 = (f32[8]{0:T(128)S(1)}, f32[8]{0:T(128)}, u32[]{:S(2)}) copy-start(f32[8]{0:T(128)} %rates_ref.5) | copy-start | bytes 100
  31.0 3.8 %copy-start.12 = (s32[64]{0:T(128)S(1)}, s32[64]{0:T(128)}, u32[]{:S(2)}) copy-start(s32[64]{0:T(128)} %dam_ref.1) | copy-start | bytes 772
where the time goes:
time: 81.4 us; the launch traced here: 81 us
  blocking collectives  25.9 us (32%)
  Pallas kernels  20.9 us (26%)
  starting transfers between devices  16.2 us (20%)
  waiting for transfers between devices  10.7 us (13%)
  local copies, waits for them, and re-layouts  6.18 us (8%)
    all_to_all x1, blocking collectives, on_device(): gathered = lax.all_to_all(parts, ('gx', 'gy'), 0, 0)  25.9 us
    pallas_call x1, Pallas kernels, on_device(): pl.pallas_call(window_kernel, out_shape=[jax.ShapeDtypeStruct((rows, cols...  19.3 us
    ppermute x4, starting transfers between devices, shift(): return lax.ppermute(value, axis, pairs)  16.2 us
    ppermute x4, waiting for transfers between devices, shift(): return lax.ppermute(value, axis, pairs)  10.7 us
    unnamed x29, local copies, waits for them, and re-layouts  5.54 us
  transfers between devices with their start and end apart: 4, of which 2 were waited for; matrix products, arithmetic and copies ran while one was open for 0% of the time, Pallas kernels for 0%

commit v1 on v0

--- a/solution.py
+++ b/solution.py
@@ -14,6 +14,7 @@
 EDGE = 8
 FIELDS = 4
 STRIP = FIELDS * REACH
+UNROLL = True
 
 
 def class_rate(classes, rates_ref):
@@ -23,61 +24,66 @@
     return rate
 
 
-def edge_columns_kernel(h_ref, x_ref, y_ref, wet_ref, class_ref, rates_ref, low_ref, high_ref):
-    rows, cols = h_ref.shape
+def coded_fields(h, x, y, wet, classes):
+    return jnp.where(wet > 0, h, 0.0), x, y, classes.astype(jnp.float32)
+
+
+def edge_kernel(h_hbm, x_hbm, y_hbm, wet_hbm, class_hbm, low_ref, high_ref, values, codes, sems):
+    rows, cols = h_hbm.shape
+    copies = []
+    for index, source in enumerate((h_hbm, x_hbm, y_hbm, wet_hbm, class_hbm)):
+        for side in range(2):
+            kept = values.at[side, index] if index < 3 else codes.at[side, index - 3]
+            part = source.at[:, pl.ds(side * (cols - LANES), LANES)]
+            copies.append(pltpu.make_async_copy(part, kept, sems.at[side, index]))
+    for copy in copies:
+        copy.start()
+    for copy in copies:
+        copy.wait()
     lane = lax.broadcasted_iota(jnp.int32, (rows, LANES), 1)
     mixed = jnp.zeros((rows, LANES), jnp.float32)
-    for side, start in ((0, 0), (1, cols - LANES)):
-        part = slice(start, start + LANES)
-        wet = wet_ref[:, part] > 0
-        fields = (
-            jnp.where(wet, h_ref[:, part], 0.0),
-            x_ref[:, part],
-            y_ref[:, part],
-            jnp.where(wet, class_rate(class_ref[:, part], rates_ref), 0.0),
-        )
+    for side in range(2):
+        fields = coded_fields(*(values[side, k] for k in range(3)), *(codes[side, k] for k in range(2)))
         for index, field in enumerate(fields):
-            first = side * STRIP + index * REACH
-            moved = first if side == 0 else first + REACH
+            first = (side * FIELDS + index) * EDGE
+            moved = first if side == 0 else first + EDGE
             shifted = pltpu.roll(field, moved, 1) if moved else field
-            mixed = jnp.where((lane >= first) & (lane < first + REACH), shifted, mixed)
+            mixed = jnp.where((lane >= first) & (lane < first + EDGE), shifted, mixed)
     turned = mixed.T
-    low_ref[...] = turned[:STRIP]
-    high_ref[...] = turned[STRIP : 2 * STRIP]
-
-
-def edge_rows_kernel(
-    h_ref, x_ref, y_ref, wet_ref, class_ref, rates_ref, left_ref, right_ref, side_ref, low_ref, high_ref
-):
+    low_ref[...] = turned[: FIELDS * EDGE]
+    high_ref[...] = turned[FIELDS * EDGE : 2 * FIELDS * EDGE]
+
+
+def beside(left_ref, right_ref):
+    place = lax.axis_index("gy")
+    left = jnp.where(place > 0, left_ref[...], 0.0)
+    right = jnp.where(place < lax.axis_size("gy") - 1, right_ref[...], 0.0)
+    return left, right
+
+
+def corner_kernel(h_ref, x_ref, y_ref, wet_ref, class_ref, left_ref, right_ref, side_ref, low_ref, high_ref):
     rows, cols = h_ref.shape
-    blank = jnp.zeros((LANES - 2 * STRIP, rows), jnp.float32)
-    turned = jnp.concatenate((right_ref[...], left_ref[...], blank), axis=0).T
-    lane = lax.broadcasted_iota(jnp.int32, (rows, LANES), 1)
-    for index in range(FIELDS):
-        first = index * REACH
-        upper = pltpu.roll(turned, (LANES - first) % LANES, 1) if first else turned
-        lower = pltpu.roll(turned, LANES - REACH - STRIP - first, 1)
-        tile = jnp.where(lane < REACH, upper, jnp.where(lane >= LANES - REACH, lower, 0.0))
-        side_ref[index] = tile
-        low_ref[first : first + REACH, cols:] = tile[:REACH]
-        high_ref[first : first + REACH, cols:] = tile[rows - REACH :]
-    for ref, start, kept in ((low_ref, 0, 0), (high_ref, rows - 8, 8 - REACH)):
-        part = slice(start, start + 8)
-        wet = wet_ref[part, :] > 0
-        fields = (
-            jnp.where(wet, h_ref[part, :], 0.0),
-            x_ref[part, :],
-            y_ref[part, :],
-            jnp.where(wet, class_rate(class_ref[part, :], rates_ref), 0.0),
-        )
-        for index, field in enumerate(fields):
-            ref[index * REACH : (index + 1) * REACH, :cols] = field[kept : kept + REACH]
+    left, right = beside(left_ref, right_ref)
+    blank = jnp.zeros((LANES - 2 * FIELDS * EDGE, rows), jnp.float32)
+    turned = jnp.concatenate((right, left, blank), axis=0).T
+    lane = lax.broadcasted_iota(jnp.int32, (EDGE, LANES), 1)
+    for end, (ref, start, kept) in enumerate(((low_ref, 0, 0), (high_ref, rows - EDGE, EDGE - REACH))):
+        part = slice(start, start + EDGE)
+        own = coded_fields(h_ref[part, :], x_ref[part, :], y_ref[part, :], wet_ref[part, :], class_ref[part, :])
+        for index in range(FIELDS):
+            upper = pltpu.roll(turned[part], (LANES - index * EDGE) % LANES, 1) if index else turned[part]
+            lower = pltpu.roll(turned[part], LANES - (1 + FIELDS + index) * EDGE, 1)
+            tile = jnp.where(lane < EDGE, upper, jnp.where(lane >= LANES - EDGE, lower, 0.0))
+            side_ref[end, index] = tile
+            place = slice(index * REACH, (index + 1) * REACH)
+            ref[place, cols:] = tile[kept : kept + REACH]
+            ref[place, :cols] = own[index][kept : kept + REACH]
 
 
 def cell_terms(height, flow_x, flow_y):
     scaled = GRAVITY * height
-    inverse = 1.0 / height
-    return flow_x * inverse, flow_y * inverse, jnp.sqrt(scaled), inverse
+    inverse = pltpu.reciprocal(height, approx=True)
+    return flow_x * inverse, flow_y * inverse, scaled * lax.rsqrt(scaled), inverse
 
 
 def waves(u_low, c_low, u_high, c_high, both):
@@ -85,7 +91,7 @@
     fast_low, fast_high = u_low + c_low, u_high + c_high
     slowest = jnp.minimum(jnp.minimum(slow_low, slow_high), 0.0)
     fastest = jnp.maximum(jnp.maximum(fast_low, fast_high), 0.0)
-    inverse = both * (1.0 / (fastest - slowest))
+    inverse = both * pltpu.reciprocal(fastest - slowest, approx=True)
     share_low = fastest * inverse
     share_high = -(slowest * inverse)
     spread = slowest * share_low
@@ -107,15 +113,9 @@
     )
 
 
-def window_kernel(
-    h_ref, x_ref, y_ref, wet_ref, class_ref, rates_ref, side_ref, top_ref, bottom_ref, dam_ref, release_ref,
-    depth_ref, adjoint_ref, grad_ref,
-    state0, state1, mask, faces, walls, weight, last, lam, back, listed,
-):
-    rows, cols = h_ref.shape
-    tiles = cols // LANES + 1
-    chunks = rows // 8 + 2
-    inner = range(tiles - 1)
+def window(chunks, after, before, put, rates_ref, listed, dams, release_ref, scratch):
+    state0, state1, mask, faces, walls, weight, last, lam, back, final = scratch
+    tiles = len(after)
     every = range(tiles)
     lane = lax.broadcasted_iota(jnp.int32, (8, LANES), 1)
 
@@ -124,11 +124,11 @@
 
     def next_col(values):
         rolled = [pltpu.roll(v, LANES - 1, 1) for v in values]
-        return [jnp.where(lane == LANES - 1, rolled[(j + 1) % tiles], rolled[j]) for j in every]
+        return [jnp.where(lane == LANES - 1, rolled[after[j]], rolled[j]) for j in every]
 
     def previous_col(values):
         rolled = [pltpu.roll(v, 1, 1) for v in values]
-        return [jnp.where(lane == 0, rolled[(j - 1) % tiles], rolled[j]) for j in every]
+        return [jnp.where(lane == 0, rolled[before[j]], rolled[j]) for j in every]
 
     def previous_row(slot, j, start, value):
         back[slot, j, pl.ds(start + 8, 8), :] = value
@@ -139,38 +139,13 @@
         for k, value in enumerate((height, flow_x, flow_y, u, v, c, inverse)):
             ref[k, j, pl.ds(start, 8), :] = value
 
-    def put_start(j, start, wet, height, flow_x, flow_y, rate):
+    def fill(j, start, wet, height, flow_x, flow_y, classes):
         put_cell(
             state0, j, start,
             jnp.where(wet, height, 1.0), jnp.where(wet, flow_x, 0.0), jnp.where(wet, flow_y, 0.0),
         )
         mask[j, pl.ds(start, 8), :] = jnp.where(wet, 1.0, 0.0)
-        weight[j, pl.ds(start, 8), :] = rate
-
-    row_first = lax.axis_index("gx") * rows
-    col_first = lax.axis_index("gy") * cols
-    total_cols = cols * lax.axis_size("gy")
-
-    def list_dam(d, count):
-        cell = dam_ref[d]
-        row = cell // total_cols
-        col = cell - row * total_cols - col_first
-        row = row - row_first
-        near = (row >= -REACH) & (row < rows + REACH) & (col >= -REACH) & (col < cols + REACH)
-
-        @pl.when(near)
-        def _():
-            place = jnp.where(col < 0, col + tiles * LANES, col)
-            listed[0, count] = d
-            listed[1, count] = row + EDGE
-            listed[2, count] = place // LANES
-            listed[3, count] = place % LANES
-            inside = (row >= 0) & (row < rows) & (col >= 0) & (col < cols)
-            listed[4, count] = jnp.where(inside, 1, 0)
-
-        return count + jnp.where(near, 1, 0)
-
-    dams = lax.fori_loop(0, dam_ref.shape[0], list_dam, 0)
+        weight[j, pl.ds(start, 8), :] = jnp.where(wet, class_rate(classes, rates_ref), 0.0)
 
     zero = jnp.zeros((8, LANES), jnp.float32)
     for j in every:
@@ -182,29 +157,10 @@
         mask[j, pl.ds(chunks * 8, 8), :] = zero
         for k in range(3):
             lam[k, j, pl.ds(chunks * 8, 8), :] = zero
-
-    def start_rows(i, carry):
-        start = pl.multiple_of(i * 8, 8)
-        for j in inner:
-            part = pl.ds(j * LANES, LANES)
-            wet = wet_ref[pl.ds(start, 8), part] > 0
-            rate = jnp.where(wet, class_rate(class_ref[pl.ds(start, 8), part], rates_ref), 0.0)
-            put_start(
-                j, start + EDGE, wet,
-                h_ref[pl.ds(start, 8), part], x_ref[pl.ds(start, 8), part], y_ref[pl.ds(start, 8), part], rate,
-            )
-        h, x, y, rate = (side_ref[k, pl.ds(start, 8), :] for k in range(FIELDS))
-        put_start(tiles - 1, start + EDGE, h > 0.0, h, x, y, rate)
-        return carry
-
-    lax.fori_loop(0, rows // 8, start_rows, 0)
-    blank = jnp.zeros((8 - REACH, LANES), jnp.float32)
-    for j in every:
-        part = slice(j * LANES, (j + 1) * LANES)
-        above = [jnp.concatenate((blank, top_ref[k * REACH : (k + 1) * REACH, part]), axis=0) for k in range(FIELDS)]
-        below = [jnp.concatenate((bottom_ref[k * REACH : (k + 1) * REACH, part], blank), axis=0) for k in range(FIELDS)]
-        for start, (h, x, y, rate) in ((0, above), (rows + EDGE, below)):
-            put_start(j, start, h > 0.0, h, x, y, rate)
+    put(fill)
+
+    def run(step):
+        lax.fori_loop(0, chunks, step, 0, unroll=UNROLL)
 
     def add_inflow(step, ref, refresh):
         def one(index, carry):
@@ -232,7 +188,7 @@
             d, row, j, col, inside = (listed[k, index] for k in range(5))
             values = lam[0, j, pl.ds(row, 1), :]
             value = jnp.sum(jnp.where(lane_row == col, values, 0.0), axis=1, keepdims=True)
-            spot = (lane_row == d + step * dam_ref.shape[0]) & (inside > 0)
+            spot = (lane_row == d + step * release_ref.shape[0]) & (inside > 0)
             return total + jnp.where(spot, (INFLOW_GAIN / TIME_RATIO) * value, 0.0)
 
         return lax.fori_loop(0, dams, one, gradient)
@@ -295,7 +251,7 @@
             )
         return carry
 
-    lax.fori_loop(0, chunks, first_step, 0)
+    run(first_step)
     add_inflow(0, state1, True)
 
     def second_step(i, carry):
@@ -317,7 +273,7 @@
             last[j, pl.ds(start, 8), :] = h[j] - TIME_RATIO * (gain[j] + (flux[j] - flux_low[j]))
         return carry
 
-    lax.fori_loop(0, chunks, second_step, 0)
+    run(second_step)
     add_inflow(1, last, False)
 
     def finish_depth(i, carry):
@@ -327,19 +283,8 @@
             lam[0, j, pl.ds(start, 8), :] = TIME_RATIO * (weight[j, pl.ds(start, 8), :] * height)
         return carry
 
-    lax.fori_loop(0, chunks, finish_depth, 0)
-
-    def store_depth(i, carry):
-        start = pl.multiple_of(i * 8, 8)
-        for j in inner:
-            part = pl.ds(j * LANES, LANES)
-            height = last[j, pl.ds(start + EDGE, 8), :]
-            depth_ref[pl.ds(start, 8), part] = jnp.where(
-                wet_ref[pl.ds(start, 8), part] > 0, height, h_ref[pl.ds(start, 8), part]
-            )
-        return carry
-
-    lax.fori_loop(0, rows // 8, store_depth, 0)
+    run(finish_depth)
+
     gradient = pick(1, jnp.zeros((1, LANES), jnp.float32))
 
     def second_back(i, carry):
@@ -384,7 +329,7 @@
             lam[2, j, pl.ds(start, 8), :] = TIME_RATIO * (to_low + high[j] + of_v * r[j])
         return carry
 
-    lax.fori_loop(0, chunks, second_back, 0)
+    run(second_back)
 
     def move_back(i, carry):
         start = pl.multiple_of(i * 8, 8)
@@ -392,9 +337,8 @@
             lam[0, j, pl.ds(start, 8), :] = back[4, j, pl.ds(start + 8, 8), :]
         return carry
 
-    lax.fori_loop(0, chunks, move_back, 0)
+    run(move_back)
     gradient = pick(0, gradient)
-    grad_ref[...] = jnp.broadcast_to(gradient, grad_ref.shape)
 
     def first_back(i, carry):
         start = pl.multiple_of(i * 8, 8)
@@ -441,7 +385,7 @@
             for j in every
         ]
         nh, th, jump, u_high, c_high = (previous_col([t[k] for t in terms]) for k in (2, 3, 4, 7, 8))
-        for j in inner:
+        for j in every:
             shut = ly[j] * at(walls, 3, j, start)
             normal = terms[j][0] + nh[j] - ly[j] * at(walls, 2, j, start)
             across = terms[j][1] + th[j]
@@ -449,81 +393,274 @@
             of_c = kept[j][3] + terms[j][6] + c_high[j] - shut * y[j]
             of_h = kept[j][1] + (jump[j] - terms[j][4]) + GRAVITY * h[j] * (kept[j][0] + normal)
             of_h = of_h + r[j] * (0.5 * (of_c * c[j]) - kept[j][2] - of_v * v[j])
-            result = (1.0 / TIME_RATIO) * lh[j] + of_h
-
-            @pl.when(i > 0)
+            final[j, pl.ds(start, 8), :] = (1.0 / TIME_RATIO) * lh[j] + of_h
+        return carry
+
+    run(first_back)
+    return gradient
+
+
+def list_dams(dam_ref, listed, rows, cols, spots):
+    total_cols = cols * lax.axis_size("gy")
+    row_first = lax.axis_index("gx") * rows
+    col_first = lax.axis_index("gy") * cols
+
+    def one(d, count):
+        cell = dam_ref[d]
+        row = lax.div(cell, jnp.int32(total_cols))
+        col = cell - row * total_cols - col_first
+        row = row - row_first
+        for held, spot in spots(row, col):
+            @pl.when(held)
             def _():
-                adjoint_ref[pl.ds(pl.multiple_of(jnp.maximum(start - EDGE, 0), 8), 8), pl.ds(j * LANES, LANES)] = result
-
-        return carry
-
-    lax.fori_loop(0, chunks - 1, first_back, 0)
+                for k, value in enumerate((d,) + spot):
+                    listed[k, count] = value
+
+            count = count + jnp.where(held, 1, 0)
+        return count
+
+    return lax.fori_loop(0, dam_ref.shape[0], one, 0, unroll=4)
+
+
+def within(value, first, end):
+    return (value >= first) & (value < end)
+
+
+def split(place):
+    return lax.shift_right_logical(place, LANES.bit_length() - 1), place & (LANES - 1)
+
+
+def inner_kernel(
+    h_ref, x_ref, y_ref, wet_ref, class_ref, rates_ref, dam_ref, release_ref,
+    depth_ref, adjoint_ref, grad_ref, listed, *scratch,
+):
+    rows, cols = h_ref.shape
+    tiles = cols // LANES
+    chunks = rows // 8
+
+    def spots(row, col):
+        tile, lane = split(col)
+        own = within(row, REACH, rows - REACH) & within(col, REACH, cols - REACH)
+        yield within(row, 0, rows) & within(col, 0, cols), (row, tile, lane, jnp.where(own, 1, 0))
+
+    dams = list_dams(dam_ref, listed, rows, cols, spots)
+
+    def put(fill):
+        def one(i, carry):
+            part = pl.ds(pl.multiple_of(i * 8, 8), 8)
+            for j in range(tiles):
+                across = pl.ds(j * LANES, LANES)
+                fill(
+                    j, pl.multiple_of(i * 8, 8), wet_ref[part, across] > 0,
+                    h_ref[part, across], x_ref[part, across], y_ref[part, across], class_ref[part, across],
+                )
+            return carry
+
+        lax.fori_loop(0, chunks, one, 0, unroll=2)
+
+    after = [(j + 1) % tiles for j in range(tiles)]
+    before = [(j - 1) % tiles for j in range(tiles)]
+    grad_ref[...] = window(chunks, after, before, put, rates_ref, listed, dams, release_ref, scratch)
+    last, final = scratch[6], scratch[9]
+    for j in range(tiles):
+        across = slice(j * LANES, (j + 1) * LANES)
+        depth_ref[:, across] = jnp.where(wet_ref[:, across] > 0, last[j, :rows, :], h_ref[:, across])
+        adjoint_ref[:, across] = final[j, :rows, :]
+
+
+def frame_kernel(
+    h_ref, x_ref, y_ref, wet_ref, class_ref, rates_ref, dam_ref, release_ref,
+    depth_in, adjoint_in, grad_in, low_ref, high_ref, left_ref, right_ref, side_ref, top_ref, bottom_ref,
+    depth_ref, adjoint_ref, grad_ref, listed, *scratch,
+):
+    rows, cols = h_ref.shape
+    tiles = cols // LANES
+    chunks = 4
+    turned = tiles + 1
+    after = [(j + 1) % turned for j in range(turned)] + [turned + 1, turned]
+    before = [(j - 1) % turned for j in range(turned)] + [turned + 1, turned]
+
+    def chunk_row(place, count):
+        return jnp.where(place < EDGE, place + EDGE, place - count + 3 * EDGE)
+
+    def near_end(place, count):
+        return within(place, -REACH, EDGE) | within(place, count - EDGE, count + REACH)
+
+    def at_end(place, count):
+        return within(place, 0, REACH) | within(place, count - REACH, count)
+
+    def spots(row, col):
+        near = within(row, -REACH, rows + REACH) & within(col, -REACH, cols + REACH)
+        tile, lane = split(jnp.where(col < 0, col + (tiles + 1) * LANES, col))
+        own = at_end(row, rows) & within(col, 0, cols)
+        yield near & near_end(row, rows), (chunk_row(row, rows), tile, lane, jnp.where(own, 1, 0))
+        tile, lane = split(jnp.where(row < 0, row + 2 * LANES, row))
+        own = at_end(col, cols) & within(row, REACH, rows - REACH)
+        yield near & near_end(col, cols), (chunk_row(col, cols), tile + turned, lane, jnp.where(own, 1, 0))
+
+    dams = list_dams(dam_ref, listed, rows, cols, spots)
+    place = lax.axis_index("gx")
+    above = jnp.where(place > 0, top_ref[...], 0.0)
+    below = jnp.where(place < lax.axis_size("gx") - 1, bottom_ref[...], 0.0)
+    left, right = beside(left_ref, right_ref)
+
+    def put(fill):
+        blank = jnp.zeros((EDGE - REACH, LANES), jnp.float32)
+
+        def coded(j, start, h, x, y, code):
+            fill(j, start, h > 0.0, h, x, y, code.astype(jnp.int32))
+
+        for j in range(tiles + 1):
+            across = slice(j * LANES, (j + 1) * LANES)
+            for start, strip in ((0, above), (3 * EDGE, below)):
+                pieces = [strip[k * REACH : (k + 1) * REACH, across] for k in range(FIELDS)]
+                coded(j, start, *(jnp.concatenate((blank, v) if start == 0 else (v, blank), axis=0) for v in pieces))
+            for end, first in ((0, 0), (1, rows - EDGE)):
+                start = (1 + end) * EDGE
+                if j < tiles:
+                    part = slice(first, first + EDGE)
+                    fill(
+                        j, start, wet_ref[part, across] > 0,
+                        h_ref[part, across], x_ref[part, across], y_ref[part, across], class_ref[part, across],
+                    )
+                else:
+                    coded(j, start, *(side_ref[end, k] for k in range(FIELDS)))
+        order = (0, 2, 1, 3)
+        for chunk, strip in enumerate((left, low_ref[...], high_ref[...], right)):
+            coded(turned, chunk * EDGE, *(strip[k * EDGE : (k + 1) * EDGE] for k in order))
+        strips = jnp.concatenate((above, below), axis=0)
+        outer = strips[:, tiles * LANES :]
+        mixed = jnp.zeros((2 * STRIP, LANES), jnp.float32)
+        lane = lax.broadcasted_iota(jnp.int32, (2 * STRIP, LANES), 1)
+        pieces = (
+            (outer, LANES - EDGE),
+            (strips[:, :LANES], 0),
+            (strips[:, (tiles - 1) * LANES : tiles * LANES], LANES - EDGE),
+            (outer, 0),
+        )
+        for chunk, (piece, first) in enumerate(pieces):
+            moved = (chunk * EDGE - first) % LANES
+            mixed = jnp.where(lane // EDGE == chunk, pltpu.roll(piece, moved, 1) if moved else piece, mixed)
+        corners = jnp.concatenate((mixed, jnp.zeros((LANES - 2 * STRIP, LANES), jnp.float32)), axis=0).T
+        corners = corners[: chunks * EDGE]
+        lane = lax.broadcasted_iota(jnp.int32, (chunks * EDGE, LANES), 1)
+        fields = []
+        for k in order:
+            from_above = pltpu.roll(corners, LANES - REACH - k * REACH, 1)
+            from_below = pltpu.roll(corners, LANES - STRIP - k * REACH, 1)
+            fields.append(jnp.where(lane < REACH, from_below, jnp.where(lane >= LANES - REACH, from_above, 0.0)))
+        for chunk in range(chunks):
+            coded(turned + 1, chunk * EDGE, *(v[chunk * EDGE : (chunk + 1) * EDGE] for v in fields))
+
+    gradient = window(chunks, after, before, put, rates_ref, listed, dams, release_ref, scratch)
+    grad_ref[...] = jnp.broadcast_to(gradient + grad_in[...], grad_ref.shape)
+
+    last, final = scratch[6], scratch[9]
+    blank = jnp.zeros((LANES - 4 * EDGE, LANES), jnp.float32)
+    ends = slice(EDGE, 3 * EDGE)
+    columns = jnp.concatenate((last[turned, ends, :], final[turned, ends, :], blank), axis=0).T
+    lane = lax.broadcasted_iota(jnp.int32, (rows, LANES), 1)
+    row = lax.broadcasted_iota(jnp.int32, (EDGE, LANES), 0)
+    for number, (ref, inner, strip) in enumerate(((depth_ref, depth_in, last), (adjoint_ref, adjoint_in, final))):
+        for j in range(tiles):
+            across = slice(j * LANES, (j + 1) * LANES)
+
+            def wet_only(value, part):
+                if number:
+                    return value
+                return jnp.where(wet_ref[part, across] > 0, value, h_ref[part, across])
+
+            whole = slice(0, rows)
+            block = inner[:, across]
+            if j == 0:
+                moved = (LANES - 2 * EDGE * number) % LANES
+                edge = pltpu.roll(columns, moved, 1) if moved else columns
+                block = jnp.where(lane < REACH, wet_only(edge, whole), block)
+            if j == tiles - 1:
+                edge = pltpu.roll(columns, LANES - 2 * EDGE - 2 * EDGE * number, 1)
+                block = jnp.where(lane >= LANES - REACH, wet_only(edge, whole), block)
+            middle = slice(EDGE, rows - EDGE)
+            ref[middle, across] = block[middle]
+            for part, start, own in (
+                (slice(0, EDGE), EDGE, row < REACH),
+                (slice(rows - EDGE, rows), 2 * EDGE, row >= EDGE - REACH),
+            ):
+                ref[part, across] = jnp.where(own, wet_only(strip[j, start : start + EDGE, :], part), block[part])
 
 
 def on_device(
     water_depth, momentum_x, momentum_y, wet_mask, damage_class, damage_rates, dam_cell, releases
 ):
     rows, cols = water_depth.shape
+    tiles = cols // LANES
     wide = cols + LANES
     rows_count = lax.axis_size("gx")
     cols_count = lax.axis_size("gy")
-    tiles = wide // LANES
-    tall = rows + 2 * EDGE + 8
     vmem = pl.BlockSpec(memory_space=pltpu.VMEM)
     smem = pl.BlockSpec(memory_space=pltpu.SMEM)
+    hbm = pl.BlockSpec(memory_space=pltpu.HBM)
     f32 = jnp.float32
     params = pltpu.CompilerParams(vmem_limit_bytes=48 * 1024 * 1024)
-    local = (water_depth, momentum_x, momentum_y, wet_mask, damage_class, damage_rates)
+    local = (water_depth, momentum_x, momentum_y, wet_mask, damage_class)
+    given = (damage_rates, dam_cell, releases)
 
     def shift(value, axis, count, step):
-        pairs = [(i, i + step) for i in range(count) if 0 <= i + step < count]
-        return lax.ppermute(value, axis, pairs)
+        return lax.ppermute(value, axis, [(i, (i + step) % count) for i in range(count)])
+
+    def array(*shape):
+        return jax.ShapeDtypeStruct(shape, f32)
+
+    def scratch(tiles, chunks, spots):
+        def cells(*lead):
+            return pltpu.VMEM(lead + (tiles, 8 * chunks + 8, LANES), f32)
+
+        listed = pltpu.SMEM((5, spots), jnp.int32)
+        return [listed, cells(7), cells(7), cells(), cells(2), cells(4), cells(), cells(), cells(3), cells(5), cells()]
 
     low, high = pl.pallas_call(
-        edge_columns_kernel,
-        out_shape=[jax.ShapeDtypeStruct((STRIP, rows), f32)] * 2,
-        in_specs=[vmem] * 5 + [smem],
+        edge_kernel,
+        out_shape=[array(FIELDS * EDGE, rows)] * 2,
+        in_specs=[hbm] * 5,
         out_specs=[vmem] * 2,
-        compiler_params=params,
-        name="edge_columns",
+        scratch_shapes=[
+            pltpu.VMEM((2, 3, rows, LANES), f32),
+            pltpu.VMEM((2, 2, rows, LANES), jnp.int32),
+            pltpu.SemaphoreType.DMA((2, 5)),
+        ],
+        compiler_params=pltpu.CompilerParams(vmem_limit_bytes=60 * 1024 * 1024),
+        name="edges",
     )(*local)
     right = shift(low, "gy", cols_count, -1)
     left = shift(high, "gy", cols_count, 1)
-    side, low, high = pl.pallas_call(
-        edge_rows_kernel,
-        out_shape=[
-            jax.ShapeDtypeStruct((FIELDS, rows, LANES), f32),
-            jax.ShapeDtypeStruct((STRIP, wide), f32),
-            jax.ShapeDtypeStruct((STRIP, wide), f32),
-        ],
-        in_specs=[vmem] * 5 + [smem] + [vmem] * 2,
+    depth, adjoint, gradient = pl.pallas_call(
+        inner_kernel,
+        out_shape=[array(rows, cols), array(rows, cols), array(1, LANES)],
+        in_specs=[vmem] * 5 + [smem] * 3,
+        out_specs=[vmem] * 3,
+        scratch_shapes=scratch(tiles, rows // 8, dam_cell.shape[0]),
+        compiler_params=params,
+        cost_estimate=pl.CostEstimate(flops=500 * rows * cols, bytes_accessed=7 * 4 * rows * cols, transcendentals=0),
+        name="inner",
+    )(*local, *given)
+    side, to_top, to_bottom = pl.pallas_call(
+        corner_kernel,
+        out_shape=[array(2, FIELDS, EDGE, LANES), array(STRIP, wide), array(STRIP, wide)],
+        in_specs=[vmem] * 7,
         out_specs=[vmem] * 3,
         compiler_params=params,
-        name="edge_rows",
+        name="corners",
     )(*local, left, right)
-    bottom = shift(low, "gx", rows_count, -1)
-    top = shift(high, "gx", rows_count, 1)
-
-    def cells(*lead):
-        return pltpu.VMEM(lead + (tiles, tall, LANES), f32)
-
-    devices = rows_count * cols_count
+    bottom = shift(to_top, "gx", rows_count, -1)
+    top = shift(to_bottom, "gx", rows_count, 1)
     depth, adjoint, parts = pl.pallas_call(
-        window_kernel,
-        out_shape=[
-            jax.ShapeDtypeStruct((rows, cols), f32),
-            jax.ShapeDtypeStruct((rows, cols), f32),
-            jax.ShapeDtypeStruct((devices, LANES), f32),
-        ],
-        in_specs=[vmem] * 5 + [smem] + [vmem] * 3 + [smem] * 2,
+        frame_kernel,
+        out_shape=[array(rows, cols), array(rows, cols), array(rows_count * cols_count, LANES)],
+        in_specs=[vmem] * 5 + [smem] * 3 + [vmem] * 10,
         out_specs=[vmem] * 3,
-        scratch_shapes=[
-            cells(7), cells(7), cells(), cells(2), cells(4), cells(), cells(), cells(3), cells(5),
-            pltpu.SMEM((5, dam_cell.shape[0]), jnp.int32),
-        ],
+        scratch_shapes=scratch(tiles + 3, 4, 2 * dam_cell.shape[0]),
         compiler_params=params,
-        name="window",
-    )(*local, side, top, bottom, dam_cell, releases)
+        name="frame",
+    )(*local, *given, depth, adjoint, gradient, low, high, left, right, side, top, bottom)
     gathered = lax.all_to_all(parts, ("gx", "gy"), 0, 0)
     release_grad = jnp.sum(gathered, axis=0).reshape(releases.shape[1], releases.shape[0]).T
     return (depth, adjoint, release_grad)

time: 81.4 us -> 64.3 us (0.79)
  waiting for transfers between devices: 10.7 us -> 2.83 us
  local copies, waits for them, and re-layouts: 6.18 us -> 0.79 us
  Pallas kernels: 20.9 us -> 18.5 us
  starting transfers between devices: 16.2 us -> 13.9 us
  blocking collectives: 25.9 us -> 27.1 us
    ppermute x4, waiting for transfers between devices: 10.7 us -> 2.83 us  [shift(): lax.ppermute(value, axis, [(i, (i + step) % count) for i in range(count)])]
    unnamed x29 -> x21, local copies, waits for them, and re-layouts: 5.54 us -> 0.14 us
    pallas_call x3 -> x4, Pallas kernels: 20.9 us -> 18.5 us  [the longest x1 9.45 us: on_device(): pl.pallas_call(inner_kernel, out_shape=[array(rows, cols), array(rows, co...]
    ppermute x4, starting transfers between devices: 16.2 us -> 13.9 us  [shift(): lax.ppermute(value, axis, [(i, (i + step) % count) for i in range(count)])]
    all_to_all x1, blocking collectives: 25.9 us -> 27.1 us  [on_device(): gathered = lax.all_to_all(parts, ('gx', 'gy'), 0, 0)]
  transfers between devices with their start and end apart: 4 -> 4, of which waited for: 2 -> 2; matrix products, arithmetic and copies ran while one was open for 0% -> 0% of each run, Pallas kernels for 0% -> 15%
where the time goes in v1:
time: 64.3 us; the launch traced here: 64.2 us
  blocking collectives  27.1 us (42%)
  Pallas kernels  18.5 us (29%)
  starting transfers between devices  13.9 us (22%)
  waiting for transfers between devices  2.83 us (4%)
  local copies, waits for them, and re-layouts  0.79 us (1%)
  between operations  0.78 us (1%)
    all_to_all x1, blocking collectives, on_device(): gathered = lax.all_to_all(parts, ('gx', 'gy'), 0, 0)  27.1 us
    ppermute x4, starting transfers between devices, shift(): lax.ppermute(value, axis, [(i, (i + step) % count) for i in range(count)])  13.9 us
    pallas_call x1, Pallas kernels, on_device(): pl.pallas_call(inner_kernel, out_shape=[array(rows, cols), array(rows, co...  9.45 us
    pallas_call x1, Pallas kernels, on_device(): pl.pallas_call(frame_kernel, out_shape=[array(rows, cols), array(rows, co...  6.74 us
    ppermute x4, waiting for transfers between devices, shift(): lax.ppermute(value, axis, [(i, (i + step) % count) for i in range(count)])  2.83 us
    pallas_call x1, Pallas kernels, on_device(): pl.pallas_call(edge_kernel, out_shape=[array(FIELDS * EDGE, rows)] * 2, i...  2.14 us
  transfers between devices with their start and end apart: 4, of which 2 were waited for; matrix products, arithmetic and copies ran while one was open for 0% of the time, Pallas kernels for 15%

profile of v1, /device:TPU:1, one launch (start us, length us, event | category | flops | bytes accessed | tf_op | source)
XLA Modules:
  0.0 64.2 jit_solution(2477635446240659967)
XLA Ops:
  0.7 2.1 %edges.1 = (f32[32,128]{1,0:T(8,128)}, f32[32,128]{1,0:T(8,128)}) custom-call(f32[128,512]{1,0:T(8,128)} %h_ref.5, f32[128,512]{1,0:T(8,128)} %x_ref.5, f32[128,512]{1,0:T(8,128)} %y_ref.5, s32[128,512]{1,0:T(8,128)} %wet_ref.5, s32[128,512]{1,0:T(8,128)} %class_ref.5), custom_call_target="tpu_custom_call" | custom-call | tf_op jit(solution)/shard_map/edges/pallas_call | solution.py:620
  2.8 3.3 %collective-permute-start.1 = (f32[32,128]{1,0:T(8,128)}, f32[32,128]{1,0:T(8,128)S(1)}, u32[]{:S(2)}, u32[]{:S(2)}) collective-permute-start(f32[32,128]{1,0:T(8,128)} %get-tuple-element.17.low_ref), channel_id=1, source_target_pairs={{0,15},{1,0},{2,1},{3,2},{4,3},{5,4},{6,5},{7,6},{8,7},{9,8},{10,9... | collective-permute-start | bytes 49160 | tf_op jit(solution)/shard_map/ppermute | solution.py:608
  6.1 5.1 %collective-permute-start = (f32[32,128]{1,0:T(8,128)}, f32[32,128]{1,0:T(8,128)S(1)}, u32[]{:S(2)}, u32[]{:S(2)}) collective-permute-start(f32[32,128]{1,0:T(8,128)} %get-tuple-element.18.high_ref), channel_id=1, source_target_pairs={{0,1},{1,2},{2,3},{3,4},{4,5},{5,6},{6,7},{7,8},{8,9},{9,10},{10,1... | collective-permute-start | bytes 49160 | tf_op jit(solution)/shard_map/ppermute | solution.py:608
  11.3 1.5 %collective-permute-done.1.right_ref = f32[32,128]{1,0:T(8,128)S(1)} collective-permute-done((f32[32,128]{1,0:T(8,128)}, f32[32,128]{1,0:T(8,128)S(1)}, u32[]{:S(2)}, u32[]{:S(2)}) %collective-permute-start.1) | collective-permute-done | bytes 16416 | tf_op jit(solution)/shard_map/ppermute | solution.py:608
  12.8 1.3 %collective-permute-done.left_ref = f32[32,128]{1,0:T(8,128)S(1)} collective-permute-done((f32[32,128]{1,0:T(8,128)}, f32[32,128]{1,0:T(8,128)S(1)}, u32[]{:S(2)}, u32[]{:S(2)}) %collective-permute-start) | collective-permute-done | bytes 16416 | tf_op jit(solution)/shard_map/ppermute | solution.py:608
  14.1 0.0 copy-done.3
  14.2 0.2 corners.1
  14.3 0.0 copy-start.9
  14.4 0.8 %collective-permute-start.2 = (f32[16,640]{1,0:T(8,128)S(1)}, f32[16,640]{1,0:T(8,128)S(1)}, u32[]{:S(2)}, u32[]{:S(2)}) collective-permute-start(f32[16,640]{1,0:T(8,128)S(1)} %get-tuple-element.20), channel_id=1, source_target_pairs={{0,16},{16,32},{32,48},{48,64},{64,80},{80,96},{96,112},{112,128},... | collective-permute-start | bytes 122888 | tf_op jit(solution)/shard_map/ppermute | solution.py:608
  15.2 4.6 %collective-permute-start.3 = (f32[16,640]{1,0:T(8,128)S(1)}, f32[16,640]{1,0:T(8,128)S(1)}, u32[]{:S(2)}, u32[]{:S(2)}) collective-permute-start(f32[16,640]{1,0:T(8,128)S(1)} %get-tuple-element.21), channel_id=1, source_target_pairs={{0,240},{16,0},{32,16},{48,32},{64,48},{80,64},{96,80},{112,96},{1... | collective-permute-start | bytes 122888 | tf_op jit(solution)/shard_map/ppermute | solution.py:608
  19.8 0.0 copy-done.9
  19.8 0.1 copy.14.release_ref
  19.9 0.0 copy-done.7
  19.9 0.0 copy-start.5
  19.9 0.0 copy-start.6
  19.9 9.5 %inner.1 = (f32[128,512]{1,0:T(8,128)S(1)}, f32[128,512]{1,0:T(8,128)S(1)}, f32[1,128]{1,0:T(1,128)S(1)}) custom-call(f32[128,512]{1,0:T(8,128)S(1)} %copy-done, f32[128,512]{1,0:T(8,128)S(1)} %copy-done.1, f32[128,512]{1,0:T(8,128)S(1)} %copy-done.2, s32[128,512]{1,0:T(8,128)S(1)} %copy-done.3, s32[128,512]{1,0:T(8,128)S(1)} %copy-done.4, f32[8]{0:T(128)S(1)} %copy-done.7, ...), custom_call_target="tpu_custom_call" | custom-call | flops 32768000 | bytes 1835008 | tf_op jit(solution)/shard_map/inner/pallas_call | solution.py:635
  29.4 0.0 collective-permute-done.2.top_ref
  29.4 0.0 collective-permute-done.3.bottom_ref
  29.4 0.0 copy-done.5
  29.4 0.0 copy-done.6
  29.4 6.7 %frame.1 = (f32[128,512]{1,0:T(8,128)}, f32[128,512]{1,0:T(8,128)}, f32[256,128]{1,0:T(8,128)S(1)}) custom-call(f32[128,512]{1,0:T(8,128)S(1)} %copy-done, f32[128,512]{1,0:T(8,128)S(1)} %copy-done.1, f32[128,512]{1,0:T(8,128)S(1)} %copy-done.2, s32[128,512]{1,0:T(8,128)S(1)} %copy-done.3, s32[128,512]{1,0:T(8,128)S(1)} %copy-done.4, f32[8]{0:T(128)S(1)} %copy-done.7, ...), custom_call_target="tpu_custom_call" | custom-call | tf_op jit(solution)/shard_map/frame/pallas_call | solution.py:655
  36.2 27.1 %all_to_all.9 = f32[256,1,128]{2,1,0:T(1,128)S(1)} all-to-all(f32[256,1,128]{2,1,0:T(1,128)S(1)} %bitcast.4), channel_id=1, replica_groups=mesh['gx'=16,'gy'=16] {'gx','gy'}, dimensions={0} | all-to-all | bytes 262144 | tf_op jit(solution)/shard_map/all_to_all | solution.py:664
  63.2 0.3 reduce_sum.9
  63.5 0.6 %reshape.11 = f32[2,64]{1,0:T(2,128)} reshape(f32[128]{0:T(128)S(1)} %reduce_sum.9) | data formatting | bytes 1024 | tf_op jit(solution)/shard_map/reshape | solution.py:665
  (12 shorter events, 0.0 us)
Async XLA Ops:
  0.6 13.5 %copy-start.4 = (s32[128,512]{1,0:T(8,128)S(1)}, s32[128,512]{1,0:T(8,128)}, u32[]{:S(2)}) copy-start(s32[128,512]{1,0:T(8,128)} %class_ref.5) | copy-start | bytes 786436
  0.6 13.5 %copy-start.3 = (s32[128,512]{1,0:T(8,128)S(1)}, s32[128,512]{1,0:T(8,128)}, u32[]{:S(2)}) copy-start(s32[128,512]{1,0:T(8,128)} %wet_ref.5) | copy-start | bytes 786436
  0.7 13.5 %copy-start.2 = (f32[128,512]{1,0:T(8,128)S(1)}, f32[128,512]{1,0:T(8,128)}, u32[]{:S(2)}) copy-start(f32[128,512]{1,0:T(8,128)} %y_ref.5) | copy-start | bytes 786436
  0.7 13.5 %copy-start.1 = (f32[128,512]{1,0:T(8,128)S(1)}, f32[128,512]{1,0:T(8,128)}, u32[]{:S(2)}) copy-start(f32[128,512]{1,0:T(8,128)} %x_ref.5) | copy-start | bytes 786436
  0.7 13.5 %copy-start = (f32[128,512]{1,0:T(8,128)S(1)}, f32[128,512]{1,0:T(8,128)}, u32[]{:S(2)}) copy-start(f32[128,512]{1,0:T(8,128)} %h_ref.5) | copy-start | bytes 786436
  2.8 10.0 %collective-permute-start.1 = (f32[32,128]{1,0:T(8,128)}, f32[32,128]{1,0:T(8,128)S(1)}, u32[]{:S(2)}, u32[]{:S(2)}) collective-permute-start(f32[32,128]{1,0:T(8,128)} %get-tuple-element.17.low_ref), channel_id=1, source_target_pairs={{0,15},{1,0},{2,1},{3,2},{4,3},{5,4},{6,5},{7,6},{8,7},{9,8},{10,9... | collective-permute-start | bytes 49160 | tf_op jit(solution)/shard_map/ppermute | solution.py:608
  6.1 8.0 %collective-permute-start = (f32[32,128]{1,0:T(8,128)}, f32[32,128]{1,0:T(8,128)S(1)}, u32[]{:S(2)}, u32[]{:S(2)}) collective-permute-start(f32[32,128]{1,0:T(8,128)} %get-tuple-element.18.high_ref), channel_id=1, source_target_pairs={{0,1},{1,2},{2,3},{3,4},{4,5},{5,6},{6,7},{7,8},{8,9},{9,10},{10,1... | collective-permute-start | bytes 49160 | tf_op jit(solution)/shard_map/ppermute | solution.py:608
  14.3 5.5 %copy-start.9 = (f32[64,2]{0,1:T(2,128)S(1)}, f32[64,2]{0,1:T(2,128)}, u32[]{:S(2)}) copy-start(f32[64,2]{0,1:T(2,128)} %param.15) | copy-start | bytes 1540
  14.4 15.1 %collective-permute-start.2 = (f32[16,640]{1,0:T(8,128)S(1)}, f32[16,640]{1,0:T(8,128)S(1)}, u32[]{:S(2)}, u32[]{:S(2)}) collective-permute-start(f32[16,640]{1,0:T(8,128)S(1)} %get-tuple-element.20), channel_id=1, source_target_pairs={{0,16},{16,32},{32,48},{48,64},{64,80},{80,96},{96,112},{112,128},... | collective-permute-start | bytes 122888 | tf_op jit(solution)/shard_map/ppermute | solution.py:608
  15.2 4.7 %copy-start.7 = (f32[8]{0:T(128)S(1)}, f32[8]{0:T(128)}, u32[]{:S(2)}) copy-start(f32[8]{0:T(128)} %rates_ref.3) | copy-start | bytes 100
  15.2 4.7 %copy-start.8 = (s32[64]{0:T(128)S(1)}, s32[64]{0:T(128)}, u32[]{:S(2)}) copy-start(s32[64]{0:T(128)} %dam_ref.3) | copy-start | bytes 772
  15.2 14.2 %collective-permute-start.3 = (f32[16,640]{1,0:T(8,128)S(1)}, f32[16,640]{1,0:T(8,128)S(1)}, u32[]{:S(2)}, u32[]{:S(2)}) collective-permute-start(f32[16,640]{1,0:T(8,128)S(1)} %get-tuple-element.21), channel_id=1, source_target_pairs={{0,240},{16,0},{32,16},{48,32},{64,48},{80,64},{96,80},{112,96},{1... | collective-permute-start | bytes 122888 | tf_op jit(solution)/shard_map/ppermute | solution.py:608
  19.9 9.5 %copy-start.5 = (f32[32,128]{1,0:T(8,128)S(1)}, f32[32,128]{1,0:T(8,128)}, u32[]{:S(2)}) copy-start(f32[32,128]{1,0:T(8,128)} %get-tuple-element.17.low_ref) | copy-start | bytes 49156
  19.9 9.5 %copy-start.6 = (f32[32,128]{1,0:T(8,128)S(1)}, f32[32,128]{1,0:T(8,128)}, u32[]{:S(2)}) copy-start(f32[32,128]{1,0:T(8,128)} %get-tuple-element.18.high_ref) | copy-start | bytes 49156

commit v2 on v1

v2 whole, which is shorter than its diff:
```python
import itertools

import jax
import jax.numpy as jnp
from jax import lax
from jax.experimental import pallas as pl
from jax.experimental.pallas import tpu as pltpu
from jax.sharding import PartitionSpec as P

GRAVITY = 9.81
TIME_RATIO = 0.05
INFLOW_GAIN = 0.25

LANES = 128
REACH = 4
EDGE = 8
FIELDS = 4
STRIP = FIELDS * REACH
UNROLL = True


def class_rate(classes, rates_ref):
    rate = jnp.full(classes.shape, rates_ref[0], jnp.float32)
    for index in range(1, rates_ref.shape[0]):
        rate = jnp.where(classes == index, rates_ref[index], rate)
    return rate


def coded_fields(h, x, y, wet, classes):
    return jnp.where(wet > 0, h, 0.0), x, y, classes.astype(jnp.float32)


def edge_kernel(h_hbm, x_hbm, y_hbm, wet_hbm, class_hbm, low_ref, high_ref, values, codes, sems):
    rows, cols = h_hbm.shape
    copies = []
    for index, source in enumerate((h_hbm, x_hbm, y_hbm, wet_hbm, class_hbm)):
        for side in range(2):
            kept = values.at[side, index] if index < 3 else codes.at[side, index - 3]
            part = source.at[:, pl.ds(side * (cols - LANES), LANES)]
            copies.append(pltpu.make_async_copy(part, kept, sems.at[side, index]))
    for copy in copies:
        copy.start()
    for copy in copies:
        copy.wait()
    lane = lax.broadcasted_iota(jnp.int32, (rows, LANES), 1)
    mixed = jnp.zeros((rows, LANES), jnp.float32)
    for side in range(2):
        fields = coded_fields(*(values[side, k] for k in range(3)), *(codes[side, k] for k in range(2)))
        for index, field in enumerate(fields):
            first = (side * FIELDS + index) * EDGE
            moved = first if side == 0 else first + EDGE
            shifted = pltpu.roll(field, moved, 1) if moved else field
            mixed = jnp.where((lane >= first) & (lane < first + EDGE), shifted, mixed)
    turned = mixed.T
    low_ref[...] = turned[: FIELDS * EDGE]
    high_ref[...] = turned[FIELDS * EDGE : 2 * FIELDS * EDGE]


def beside(left_ref, right_ref):
    place = lax.axis_index("gy")
    left = jnp.where(place > 0, left_ref[...], 0.0)
    right = jnp.where(place < lax.axis_size("gy") - 1, right_ref[...], 0.0)
    return left, right


def corner_kernel(ends_ref, left_ref, right_ref, side_ref, low_ref, high_ref):
    rows = left_ref.shape[1]
    cols = ends_ref.shape[2]
    left, right = beside(left_ref, right_ref)
    blank = jnp.zeros((LANES - 2 * FIELDS * EDGE, rows), jnp.float32)
    turned = jnp.concatenate((right, left, blank), axis=0).T
    lane = lax.broadcasted_iota(jnp.int32, (EDGE, LANES), 1)
    for end, (ref, start, kept) in enumerate(((low_ref, 0, 0), (high_ref, rows - EDGE, EDGE - REACH))):
        part = turned[start : start + EDGE]
        ref[:, :cols] = ends_ref[end]
        for index in range(FIELDS):
            upper = pltpu.roll(part, LANES - index * EDGE, 1) if index else part
            lower = pltpu.roll(part, LANES - (1 + FIELDS + index) * EDGE, 1)
            tile = jnp.where(lane < EDGE, upper, jnp.where(lane >= LANES - EDGE, lower, 0.0))
            side_ref[end, index] = tile
            ref[index * REACH : (index + 1) * REACH, cols:] = tile[kept : kept + REACH]


def cell_terms(height, flow_x, flow_y):
    scaled = GRAVITY * height
    inverse = pltpu.reciprocal(height, approx=True)
    return flow_x * inverse, flow_y * inverse, scaled * lax.rsqrt(scaled), inverse


def waves(u_low, c_low, u_high, c_high, both):
    slow_low, slow_high = u_low - c_low, u_high - c_high
    fast_low, fast_high = u_low + c_low, u_high + c_high
    slowest = jnp.minimum(jnp.minimum(slow_low, slow_high), 0.0)
    fastest = jnp.maximum(jnp.maximum(fast_low, fast_high), 0.0)
    inverse = both * pltpu.reciprocal(fastest - slowest, approx=True)
    share_low = fastest * inverse
    share_high = -(slowest * inverse)
    spread = slowest * share_low
    return slowest, fastest, inverse, share_low, share_high, spread, slow_low <= slow_high, fast_low >= fast_high


def speed_terms(slowest, fastest, of_slowest, of_fastest, slow_is_low, fast_is_low):
    of_slowest = jnp.where(slowest < 0.0, of_slowest, 0.0)
    of_fastest = jnp.where(fastest > 0.0, of_fastest, 0.0)
    slow_to_low = jnp.where(slow_is_low, of_slowest, 0.0)
    fast_to_low = jnp.where(fast_is_low, of_fastest, 0.0)
    slow_to_high = of_slowest - slow_to_low
    fast_to_high = of_fastest - fast_to_low
    return (
        fast_to_low + slow_to_low,
        fast_to_low - slow_to_low,
        fast_to_high + slow_to_high,
        fast_to_high - slow_to_high,
    )


def window(chunks, after, before, put, listed, dams, rates_ref, release_ref, held):
    state0, state1, mask, faces, walls, weight, last, lam0, lam, back, final = (
        held.get(name) for name in (
            "state0", "state1", "mask", "faces", "walls", "weight", "last", "lam0", "lam", "back", "final",
        )
    )
    tiles = len(after)
    every = range(tiles)
    lane = lax.broadcasted_iota(jnp.int32, (8, LANES), 1)

    def at(ref, k, j, start):
        return ref[k, j, pl.ds(start, 8), :]

    def next_col(values):
        rolled = [pltpu.roll(v, LANES - 1, 1) for v in values]
        return [jnp.where(lane == LANES - 1, rolled[after[j]], rolled[j]) for j in every]

    def previous_col(values):
        rolled = [pltpu.roll(v, 1, 1) for v in values]
        return [jnp.where(lane == 0, rolled[before[j]], rolled[j]) for j in every]

    def previous_row(slot, j, start, value):
        back[slot, j, pl.ds(start + 8, 8), :] = value
        return back[slot, j, pl.ds(start + 7, 8), :]

    def put_cell(ref, j, start, height, flow_x, flow_y):
        u, v, c, inverse = cell_terms(height, flow_x, flow_y)
        for k, value in enumerate((height, flow_x, flow_y, u, v, c, inverse)):
            ref[k, j, pl.ds(start, 8), :] = value

    def fill(j, start, wet, height, flow_x, flow_y, classes):
        put_cell(
            state0, j, start,
            jnp.where(wet, height, 1.0), jnp.where(wet, flow_x, 0.0), jnp.where(wet, flow_y, 0.0),
        )
        mask[j, pl.ds(start, 8), :] = jnp.where(wet, 1.0, 0.0)
        weight[j, pl.ds(start, 8), :] = jnp.where(wet, class_rate(classes, rates_ref), 0.0)

    def clear(ref, start, value=0.0):
        index = tuple(range(n) for n in ref.shape[:-2])
        for lead in itertools.product(*index):
            ref[lead + (pl.ds(start, 8), slice(None))] = jnp.full((8, LANES), value, jnp.float32)

    def run(step):
        lax.fori_loop(0, chunks, step, 0, unroll=UNROLL)

    def add_inflow(step, ref, refresh):
        def one(index, carry):
            d, row, j, col = (listed[k, index] for k in range(4))
            if refresh:
                old = [ref[k, j, pl.ds(row, 1), :] for k in range(3)]
            else:
                old = [ref[j, pl.ds(row, 1), :]]
            here = lax.broadcasted_iota(jnp.int32, (1, LANES), 1) == col
            height = old[0] + jnp.where(here, INFLOW_GAIN * release_ref[d, step], 0.0)
            if refresh:
                terms = (height, old[1], old[2]) + cell_terms(height, old[1], old[2])
                for k, value in enumerate(terms):
                    ref[k, j, pl.ds(row, 1), :] = value
            else:
                ref[j, pl.ds(row, 1), :] = height
            return carry

        lax.fori_loop(0, dams, one, 0)

    def pick(step, ref, gradient):
        lane_row = lax.broadcasted_iota(jnp.int32, (1, LANES), 1)

        def one(index, total):
            d, row, j, col, inside = (listed[k, index] for k in range(5))
            values = ref[j, pl.ds(row, 1), :]
            value = jnp.sum(jnp.where(lane_row == col, values, 0.0), axis=1, keepdims=True)
            spot = (lane_row == d + step * release_ref.shape[0]) & (inside > 0)
            return total + jnp.where(spot, (INFLOW_GAIN / TIME_RATIO) * value, 0.0)

        return lax.fori_loop(0, dams, one, gradient)

    def forward():
        clear(back, 0)
        for ref in (state0, state1):
            for k in range(7):
                clear(ref.at[k], chunks * 8, 1.0 if k in (0, 5, 6) else 0.0)
        clear(mask, chunks * 8)
        clear(lam0, chunks * 8)
        put(fill)

        def first_step(i, carry):
            start = pl.multiple_of(i * 8, 8)
            low = [[at(state0, k, j, start) for j in every] for k in range(6)]
            h, x, y, u, v, c = low
            m = [mask[j, pl.ds(start, 8), :] for j in every]
            half = [(0.5 * GRAVITY) * h[j] * h[j] for j in every]
            cross = [x[j] * v[j] for j in every]
            press_x = [x[j] * u[j] + half[j] for j in every]
            press_y = [y[j] * v[j] + half[j] for j in every]
            gain = []
            for j in every:
                hn, xn, yn, un, cn = (at(state0, k, j, start + 1) for k in (0, 1, 2, 3, 5))
                both = m[j] * mask[j, pl.ds(start + 1, 8), :]
                faces[0, j, pl.ds(start, 8), :] = both
                _, _, _, wl, wh, sp, _, _ = waves(u[j], c[j], un, cn, both)
                fh = wl * x[j] + wh * xn + sp * (hn - h[j])
                fn = wl * press_x[j] + wh * (xn * un + (0.5 * GRAVITY) * hn * hn) + sp * (xn - x[j])
                ft = wl * cross[j] + wh * (yn * un) + sp * (yn - y[j])
                both_low = previous_row(0, j, start, both)
                tilt = both_low - both
                shut = 2.0 * m[j] - both - both_low
                walls[0, j, pl.ds(start, 8), :] = tilt
                walls[1, j, pl.ds(start, 8), :] = shut
                gain.append(
                    [
                        fh - previous_row(1, j, start, fh),
                        fn - previous_row(2, j, start, fn) + tilt * press_x[j] + shut * ((jnp.abs(u[j]) + c[j]) * x[j]),
                        ft - previous_row(3, j, start, ft),
                    ]
                )
            hn, xn, yn, vn, cn, pn, tn, mn = (next_col(q) for q in (h, x, y, v, c, press_y, cross, m))
            flux = [[], [], []]
            both_up = []
            for j in every:
                both = m[j] * mn[j]
                faces[1, j, pl.ds(start, 8), :] = both
                both_up.append(both)
                _, _, _, wl, wh, sp, _, _ = waves(v[j], c[j], vn[j], cn[j], both)
                flux[0].append(wl * y[j] + wh * yn[j] + sp * (hn[j] - h[j]))
                flux[1].append(wl * press_y[j] + wh * pn[j] + sp * (yn[j] - y[j]))
                flux[2].append(wl * cross[j] + wh * tn[j] + sp * (xn[j] - x[j]))
            flux_low = [previous_col(q) for q in flux]
            both_low = previous_col(both_up)
            for j in every:
                tilt = both_low[j] - both_up[j]
                shut = 2.0 * m[j] - both_up[j] - both_low[j]
                walls[2, j, pl.ds(start, 8), :] = tilt
                walls[3, j, pl.ds(start, 8), :] = shut
                change_h = gain[j][0] + (flux[0][j] - flux_low[0][j])
                change_x = gain[j][1] + (flux[2][j] - flux_low[2][j])
                change_y = gain[j][2] + (flux[1][j] - flux_low[1][j])
                change_y = change_y + tilt * press_y[j] + shut * ((jnp.abs(v[j]) + c[j]) * y[j])
                put_cell(
                    state1, j, start,
                    h[j] - TIME_RATIO * change_h, x[j] - TIME_RATIO * change_x, y[j] - TIME_RATIO * change_y,
                )
            return carry

        run(first_step)
        add_inflow(0, state1, True)

        def second_step(i, carry):
            start = pl.multiple_of(i * 8, 8)
            h, x, y, u, v, c = [[at(state1, k, j, start) for j in every] for k in range(6)]
            gain = []
            for j in every:
                hn, xn, un, cn = (at(state1, k, j, start + 1) for k in (0, 1, 3, 5))
                _, _, _, wl, wh, sp, _, _ = waves(u[j], c[j], un, cn, at(faces, 0, j, start))
                fh = wl * x[j] + wh * xn + sp * (hn - h[j])
                gain.append(fh - previous_row(0, j, start, fh))
            hn, yn, vn, cn = (next_col(q) for q in (h, y, v, c))
            flux = []
            for j in every:
                _, _, _, wl, wh, sp, _, _ = waves(v[j], c[j], vn[j], cn[j], at(faces, 1, j, start))
                flux.append(wl * y[j] + wh * yn[j] + sp * (hn[j] - h[j]))
            flux_low = previous_col(flux)
            for j in every:
                last[j, pl.ds(start, 8), :] = h[j] - TIME_RATIO * (gain[j] + (flux[j] - flux_low[j]))
            return carry

        run(second_step)
        add_inflow(1, last, False)

        def finish_depth(i, carry):
            start = pl.multiple_of(i * 8, 8)
            for j in every:
                height = last[j, pl.ds(start, 8), :]
                lam0[j, pl.ds(start, 8), :] = TIME_RATIO * (weight[j, pl.ds(start, 8), :] * height)
            return carry

        run(finish_depth)

        return pick(1, lam0, jnp.zeros((1, LANES), jnp.float32))


    def backward(gradient):
        clear(back, 0)
        clear(lam, chunks * 8)

        def second_back(i, carry):
            start = pl.multiple_of(i * 8, 8)
            h, x, y, u, v, c, r = [[at(state1, k, j, start) for j in every] for k in range(7)]
            lh = [lam0[j, pl.ds(start, 8), :] for j in every]

            def face(hl, nl, ul, cl, hh, nh, uh, ch, gl, gh, both):
                slow, fast, inv, wl, wh, sp, slow_low, fast_low = waves(ul, cl, uh, ch, both)
                g = gh - gl
                dn, dh = nh - nl, hh - hl
                to_low, to_high = wl * g, wh * g
                of_slow = -(to_low * inv) * (dn - fast * dh)
                of_fast = -(to_high * inv) * (dn - slow * dh)
                return (to_low, to_high, sp * g) + speed_terms(slow, fast, of_slow, of_fast, slow_low, fast_low)

            partial_h, partial_u, partial_c, flow = [], [], [], []
            for j in every:
                hn, xn, un, cn = (at(state1, k, j, start + 1) for k in (0, 1, 3, 5))
                to_low, to_high, jump, u_low, c_low, u_high, c_high = face(
                    h[j], x[j], u[j], c[j], hn, xn, un, cn, lh[j], lam0[j, pl.ds(start + 1, 8), :], at(faces, 0, j, start)
                )
                of_u = u_low + previous_row(2, j, start, u_high)
                partial_h.append(previous_row(0, j, start, jump) - jump)
                partial_c.append(c_low + previous_row(3, j, start, c_high))
                partial_u.append(of_u * u[j])
                flow.append(to_low + previous_row(1, j, start, to_high) + of_u * r[j])
            hn, yn, vn, cn, ln = (next_col(q) for q in (h, y, v, c, lh))
            terms = [
                face(h[j], y[j], v[j], c[j], hn[j], yn[j], vn[j], cn[j], lh[j], ln[j], at(faces, 1, j, start))
                for j in every
            ]
            high, jump, u_high, c_high = (previous_col([t[k] for t in terms]) for k in (1, 2, 5, 6))
            for j in every:
                to_low, _, own_jump, u_low, c_low, _, _ = terms[j]
                of_v = u_low + u_high[j]
                of_c = partial_c[j] + c_low + c_high[j]
                of_h = partial_h[j] + (jump[j] - own_jump)
                of_h = of_h + r[j] * (0.5 * (of_c * c[j]) - partial_u[j] - of_v * v[j])
                lam[0, j, pl.ds(start, 8), :] = lh[j] + TIME_RATIO * of_h
                lam[1, j, pl.ds(start, 8), :] = TIME_RATIO * flow[j]
                lam[2, j, pl.ds(start, 8), :] = TIME_RATIO * (to_low + high[j] + of_v * r[j])
            return carry

        run(second_back)

        gradient = pick(0, lam.at[0], gradient)

        def first_back(i, carry):
            start = pl.multiple_of(i * 8, 8)
            h, x, y, u, v, c, r = [[at(state0, k, j, start) for j in every] for k in range(7)]
            lh, lx, ly = [[at(lam, k, j, start) for j in every] for k in range(3)]
            half = [(0.5 * GRAVITY) * h[j] * h[j] for j in every]
            cross = [x[j] * v[j] for j in every]

            def face(hl, nl, tl, ul, cl, pl_, kl, hh, nh, th, uh, ch, ph, kh, gl, gh, both):
                slow, fast, inv, wl, wh, sp, slow_low, fast_low = waves(ul, cl, uh, ch, both)
                g_h, g_n, g_t = (b - a for a, b in zip(gl, gh))
                dn = nh - nl
                of_flux = g_h * dn + g_n * (ph - pl_) + g_t * (kh - kl)
                of_jump = g_h * (hh - hl) + g_n * dn + g_t * (th - tl)
                of_slow = -(wl * inv) * (of_flux - fast * of_jump)
                of_fast = -(wh * inv) * (of_flux - slow * of_jump)
                return (wl * g_n, wl * g_t, wh * g_n, wh * g_t, sp * g_h) + speed_terms(
                    slow, fast, of_slow, of_fast, slow_low, fast_low
                )

            kept = []
            for j in every:
                hn, xn, yn, un, cn = (at(state0, k, j, start + 1) for k in (0, 1, 2, 3, 5))
                nl, tl, nh, th, jump, u_low, c_low, u_high, c_high = face(
                    h[j], x[j], y[j], u[j], c[j], x[j] * u[j] + half[j], cross[j],
                    hn, xn, yn, un, cn, xn * un + (0.5 * GRAVITY) * hn * hn, yn * un,
                    (lh[j], lx[j], ly[j]), tuple(at(lam, k, j, start + 1) for k in range(3)), at(faces, 0, j, start),
                )
                shut = lx[j] * at(walls, 1, j, start)
                normal = nl + previous_row(0, j, start, nh) - lx[j] * at(walls, 0, j, start)
                across = tl + previous_row(1, j, start, th)
                of_u = normal * x[j] + across * y[j] + u_low + previous_row(3, j, start, u_high) - shut * jnp.abs(x[j])
                of_c = c_low + previous_row(4, j, start, c_high) - shut * x[j]
                kept.append((normal, previous_row(2, j, start, jump) - jump, of_u * u[j], of_c))
            press = [y[j] * v[j] + half[j] for j in every]
            hn, xn, yn, vn, cn, pn, kn = (next_col(q) for q in (h, x, y, v, c, press, cross))
            lhn, lxn, lyn = (next_col(q) for q in (lh, lx, ly))
            terms = [
                face(
                    h[j], y[j], x[j], v[j], c[j], press[j], cross[j],
                    hn[j], yn[j], xn[j], vn[j], cn[j], pn[j], kn[j],
                    (lh[j], ly[j], lx[j]), (lhn[j], lyn[j], lxn[j]), at(faces, 1, j, start),
                )
                for j in every
            ]
            nh, th, jump, u_high, c_high = (previous_col([t[k] for t in terms]) for k in (2, 3, 4, 7, 8))
            for j in every:
                shut = ly[j] * at(walls, 3, j, start)
                normal = terms[j][0] + nh[j] - ly[j] * at(walls, 2, j, start)
                across = terms[j][1] + th[j]
                of_v = normal * y[j] + across * x[j] + terms[j][5] + u_high[j] - shut * jnp.abs(y[j])
                of_c = kept[j][3] + terms[j][6] + c_high[j] - shut * y[j]
                of_h = kept[j][1] + (jump[j] - terms[j][4]) + GRAVITY * h[j] * (kept[j][0] + normal)
                of_h = of_h + r[j] * (0.5 * (of_c * c[j]) - kept[j][2] - of_v * v[j])
                final[j, pl.ds(start, 8), :] = (1.0 / TIME_RATIO) * lh[j] + of_h
            return carry

        run(first_back)
        return gradient

    return forward, backward


def list_dams(dam_ref, listed, rows, cols, spots):
    total_cols = cols * lax.axis_size("gy")
    row_first = lax.axis_index("gx") * rows
    col_first = lax.axis_index("gy") * cols

    def local(cell):
        if total_cols & (total_cols - 1):
            row = lax.div(cell, jnp.full(jnp.shape(cell), total_cols, jnp.int32))
        else:
            row = lax.shift_right_logical(cell, jnp.full(jnp.shape(cell), total_cols.bit_length() - 1, jnp.int32))
        return row - row_first, cell - row * total_cols - col_first

    cells = dam_ref[...]
    none = cells.shape[1]
    number = lax.broadcasted_iota(jnp.int32, cells.shape, 1)
    row, col = local(cells)
    near = within(row, -REACH, rows + REACH) & within(col, -REACH, cols + REACH)
    number = jnp.where(near, number, none)

    def one(state):
        d, count = state
        row, col = local(jnp.max(jnp.where(number == d, cells, 0)))
        for held, spot in spots(row, col):
            @pl.when(held)
            def _():
                for k, value in enumerate((d,) + spot):
                    listed[k, count] = value

            count = count + jnp.where(held, 1, 0)
        return jnp.min(jnp.where(number > d, number, none)), count

    return lax.while_loop(lambda state: state[0] < none, one, (jnp.min(number), jnp.int32(0)))[1]


def within(value, first, end):
    return (value >= first) & (value < end)


def split(place):
    return lax.shift_right_logical(place, LANES.bit_length() - 1), place & (LANES - 1)


def inner_spots(rows, cols):
    def spots(row, col):
        tile, lane = split(col)
        own = within(row, REACH, rows - REACH) & within(col, REACH, cols - REACH)
        yield within(row, 0, rows) & within(col, 0, cols), (row, tile, lane, jnp.where(own, 1, 0))

    return spots


def ring(tiles):
    return [(j + 1) % tiles for j in range(tiles)], [(j - 1) % tiles for j in range(tiles)]


KEPT = ("state0", "state1", "faces", "walls", "lam0")


def inner_forward_kernel(
    h_ref, x_ref, y_ref, wet_ref, class_ref, rates_ref, dam_ref, release_ref,
    ends_ref, depth_ref, grad_ref, *rest,
):
    held = dict(zip(KEPT + ("listed", "mask", "weight", "last", "back"), rest))
    rows, cols = h_ref.shape
    tiles = cols // LANES
    chunks = rows // 8
    for end, (start, kept) in enumerate(((0, 0), (rows - EDGE, EDGE - REACH))):
        part = slice(start, start + EDGE)
        own = coded_fields(h_ref[part, :], x_ref[part, :], y_ref[part, :], wet_ref[part, :], class_ref[part, :])
        for index in range(FIELDS):
            ends_ref[end, index * REACH : (index + 1) * REACH, :] = own[index][kept : kept + REACH]
    dams = list_dams(dam_ref, held["listed"], rows, cols, inner_spots(rows, cols))

    def put(fill):
        def one(i, carry):
            part = pl.ds(pl.multiple_of(i * 8, 8), 8)
            for j in range(tiles):
                across = pl.ds(j * LANES, LANES)
                fill(
                    j, pl.multiple_of(i * 8, 8), wet_ref[part, across] > 0,
                    h_ref[part, across], x_ref[part, across], y_ref[part, across], class_ref[part, across],
                )
            return carry

        lax.fori_loop(0, chunks, one, 0, unroll=2)

    forward, _ = window(chunks, *ring(tiles), put, held["listed"], dams, rates_ref, release_ref, held)
    grad_ref[...] = forward()
    for j in range(tiles):
        across = slice(j * LANES, (j + 1) * LANES)
        depth_ref[:, across] = jnp.where(wet_ref[:, across] > 0, held["last"][j, :rows, :], h_ref[:, across])


def inner_backward_kernel(*refs):
    names = KEPT + ("dams", "grad_in", "adjoint", "grad", "listed", "lam", "back", "final")
    held = dict(zip(names, refs))
    rows, cols = held["adjoint"].shape
    tiles = cols // LANES
    dams = list_dams(held["dams"], held["listed"], rows, cols, inner_spots(rows, cols))
    shape = jax.ShapeDtypeStruct((held["dams"].shape[1],), jnp.float32)
    _, backward = window(rows // 8, *ring(tiles), None, held["listed"], dams, None, shape, held)
    held["grad"][...] = backward(held["grad_in"][...])
    for j in range(tiles):
        held["adjoint"][:, j * LANES : (j + 1) * LANES] = held["final"][j, :rows, :]


def frame_kernel(
    h_ref, x_ref, y_ref, wet_ref, class_ref, rates_ref, dam_ref, release_ref,
    depth_in, adjoint_in, grad_in, low_ref, high_ref, left_ref, right_ref, side_ref, top_ref, bottom_ref,
    depth_ref, adjoint_ref, grad_ref, *rest,
):
    rows, cols = h_ref.shape
    tiles = cols // LANES
    chunks = 4
    turned = tiles + 1
    after = [(j + 1) % turned for j in range(turned)] + [turned + 1, turned]
    before = [(j - 1) % turned for j in range(turned)] + [turned + 1, turned]

    def chunk_row(place, count):
        return jnp.where(place < EDGE, place + EDGE, place - count + 3 * EDGE)

    def near_end(place, count):
        return within(place, -REACH, EDGE) | within(place, count - EDGE, count + REACH)

    def at_end(place, count):
        return within(place, 0, REACH) | within(place, count - REACH, count)

    def spots(row, col):
        near = within(row, -REACH, rows + REACH) & within(col, -REACH, cols + REACH)
        tile, lane = split(jnp.where(col < 0, col + (tiles + 1) * LANES, col))
        own = at_end(row, rows) & within(col, 0, cols)
        yield near & near_end(row, rows), (chunk_row(row, rows), tile, lane, jnp.where(own, 1, 0))
        tile, lane = split(jnp.where(row < 0, row + 2 * LANES, row))
        own = at_end(col, cols) & within(row, REACH, rows - REACH)
        yield near & near_end(col, cols), (chunk_row(col, cols), tile + turned, lane, jnp.where(own, 1, 0))

    held = dict(zip(KEPT + ("listed", "mask", "weight", "last", "back", "lam", "final"), rest))
    dams = list_dams(dam_ref, held["listed"], rows, cols, spots)
    place = lax.axis_index("gx")
    above = jnp.where(place > 0, top_ref[...], 0.0)
    below = jnp.where(place < lax.axis_size("gx") - 1, bottom_ref[...], 0.0)
    left, right = beside(left_ref, right_ref)

    def put(fill):
        blank = jnp.zeros((EDGE - REACH, LANES), jnp.float32)

        def coded(j, start, h, x, y, code):
            fill(j, start, h > 0.0, h, x, y, code.astype(jnp.int32))

        for j in range(tiles + 1):
            across = slice(j * LANES, (j + 1) * LANES)
            for start, strip in ((0, above), (3 * EDGE, below)):
                pieces = [strip[k * REACH : (k + 1) * REACH, across] for k in range(FIELDS)]
                coded(j, start, *(jnp.concatenate((blank, v) if start == 0 else (v, blank), axis=0) for v in pieces))
            for end, first in ((0, 0), (1, rows - EDGE)):
                start = (1 + end) * EDGE
                if j < tiles:
                    part = slice(first, first + EDGE)
                    fill(
                        j, start, wet_ref[part, across] > 0,
                        h_ref[part, across], x_ref[part, across], y_ref[part, across], class_ref[part, across],
                    )
                else:
                    coded(j, start, *(side_ref[end, k] for k in range(FIELDS)))
        order = (0, 2, 1, 3)
        for chunk, strip in enumerate((left, low_ref[...], high_ref[...], right)):
            coded(turned, chunk * EDGE, *(strip[k * EDGE : (k + 1) * EDGE] for k in order))
        strips = jnp.concatenate((above, below), axis=0)
        outer = strips[:, tiles * LANES :]
        mixed = jnp.zeros((2 * STRIP, LANES), jnp.float32)
        lane = lax.broadcasted_iota(jnp.int32, (2 * STRIP, LANES), 1)
        pieces = (
            (outer, LANES - EDGE),
            (strips[:, :LANES], 0),
            (strips[:, (tiles - 1) * LANES : tiles * LANES], LANES - EDGE),
            (outer, 0),
        )
        for chunk, (piece, first) in enumerate(pieces):
            moved = (chunk * EDGE - first) % LANES
            mixed = jnp.where(lane // EDGE == chunk, pltpu.roll(piece, moved, 1) if moved else piece, mixed)
        corners = jnp.concatenate((mixed, jnp.zeros((LANES - 2 * STRIP, LANES), jnp.float32)), axis=0).T
        corners = corners[: chunks * EDGE]
        lane = lax.broadcasted_iota(jnp.int32, (chunks * EDGE, LANES), 1)
        fields = []
        for k in order:
            from_above = pltpu.roll(corners, LANES - REACH - k * REACH, 1)
            from_below = pltpu.roll(corners, LANES - STRIP - k * REACH, 1)
            fields.append(jnp.where(lane < REACH, from_below, jnp.where(lane >= LANES - REACH, from_above, 0.0)))
        for chunk in range(chunks):
            coded(turned + 1, chunk * EDGE, *(v[chunk * EDGE : (chunk + 1) * EDGE] for v in fields))

    forward, backward = window(chunks, after, before, put, held["listed"], dams, rates_ref, release_ref, held)
    grad_ref[...] = jnp.broadcast_to(backward(forward() + grad_in[...]), grad_ref.shape)
    last, final = held["last"], held["final"]
    blank = jnp.zeros((LANES - 4 * EDGE, LANES), jnp.float32)
    ends = slice(EDGE, 3 * EDGE)
    columns = jnp.concatenate((last[turned, ends, :], final[turned, ends, :], blank), axis=0).T
    lane = lax.broadcasted_iota(jnp.int32, (rows, LANES), 1)
    row = lax.broadcasted_iota(jnp.int32, (EDGE, LANES), 0)
    for number, (ref, inner, strip) in enumerate(((depth_ref, depth_in, last), (adjoint_ref, adjoint_in, final))):
        for j in range(tiles):
            across = slice(j * LANES, (j + 1) * LANES)

            def wet_only(value, part):
                if number:
                    return value
                return jnp.where(wet_ref[part, across] > 0, value, h_ref[part, across])

            whole = slice(0, rows)
            block = inner[:, across]
            if j == 0:
                moved = (LANES - 2 * EDGE * number) % LANES
                edge = pltpu.roll(columns, moved, 1) if moved else columns
                block = jnp.where(lane < REACH, wet_only(edge, whole), block)
            if j == tiles - 1:
                edge = pltpu.roll(columns, LANES - 2 * EDGE - 2 * EDGE * number, 1)
                block = jnp.where(lane >= LANES - REACH, wet_only(edge, whole), block)
            middle = slice(EDGE, rows - EDGE)
            ref[middle, across] = block[middle]
            for part, start, own in (
                (slice(0, EDGE), EDGE, row < REACH),
                (slice(rows - EDGE, rows), 2 * EDGE, row >= EDGE - REACH),
            ):
                ref[part, across] = jnp.where(own, wet_only(strip[j, start : start + EDGE, :], part), block[part])


def on_device(
    water_depth, momentum_x, momentum_y, wet_mask, damage_class, damage_rates, dam_cell, releases
):
    rows, cols = water_depth.shape
    tiles = cols // LANES
    wide = cols + LANES
    rows_count = lax.axis_size("gx")
    cols_count = lax.axis_size("gy")
    vmem = pl.BlockSpec(memory_space=pltpu.VMEM)
    smem = pl.BlockSpec(memory_space=pltpu.SMEM)
    hbm = pl.BlockSpec(memory_space=pltpu.HBM)
    f32 = jnp.float32
    local = (water_depth, momentum_x, momentum_y, wet_mask, damage_class)
    given = (damage_rates, dam_cell.reshape(1, -1), releases)

    def shift(value, axis, count, step):
        return lax.ppermute(value, axis, [(i, (i + step) % count) for i in range(count)])

    def array(*shape):
        return jax.ShapeDtypeStruct(shape, f32)

    def need(names, tiles, chunks):
        leads = dict(state0=(7,), state1=(7,), faces=(2,), walls=(4,), lam=(3,), back=(5,))
        return [array(*leads.get(name, ()), tiles, 8 * chunks + 8, LANES) for name in names]

    def scratch(names, tiles, chunks, spots):
        listed = pltpu.SMEM((5, spots), jnp.int32)
        return [listed] + [pltpu.VMEM(v.shape, v.dtype) for v in need(names, tiles, chunks)]

    low, high = pl.pallas_call(
        edge_kernel,
        out_shape=[array(FIELDS * EDGE, rows)] * 2,
        in_specs=[hbm] * 5,
        out_specs=[vmem] * 2,
        scratch_shapes=[
            pltpu.VMEM((2, 3, rows, LANES), f32),
            pltpu.VMEM((2, 2, rows, LANES), jnp.int32),
            pltpu.SemaphoreType.DMA((2, 5)),
        ],
        compiler_params=pltpu.CompilerParams(vmem_limit_bytes=60 * 1024 * 1024),
        cost_estimate=pl.CostEstimate(flops=10**9, bytes_accessed=4 * 10**7, transcendentals=0),
        name="edges",
    )(*local)
    right = shift(low, "gy", cols_count, -1)
    left = shift(high, "gy", cols_count, 1)
    kept = need(KEPT, tiles, rows // 8)
    dams = dam_cell.shape[0]
    inner_params = pltpu.CompilerParams(vmem_limit_bytes=16 * 1024 * 1024)
    ends, depth, gradient, *kept = pl.pallas_call(
        inner_forward_kernel,
        out_shape=[array(2, STRIP, cols), array(rows, cols), array(1, LANES)] + kept,
        in_specs=[vmem] * 5 + [smem, vmem, smem],
        out_specs=[vmem] * (3 + len(kept)),
        scratch_shapes=scratch(("mask", "weight", "last", "back"), tiles, rows // 8, dams),
        compiler_params=inner_params,
        cost_estimate=pl.CostEstimate(flops=200 * rows * cols, bytes_accessed=6 * 4 * rows * cols, transcendentals=0),
        name="inner_forward",
    )(*local, *given)
    side, to_top, to_bottom = pl.pallas_call(
        corner_kernel,
        out_shape=[array(2, FIELDS, EDGE, LANES), array(STRIP, wide), array(STRIP, wide)],
        in_specs=[vmem] * 3,
        out_specs=[vmem] * 3,
        compiler_params=inner_params,
        name="corners",
    )(ends, left, right)
    adjoint, gradient = pl.pallas_call(
        inner_backward_kernel,
        out_shape=[array(rows, cols), array(1, LANES)],
        in_specs=[vmem] * (len(kept) + 2),
        out_specs=[vmem] * 2,
        scratch_shapes=scratch(("lam", "back", "final"), tiles, rows // 8, dams),
        compiler_params=inner_params,
        cost_estimate=pl.CostEstimate(flops=300 * rows * cols, bytes_accessed=6 * 4 * rows * cols, transcendentals=0),
        name="inner_backward",
    )(*kept, given[1], gradient)
    bottom = shift(to_top, "gx", rows_count, -1)
    top = shift(to_bottom, "gx", rows_count, 1)
    depth, adjoint, parts = pl.pallas_call(
        frame_kernel,
        out_shape=[array(rows, cols), array(rows, cols), array(rows_count * cols_count, LANES)],
        in_specs=[vmem] * 5 + [smem, vmem, smem] + [vmem] * 10,
        out_specs=[vmem] * 3,
        scratch_shapes=(
            [pltpu.VMEM(v.shape, v.dtype) for v in need(KEPT, tiles + 3, 4)]
            + scratch(("mask", "weight", "last", "back", "lam", "final"), tiles + 3, 4, 2 * dams)
        ),
        compiler_params=inner_params,
        name="frame",
    )(*local, *given, depth, adjoint, gradient, low, high, left, right, side, top, bottom)
    gathered = lax.all_to_all(parts, ("gx", "gy"), 0, 0)
    release_grad = jnp.sum(gathered, axis=0).reshape(releases.shape[1], releases.shape[0]).T
    return (depth, adjoint, release_grad)


def solution(mesh):
    in_specs = (P("gx", "gy"),) * 5 + (P(), P(), P())
    out_specs = (P("gx", "gy"), P("gx", "gy"), P())
    return jax.shard_map(
        on_device, mesh=mesh, in_specs=in_specs, out_specs=out_specs, check_vma=False
    )
```

time: 64.3 us -> 58.1 us (0.904); the launches traced: 64.2 us -> 57.3 us
  blocking collectives: 27.1 us -> 21.2 us
  waiting for transfers between devices: 2.83 us -> 1.27 us
  Pallas kernels: 18.5 us -> 19.2 us
    all_to_all x1, blocking collectives: 27.1 us -> 21.2 us  [on_device(): gathered = lax.all_to_all(parts, ('gx', 'gy'), 0, 0)]
    pallas_call x1 -> x2, Pallas kernels: 9.45 us -> 11.2 us  [the longest x1 5.84 us: on_device(): pl.pallas_call(inner_forward_kernel, out_shape=[array(2, STRIP, cols), ar...]
    ppermute x4, waiting for transfers between devices: 2.83 us -> 1.27 us  [shift(): lax.ppermute(value, axis, [(i, (i + step) % count) for i in range(count)])]
    pallas_call x1, Pallas kernels: 6.74 us -> 5.65 us  [on_device(): pl.pallas_call(frame_kernel, out_shape=[array(rows, cols), array(rows, co...]
  transfers between devices with their start and end apart: 4 -> 4, of which waited for: 2 -> 1; matrix products, arithmetic and copies ran while one was open for 0% -> 0% of each run, Pallas kernels for 15% -> 20%
where the time goes in v2:
time: 58.1 us; the launch traced here: 57.3 us
  blocking collectives  21.2 us (36%)
  Pallas kernels  19.2 us (33%)
  starting transfers between devices  13.8 us (24%)
  waiting for transfers between devices  1.27 us (2%)
  between operations  0.81 us (1%)
  local copies, waits for them, and re-layouts  0.78 us (1%)
    all_to_all x1, blocking collectives, on_device(): gathered = lax.all_to_all(parts, ('gx', 'gy'), 0, 0)  21.2 us
    ppermute x4, starting transfers between devices, shift(): lax.ppermute(value, axis, [(i, (i + step) % count) for i in range(count)])  13.8 us
    pallas_call x1, Pallas kernels, on_device(): pl.pallas_call(inner_forward_kernel, out_shape=[array(2, STRIP, cols), ar...  5.84 us
    pallas_call x1, Pallas kernels, on_device(): pl.pallas_call(frame_kernel, out_shape=[array(rows, cols), array(rows, co...  5.65 us
    pallas_call x1, Pallas kernels, on_device(): pl.pallas_call(inner_backward_kernel, out_shape=[array(rows, cols), array...  5.36 us
    pallas_call x1, Pallas kernels, on_device(): pl.pallas_call(edge_kernel, out_shape=[array(FIELDS * EDGE, rows)] * 2, i...  2.14 us
    ppermute x4, waiting for transfers between devices, shift(): lax.ppermute(value, axis, [(i, (i + step) % count) for i in range(count)])  1.27 us
  transfers between devices with their start and end apart: 4, of which 1 were waited for; matrix products, arithmetic and copies ran while one was open for 0% of the time, Pallas kernels for 20%

profile of v2, /device:TPU:1, one launch (start us, length us, event | category | flops | bytes accessed | tf_op | source)
XLA Modules:
  0.0 57.3 jit_solution(12388699476828089816)
XLA Ops:
  0.6 0.0 copy-start.2
  0.6 0.0 copy-start.3
  0.7 0.0 copy-start.4
  0.7 0.0 copy-start
  0.7 0.0 copy-start.1
  0.7 0.0 copy-start.9
  0.7 0.0 copy-start.7
  0.7 2.1 %edges.1 = (f32[32,128]{1,0:T(8,128)}, f32[32,128]{1,0:T(8,128)}) custom-call(f32[128,512]{1,0:T(8,128)} %h_ref.3, f32[128,512]{1,0:T(8,128)} %x_ref.3, f32[128,512]{1,0:T(8,128)} %y_ref.3, s32[128,512]{1,0:T(8,128)} %wet_ref.3, s32[128,512]{1,0:T(8,128)} %class_ref.3), custom_call_target="tpu_custom_call" | custom-call | flops 1000000000 | bytes 40000000 | tf_op jit(solution)/shard_map/edges/pallas_call | solution.py:665
  2.9 8.4 %collective-permute-start = (f32[32,128]{1,0:T(8,128)}, f32[32,128]{1,0:T(8,128)S(1)}, u32[]{:S(2)}, u32[]{:S(2)}) collective-permute-start(f32[32,128]{1,0:T(8,128)} %get-tuple-element.31.high_ref), channel_id=1, source_target_pairs={{0,1},{1,2},{2,3},{3,4},{4,5},{5,6},{6,7},{7,8},{8,9},{9,10},{10,1... | collective-permute-start | bytes 49160 | tf_op jit(solution)/shard_map/ppermute | solution.py:652
  11.2 0.0 collective-permute-start.1
  11.2 0.1 copy.14.release_ref
  11.4 5.8 %inner_forward.1 = (f32[2,16,512]{2,1,0:T(8,128)S(1)}, f32[128,512]{1,0:T(8,128)S(1)}, f32[1,128]{1,0:T(1,128)S(1)}, f32[7,4,136,128]{3,2,1,0:T(8,128)S(1)}, f32...) custom-call(f32[128,512]{1,0:T(8,128)S(1)} %copy-done, ...), custom_call_target="tpu_custom_call" | custom-call | flops 13107200 | bytes 1572864 | tf_op jit(solution)/shard_map/inner_forward/pallas_call | solution.py:684
  17.2 0.0 collective-permute-done.left_ref
  17.3 1.3 %collective-permute-done.1.right_ref = f32[32,128]{1,0:T(8,128)S(1)} collective-permute-done((f32[32,128]{1,0:T(8,128)}, f32[32,128]{1,0:T(8,128)S(1)}, u32[]{:S(2)}, u32[]{:S(2)}) %collective-permute-start.1) | collective-permute-done | bytes 16416 | tf_op jit(solution)/shard_map/ppermute | solution.py:652
  18.5 0.2 corners.1
  18.7 0.8 %collective-permute-start.2 = (f32[16,640]{1,0:T(8,128)S(1)}, f32[16,640]{1,0:T(8,128)S(1)}, u32[]{:S(2)}, u32[]{:S(2)}) collective-permute-start(f32[16,640]{1,0:T(8,128)S(1)} %get-tuple-element.34), channel_id=1, source_target_pairs={{0,16},{16,32},{32,48},{48,64},{64,80},{80,96},{96,112},{112,128},... | collective-permute-start | bytes 122888 | tf_op jit(solution)/shard_map/ppermute | solution.py:652
  19.5 4.6 %collective-permute-start.3 = (f32[16,640]{1,0:T(8,128)S(1)}, f32[16,640]{1,0:T(8,128)S(1)}, u32[]{:S(2)}, u32[]{:S(2)}) collective-permute-start(f32[16,640]{1,0:T(8,128)S(1)} %get-tuple-element.35), channel_id=1, source_target_pairs={{0,240},{16,0},{32,16},{48,32},{64,48},{80,64},{96,80},{112,96},{1... | collective-permute-start | bytes 122888 | tf_op jit(solution)/shard_map/ppermute | solution.py:652
  24.2 5.4 %inner_backward.1 = (f32[128,512]{1,0:T(8,128)S(1)}, f32[1,128]{1,0:T(1,128)S(1)}) custom-call(f32[7,4,136,128]{3,2,1,0:T(8,128)S(1)} %get-tuple-element.22.refs_0_, f32[7,4,136,128]{3,2,1,0:T(8,128)S(1)} %get-tuple-element.23.refs_1_, f32[2,4,136,128]{3,2,1,0:T(8,128)S(1)} %get-tuple-element.24.refs_2_, f32[4,4,136,128]{3,2,1,0:T(8,128)S(1)} %get-tuple-element.25.refs_3_, ...), custom_call_target="tpu_custom_call" | custom-call | flops 19660800 | bytes 1572864 | tf_op jit(solution)/shard_map/inner_backward/pallas_call | solution.py:702
  29.5 0.0 collective-permute-done.2.top_ref
  29.5 0.0 collective-permute-done.3.bottom_ref
  29.6 5.6 %frame.1 = (f32[128,512]{1,0:T(8,128)}, f32[128,512]{1,0:T(8,128)}, f32[256,128]{1,0:T(8,128)S(1)}) custom-call(f32[128,512]{1,0:T(8,128)S(1)} %copy-done, f32[128,512]{1,0:T(8,128)S(1)} %copy-done.1, f32[128,512]{1,0:T(8,128)S(1)} %copy-done.2, s32[128,512]{1,0:T(8,128)S(1)} %copy-done.3, s32[128,512]{1,0:T(8,128)S(1)} %copy-done.4, f32[8]{0:T(128)S(1)} %copy-done.8, ...), custom_call_target="tpu_custom_call" | custom-call | tf_op jit(solution)/shard_map/frame/pallas_call | solution.py:714
  35.2 21.2 %all_to_all.9 = f32[256,1,128]{2,1,0:T(1,128)S(1)} all-to-all(f32[256,1,128]{2,1,0:T(1,128)S(1)} %bitcast.5), channel_id=1, replica_groups=mesh['gx'=16,'gy'=16] {'gx','gy'}, dimensions={0} | all-to-all | bytes 262144 | tf_op jit(solution)/shard_map/all_to_all | solution.py:726
  56.4 0.3 reduce_sum.9
  56.7 0.6 %reshape.15 = f32[2,64]{1,0:T(2,128)} reshape(f32[128]{0:T(128)S(1)} %reduce_sum.9) | data formatting | bytes 1024 | tf_op jit(solution)/shard_map/reshape | solution.py:727
  (13 shorter events, 0.0 us)
Async XLA Ops:
  0.6 10.7 %copy-start.2 = (f32[128,512]{1,0:T(8,128)S(1)}, f32[128,512]{1,0:T(8,128)}, u32[]{:S(2)}) copy-start(f32[128,512]{1,0:T(8,128)} %y_ref.3) | copy-start | bytes 786436
  0.6 10.7 %copy-start.3 = (s32[128,512]{1,0:T(8,128)S(1)}, s32[128,512]{1,0:T(8,128)}, u32[]{:S(2)}) copy-start(s32[128,512]{1,0:T(8,128)} %wet_ref.3) | copy-start | bytes 786436
  0.7 10.7 %copy-start.4 = (s32[128,512]{1,0:T(8,128)S(1)}, s32[128,512]{1,0:T(8,128)}, u32[]{:S(2)}) copy-start(s32[128,512]{1,0:T(8,128)} %class_ref.3) | copy-start | bytes 786436
  0.7 10.7 %copy-start = (f32[128,512]{1,0:T(8,128)S(1)}, f32[128,512]{1,0:T(8,128)}, u32[]{:S(2)}) copy-start(f32[128,512]{1,0:T(8,128)} %h_ref.3) | copy-start | bytes 786436
  0.7 10.7 %copy-start.1 = (f32[128,512]{1,0:T(8,128)S(1)}, f32[128,512]{1,0:T(8,128)}, u32[]{:S(2)}) copy-start(f32[128,512]{1,0:T(8,128)} %x_ref.3) | copy-start | bytes 786436
  0.7 10.6 %copy-start.9 = (f32[64,2]{0,1:T(2,128)S(1)}, f32[64,2]{0,1:T(2,128)}, u32[]{:S(2)}) copy-start(f32[64,2]{0,1:T(2,128)} %param.15) | copy-start | bytes 1540
  0.7 10.7 %copy-start.7 = (s32[64]{0:T(128)S(1)}, s32[64]{0:T(128)}, u32[]{:S(2)}) copy-start(s32[64]{0:T(128)} %param.14) | copy-start | bytes 772
  0.7 10.7 %copy-start.8 = (f32[8]{0:T(128)S(1)}, f32[8]{0:T(128)}, u32[]{:S(2)}) copy-start(f32[8]{0:T(128)} %rates_ref.3) | copy-start | bytes 100
  2.9 14.4 %collective-permute-start = (f32[32,128]{1,0:T(8,128)}, f32[32,128]{1,0:T(8,128)S(1)}, u32[]{:S(2)}, u32[]{:S(2)}) collective-permute-start(f32[32,128]{1,0:T(8,128)} %get-tuple-element.31.high_ref), channel_id=1, source_target_pairs={{0,1},{1,2},{2,3},{3,4},{4,5},{5,6},{6,7},{7,8},{8,9},{9,10},{10,1... | collective-permute-start | bytes 49160 | tf_op jit(solution)/shard_map/ppermute | solution.py:652
  11.2 7.3 %collective-permute-start.1 = (f32[32,128]{1,0:T(8,128)}, f32[32,128]{1,0:T(8,128)S(1)}, u32[]{:S(2)}, u32[]{:S(2)}) collective-permute-start(f32[32,128]{1,0:T(8,128)} %get-tuple-element.30.low_ref), channel_id=1, source_target_pairs={{0,15},{1,0},{2,1},{3,2},{4,3},{5,4},{6,5},{7,6},{8,7},{9,8},{10,9... | collective-permute-start | bytes 49160 | tf_op jit(solution)/shard_map/ppermute | solution.py:652
  18.7 10.8 %collective-permute-start.2 = (f32[16,640]{1,0:T(8,128)S(1)}, f32[16,640]{1,0:T(8,128)S(1)}, u32[]{:S(2)}, u32[]{:S(2)}) collective-permute-start(f32[16,640]{1,0:T(8,128)S(1)} %get-tuple-element.34), channel_id=1, source_target_pairs={{0,16},{16,32},{32,48},{48,64},{64,80},{80,96},{96,112},{112,128},... | collective-permute-start | bytes 122888 | tf_op jit(solution)/shard_map/ppermute | solution.py:652
  19.5 10.0 %collective-permute-start.3 = (f32[16,640]{1,0:T(8,128)S(1)}, f32[16,640]{1,0:T(8,128)S(1)}, u32[]{:S(2)}, u32[]{:S(2)}) collective-permute-start(f32[16,640]{1,0:T(8,128)S(1)} %get-tuple-element.35), channel_id=1, source_target_pairs={{0,240},{16,0},{32,16},{48,32},{64,48},{80,64},{96,80},{112,96},{1... | collective-permute-start | bytes 122888 | tf_op jit(solution)/shard_map/ppermute | solution.py:652
  24.2 5.4 %copy-start.5 = (f32[32,128]{1,0:T(8,128)S(1)}, f32[32,128]{1,0:T(8,128)}, u32[]{:S(2)}) copy-start(f32[32,128]{1,0:T(8,128)} %get-tuple-element.30.low_ref) | copy-start | bytes 49156
  24.2 5.4 %copy-start.6 = (f32[32,128]{1,0:T(8,128)S(1)}, f32[32,128]{1,0:T(8,128)}, u32[]{:S(2)}) copy-start(f32[32,128]{1,0:T(8,128)} %get-tuple-element.31.high_ref) | copy-start | bytes 49156

commit v3 on v2

--- a/solution.py
+++ b/solution.py
@@ -30,7 +30,16 @@
     return jnp.where(wet > 0, h, 0.0), x, y, classes.astype(jnp.float32)
 
 
-def edge_kernel(h_hbm, x_hbm, y_hbm, wet_hbm, class_hbm, low_ref, high_ref, values, codes, sems):
+def is_even(axis):
+    return (lax.axis_index(axis) & 1) == 0
+
+
+def low_and_high(axis, near, far):
+    even = is_even(axis)
+    return jnp.where(even, far, near), jnp.where(even, near, far)
+
+
+def edge_kernel(h_hbm, x_hbm, y_hbm, wet_hbm, class_hbm, near_ref, far_ref, values, codes, sems):
     rows, cols = h_hbm.shape
     copies = []
     for index, source in enumerate((h_hbm, x_hbm, y_hbm, wet_hbm, class_hbm)):
@@ -52,33 +61,37 @@
             shifted = pltpu.roll(field, moved, 1) if moved else field
             mixed = jnp.where((lane >= first) & (lane < first + EDGE), shifted, mixed)
     turned = mixed.T
-    low_ref[...] = turned[: FIELDS * EDGE]
-    high_ref[...] = turned[FIELDS * EDGE : 2 * FIELDS * EDGE]
-
-
-def beside(left_ref, right_ref):
-    place = lax.axis_index("gy")
-    left = jnp.where(place > 0, left_ref[...], 0.0)
-    right = jnp.where(place < lax.axis_size("gy") - 1, right_ref[...], 0.0)
-    return left, right
-
-
-def corner_kernel(ends_ref, left_ref, right_ref, side_ref, low_ref, high_ref):
-    rows = left_ref.shape[1]
+    far_ref[...], near_ref[...] = low_and_high("gy", turned[FIELDS * EDGE : 2 * FIELDS * EDGE], turned[: FIELDS * EDGE])
+
+
+def beside(axis, near_ref, far_ref):
+    place = lax.axis_index(axis)
+    low, high = low_and_high(axis, near_ref[...], far_ref[...])
+    return jnp.where(place > 0, low, 0.0), jnp.where(place < lax.axis_size(axis) - 1, high, 0.0)
+
+
+def corner_kernel(ends_ref, near_in, far_in, side_ref, near_ref, far_ref):
+    rows = near_in.shape[1]
     cols = ends_ref.shape[2]
-    left, right = beside(left_ref, right_ref)
+    even = is_even("gx")
+    left, right = beside("gy", near_in, far_in)
     blank = jnp.zeros((LANES - 2 * FIELDS * EDGE, rows), jnp.float32)
     turned = jnp.concatenate((right, left, blank), axis=0).T
     lane = lax.broadcasted_iota(jnp.int32, (EDGE, LANES), 1)
-    for end, (ref, start, kept) in enumerate(((low_ref, 0, 0), (high_ref, rows - EDGE, EDGE - REACH))):
+    strips = []
+    for end, start, kept in ((0, 0, 0), (1, rows - EDGE, EDGE - REACH)):
         part = turned[start : start + EDGE]
-        ref[:, :cols] = ends_ref[end]
+        pieces = []
         for index in range(FIELDS):
             upper = pltpu.roll(part, LANES - index * EDGE, 1) if index else part
             lower = pltpu.roll(part, LANES - (1 + FIELDS + index) * EDGE, 1)
             tile = jnp.where(lane < EDGE, upper, jnp.where(lane >= LANES - EDGE, lower, 0.0))
             side_ref[end, index] = tile
-            ref[index * REACH : (index + 1) * REACH, cols:] = tile[kept : kept + REACH]
+            pieces.append(tile[kept : kept + REACH])
+        strips.append((ends_ref[end], jnp.concatenate(pieces, axis=0)))
+    for part, low, high in zip((slice(0, cols), slice(cols, cols + LANES)), *strips):
+        near_ref[:, part] = jnp.where(even, high, low)
+        far_ref[:, part] = jnp.where(even, low, high)
 
 
 def cell_terms(height, flow_x, flow_y):
@@ -515,7 +528,7 @@
 
 def frame_kernel(
     h_ref, x_ref, y_ref, wet_ref, class_ref, rates_ref, dam_ref, release_ref,
-    depth_in, adjoint_in, grad_in, low_ref, high_ref, left_ref, right_ref, side_ref, top_ref, bottom_ref,
+    depth_in, adjoint_in, grad_in, near_own, far_own, near_col, far_col, side_ref, near_row, far_row,
     depth_ref, adjoint_ref, grad_ref, *rest,
 ):
     rows, cols = h_ref.shape
@@ -545,10 +558,9 @@
 
     held = dict(zip(KEPT + ("listed", "mask", "weight", "last", "back", "lam", "final"), rest))
     dams = list_dams(dam_ref, held["listed"], rows, cols, spots)
-    place = lax.axis_index("gx")
-    above = jnp.where(place > 0, top_ref[...], 0.0)
-    below = jnp.where(place < lax.axis_size("gx") - 1, bottom_ref[...], 0.0)
-    left, right = beside(left_ref, right_ref)
+    above, below = beside("gx", near_row, far_row)
+    left, right = beside("gy", near_col, far_col)
+    first_cols, last_cols = low_and_high("gy", near_own[...], far_own[...])
 
     def put(fill):
         blank = jnp.zeros((EDGE - REACH, LANES), jnp.float32)
@@ -572,7 +584,7 @@
                 else:
                     coded(j, start, *(side_ref[end, k] for k in range(FIELDS)))
         order = (0, 2, 1, 3)
-        for chunk, strip in enumerate((left, low_ref[...], high_ref[...], right)):
+        for chunk, strip in enumerate((left, first_cols, last_cols, right)):
             coded(turned, chunk * EDGE, *(strip[k * EDGE : (k + 1) * EDGE] for k in order))
         strips = jnp.concatenate((above, below), axis=0)
         outer = strips[:, tiles * LANES :]
@@ -633,6 +645,14 @@
                 ref[part, across] = jnp.where(own, wet_only(strip[j, start : start + EDGE, :], part), block[part])
 
 
+def total_kernel(parts_ref, out_ref):
+    total = jnp.sum(parts_ref[...], axis=0, keepdims=True)
+    steps, dams = out_ref.shape
+    for step in range(steps):
+        moved = pltpu.roll(total, LANES - step * dams, 1) if step else total
+        out_ref[step : step + 1, :] = moved[:, :dams]
+
+
 def on_device(
     water_depth, momentum_x, momentum_y, wet_mask, damage_class, damage_rates, dam_cell, releases
 ):
@@ -648,8 +668,9 @@
     local = (water_depth, momentum_x, momentum_y, wet_mask, damage_class)
     given = (damage_rates, dam_cell.reshape(1, -1), releases)
 
-    def shift(value, axis, count, step):
-        return lax.ppermute(value, axis, [(i, (i + step) % count) for i in range(count)])
+    def swap(near, far, axis, count):
+        near = lax.ppermute(near, axis, [(i, i + 1 - 2 * (i % 2)) for i in range(count)])
+        return near, lax.ppermute(far, axis, [(i, (i - 1 + 2 * (i % 2)) % count) for i in range(count)])
 
     def array(*shape):
         return jax.ShapeDtypeStruct(shape, f32)
@@ -662,7 +683,7 @@
         listed = pltpu.SMEM((5, spots), jnp.int32)
         return [listed] + [pltpu.VMEM(v.shape, v.dtype) for v in need(names, tiles, chunks)]
 
-    low, high = pl.pallas_call(
+    own = pl.pallas_call(
         edge_kernel,
         out_shape=[array(FIELDS * EDGE, rows)] * 2,
         in_specs=[hbm] * 5,
@@ -676,8 +697,7 @@
         cost_estimate=pl.CostEstimate(flops=10**9, bytes_accessed=4 * 10**7, transcendentals=0),
         name="edges",
     )(*local)
-    right = shift(low, "gy", cols_count, -1)
-    left = shift(high, "gy", cols_count, 1)
+    beside_cols = swap(*own, "gy", cols_count)
     kept = need(KEPT, tiles, rows // 8)
     dams = dam_cell.shape[0]
     inner_params = pltpu.CompilerParams(vmem_limit_bytes=16 * 1024 * 1024)
@@ -691,14 +711,14 @@
         cost_estimate=pl.CostEstimate(flops=200 * rows * cols, bytes_accessed=6 * 4 * rows * cols, transcendentals=0),
         name="inner_forward",
     )(*local, *given)
-    side, to_top, to_bottom = pl.pallas_call(
+    side, *to_rows = pl.pallas_call(
         corner_kernel,
         out_shape=[array(2, FIELDS, EDGE, LANES), array(STRIP, wide), array(STRIP, wide)],
         in_specs=[vmem] * 3,
         out_specs=[vmem] * 3,
         compiler_params=inner_params,
         name="corners",
-    )(ends, left, right)
+    )(ends, *beside_cols)
     adjoint, gradient = pl.pallas_call(
         inner_backward_kernel,
         out_shape=[array(rows, cols), array(1, LANES)],
@@ -709,8 +729,7 @@
         cost_estimate=pl.CostEstimate(flops=300 * rows * cols, bytes_accessed=6 * 4 * rows * cols, transcendentals=0),
         name="inner_backward",
     )(*kept, given[1], gradient)
-    bottom = shift(to_top, "gx", rows_count, -1)
-    top = shift(to_bottom, "gx", rows_count, 1)
+    beside_rows = swap(*to_rows, "gx", rows_count)
     depth, adjoint, parts = pl.pallas_call(
         frame_kernel,
         out_shape=[array(rows, cols), array(rows, cols), array(rows_count * cols_count, LANES)],
@@ -722,10 +741,17 @@
         ),
         compiler_params=inner_params,
         name="frame",
-    )(*local, *given, depth, adjoint, gradient, low, high, left, right, side, top, bottom)
+    )(*local, *given, depth, adjoint, gradient, *own, *beside_cols, side, *beside_rows)
     gathered = lax.all_to_all(parts, ("gx", "gy"), 0, 0)
-    release_grad = jnp.sum(gathered, axis=0).reshape(releases.shape[1], releases.shape[0]).T
-    return (depth, adjoint, release_grad)
+    release_grad = pl.pallas_call(
+        total_kernel,
+        out_shape=array(releases.shape[1], releases.shape[0]),
+        in_specs=[vmem],
+        out_specs=vmem,
+        compiler_params=inner_params,
+        name="total",
+    )(gathered)
+    return (depth, adjoint, release_grad.T)
 
 
 def solution(mesh):

time: 58.1 us -> 53.4 us (0.919); the launches traced: 57.3 us -> 53.3 us
  Pallas kernels: 19.2 us -> 17 us
  waiting for transfers between devices: 1.27 us -> 0.01 us
  blocking collectives: 21.2 us -> 21.9 us
  local copies, waits for them, and re-layouts: 0.78 us -> 0.14 us
    ppermute x4, waiting for transfers between devices: 1.27 us -> 0.01 us  [the longest x2 0.01 us: swap(): lax.ppermute(near, axis, [(i, i + 1 - 2 * (i % 2)) for i in range(count)])]
    pallas_call x1, Pallas kernels: 5.65 us -> 4.58 us  [on_device(): pl.pallas_call(frame_kernel, out_shape=[array(rows, cols), array(rows, co...]
    pallas_call x1, Pallas kernels: 5.84 us -> 4.88 us  [on_device(): pl.pallas_call(inner_forward_kernel, out_shape=[array(2, STRIP, cols), ar...]
    pallas_call x1, Pallas kernels: 5.36 us -> 4.49 us  [on_device(): pl.pallas_call(inner_backward_kernel, out_shape=[array(rows, cols), array...]
    all_to_all x1, blocking collectives: 21.2 us -> 21.9 us  [on_device(): gathered = lax.all_to_all(parts, ('gx', 'gy'), 0, 0)]
    pallas_call x0 -> x1, Pallas kernels: none -> 0.67 us  [on_device(): pl.pallas_call(total_kernel, out_shape=array(releases.shape[1], releases....]
    reshape x1 -> x0, local copies, waits for them, and re-layouts: 0.65 us -> none  [on_device(): jnp.sum(gathered, axis=0).reshape(releases.shape[1], releases.shape[0])]
  transfers between devices with their start and end apart: 4 -> 4, of which waited for: 1 -> 0; matrix products, arithmetic and copies ran while one was open for 0% -> 0% of each run, Pallas kernels for 20% -> 18%
where the time goes in v3:
time: 53.4 us; the launch traced here: 53.3 us
  blocking collectives  21.9 us (41%)
  Pallas kernels  17 us (32%)
  starting transfers between devices  13.4 us (25%)
  between operations  0.82 us (2%)
    all_to_all x1, blocking collectives, on_device(): gathered = lax.all_to_all(parts, ('gx', 'gy'), 0, 0)  21.9 us
    ppermute x2, starting transfers between devices, swap(): lax.ppermute(far, axis, [(i, (i - 1 + 2 * (i % 2)) % count) for i in rang...  9.25 us
    pallas_call x1, Pallas kernels, on_device(): pl.pallas_call(inner_forward_kernel, out_shape=[array(2, STRIP, cols), ar...  4.88 us
    pallas_call x1, Pallas kernels, on_device(): pl.pallas_call(frame_kernel, out_shape=[array(rows, cols), array(rows, co...  4.58 us
    pallas_call x1, Pallas kernels, on_device(): pl.pallas_call(inner_backward_kernel, out_shape=[array(rows, cols), array...  4.49 us
    ppermute x2, starting transfers between devices, swap(): lax.ppermute(near, axis, [(i, i + 1 - 2 * (i % 2)) for i in range(count)])  4.15 us
    pallas_call x1, Pallas kernels, on_device(): pl.pallas_call(edge_kernel, out_shape=[array(FIELDS * EDGE, rows)] * 2, i...  2.14 us
  transfers between devices with their start and end apart: 4, of which 0 were waited for; matrix products, arithmetic and copies ran while one was open for 0% of the time, Pallas kernels for 18%

profile of v3, /device:TPU:1, one launch (start us, length us, event | category | flops | bytes accessed | tf_op | source)
XLA Modules:
  0.0 53.3 jit_solution(3181456708442821493)
XLA Ops:
  0.6 0.0 copy-start.2
  0.6 0.0 copy-start.3
  0.7 0.0 copy-start.4
  0.7 0.0 copy-start
  0.7 0.0 copy-start.1
  0.7 0.0 copy-start.9
  0.7 0.0 copy-start.7
  0.7 0.0 copy-start.8
  0.7 2.1 %edges.1 = (f32[32,128]{1,0:T(8,128)}, f32[32,128]{1,0:T(8,128)}) custom-call(f32[128,512]{1,0:T(8,128)} %h_ref.3, f32[128,512]{1,0:T(8,128)} %x_ref.3, f32[128,512]{1,0:T(8,128)} %y_ref.3, s32[128,512]{1,0:T(8,128)} %wet_ref.3, s32[128,512]{1,0:T(8,128)} %class_ref.3), custom_call_target="tpu_custom_call" | custom-call | flops 1000000000 | bytes 40000000 | tf_op jit(solution)/shard_map/edges/pallas_call | solution.py:686
  2.9 3.3 %collective-permute-start = (f32[32,128]{1,0:T(8,128)}, f32[32,128]{1,0:T(8,128)S(1)}, u32[]{:S(2)}, u32[]{:S(2)}) collective-permute-start(f32[32,128]{1,0:T(8,128)} %get-tuple-element.30.near_own), channel_id=1, source_target_pairs={{0,1},{1,0},{2,3},{3,2},{4,5},{5,4},{6,7},{7,6},{8,9},{9,8},{10,11... | collective-permute-start | bytes 49160 | tf_op jit(solution)/shard_map/ppermute | solution.py:672
  6.2 5.2 %collective-permute-start.1 = (f32[32,128]{1,0:T(8,128)}, f32[32,128]{1,0:T(8,128)S(1)}, u32[]{:S(2)}, u32[]{:S(2)}) collective-permute-start(f32[32,128]{1,0:T(8,128)} %get-tuple-element.31.far_own), channel_id=1, source_target_pairs={{0,15},{1,2},{2,1},{3,4},{4,3},{5,6},{6,5},{7,8},{8,7},{9,10},{10,... | collective-permute-start | bytes 49160 | tf_op jit(solution)/shard_map/ppermute | solution.py:673
  11.4 0.1 copy.14.release_ref
  11.5 4.9 %inner_forward.1 = (f32[2,16,512]{2,1,0:T(8,128)S(1)}, f32[128,512]{1,0:T(8,128)S(1)}, f32[1,128]{1,0:T(1,128)S(1)}, f32[7,4,136,128]{3,2,1,0:T(8,128)S(1)}, f32...) custom-call(f32[128,512]{1,0:T(8,128)S(1)} %copy-done, ...), custom_call_target="tpu_custom_call" | custom-call | flops 13107200 | bytes 1572864 | tf_op jit(solution)/shard_map/inner_forward/pallas_call | solution.py:704
  16.4 0.0 collective-permute-done.near_in.near_col
  16.4 0.0 collective-permute-done.1.far_in.far_col
  16.4 0.2 corners.1
  16.6 0.8 %collective-permute-start.2 = (f32[16,640]{1,0:T(8,128)S(1)}, f32[16,640]{1,0:T(8,128)S(1)}, u32[]{:S(2)}, u32[]{:S(2)}) collective-permute-start(f32[16,640]{1,0:T(8,128)S(1)} %get-tuple-element.34), channel_id=1, source_target_pairs={{0,16},{16,0},{32,48},{48,32},{64,80},{80,64},{96,112},{112,96},{1... | collective-permute-start | bytes 122888 | tf_op jit(solution)/shard_map/ppermute | solution.py:672
  17.4 4.1 %collective-permute-start.3 = (f32[16,640]{1,0:T(8,128)S(1)}, f32[16,640]{1,0:T(8,128)S(1)}, u32[]{:S(2)}, u32[]{:S(2)}) collective-permute-start(f32[16,640]{1,0:T(8,128)S(1)} %get-tuple-element.35), channel_id=1, source_target_pairs={{0,240},{16,32},{32,16},{48,64},{64,48},{80,96},{96,80},{112,128},... | collective-permute-start | bytes 122888 | tf_op jit(solution)/shard_map/ppermute | solution.py:673
  21.5 4.5 %inner_backward.1 = (f32[128,512]{1,0:T(8,128)S(1)}, f32[1,128]{1,0:T(1,128)S(1)}) custom-call(f32[7,4,136,128]{3,2,1,0:T(8,128)S(1)} %get-tuple-element.22.refs_0_, f32[7,4,136,128]{3,2,1,0:T(8,128)S(1)} %get-tuple-element.23.refs_1_, f32[2,4,136,128]{3,2,1,0:T(8,128)S(1)} %get-tuple-element.24.refs_2_, f32[4,4,136,128]{3,2,1,0:T(8,128)S(1)} %get-tuple-element.25.refs_3_, ...), custom_call_target="tpu_custom_call" | custom-call | flops 19660800 | bytes 1572864 | tf_op jit(solution)/shard_map/inner_backward/pallas_call | solution.py:722
  26.0 0.0 collective-permute-done.2.near_row
  26.0 0.0 collective-permute-done.3.far_row
  26.1 4.6 %frame.1 = (f32[128,512]{1,0:T(8,128)}, f32[128,512]{1,0:T(8,128)}, f32[256,128]{1,0:T(8,128)S(1)}) custom-call(f32[128,512]{1,0:T(8,128)S(1)} %copy-done, f32[128,512]{1,0:T(8,128)S(1)} %copy-done.1, f32[128,512]{1,0:T(8,128)S(1)} %copy-done.2, s32[128,512]{1,0:T(8,128)S(1)} %copy-done.3, s32[128,512]{1,0:T(8,128)S(1)} %copy-done.4, f32[8]{0:T(128)S(1)} %copy-done.8, ...), custom_call_target="tpu_custom_call" | custom-call | tf_op jit(solution)/shard_map/frame/pallas_call | solution.py:733
  30.7 21.9 %all_to_all.11 = f32[256,1,128]{2,1,0:T(1,128)S(1)} all-to-all(f32[256,1,128]{2,1,0:T(1,128)S(1)} %bitcast.7), channel_id=1, replica_groups=mesh['gx'=16,'gy'=16] {'gx','gy'}, dimensions={0} | all-to-all | bytes 262144 | tf_op jit(solution)/shard_map/all_to_all | solution.py:745
  52.6 0.7 %total.1 = f32[2,64]{1,0:T(2,128)} custom-call(f32[256,128]{1,0:T(8,128)S(1)} %bitcast.6), custom_call_target="tpu_custom_call" | custom-call | tf_op jit(solution)/shard_map/total/pallas_call | solution.py:746
  (12 shorter events, 0.0 us)
Async XLA Ops:
  0.6 10.8 %copy-start.2 = (f32[128,512]{1,0:T(8,128)S(1)}, f32[128,512]{1,0:T(8,128)}, u32[]{:S(2)}) copy-start(f32[128,512]{1,0:T(8,128)} %y_ref.3) | copy-start | bytes 786436
  0.6 10.8 %copy-start.3 = (s32[128,512]{1,0:T(8,128)S(1)}, s32[128,512]{1,0:T(8,128)}, u32[]{:S(2)}) copy-start(s32[128,512]{1,0:T(8,128)} %wet_ref.3) | copy-start | bytes 786436
  0.7 10.8 %copy-start.4 = (s32[128,512]{1,0:T(8,128)S(1)}, s32[128,512]{1,0:T(8,128)}, u32[]{:S(2)}) copy-start(s32[128,512]{1,0:T(8,128)} %class_ref.3) | copy-start | bytes 786436
  0.7 10.8 %copy-start = (f32[128,512]{1,0:T(8,128)S(1)}, f32[128,512]{1,0:T(8,128)}, u32[]{:S(2)}) copy-start(f32[128,512]{1,0:T(8,128)} %h_ref.3) | copy-start | bytes 786436
  0.7 10.8 %copy-start.1 = (f32[128,512]{1,0:T(8,128)S(1)}, f32[128,512]{1,0:T(8,128)}, u32[]{:S(2)}) copy-start(f32[128,512]{1,0:T(8,128)} %x_ref.3) | copy-start | bytes 786436
  0.7 10.7 %copy-start.9 = (f32[64,2]{0,1:T(2,128)S(1)}, f32[64,2]{0,1:T(2,128)}, u32[]{:S(2)}) copy-start(f32[64,2]{0,1:T(2,128)} %param.15) | copy-start | bytes 1540
  0.7 10.8 %copy-start.7 = (s32[64]{0:T(128)S(1)}, s32[64]{0:T(128)}, u32[]{:S(2)}) copy-start(s32[64]{0:T(128)} %param.14) | copy-start | bytes 772
  0.7 10.8 %copy-start.8 = (f32[8]{0:T(128)S(1)}, f32[8]{0:T(128)}, u32[]{:S(2)}) copy-start(f32[8]{0:T(128)} %rates_ref.3) | copy-start | bytes 100
  2.9 13.5 %collective-permute-start = (f32[32,128]{1,0:T(8,128)}, f32[32,128]{1,0:T(8,128)S(1)}, u32[]{:S(2)}, u32[]{:S(2)}) collective-permute-start(f32[32,128]{1,0:T(8,128)} %get-tuple-element.30.near_own), channel_id=1, source_target_pairs={{0,1},{1,0},{2,3},{3,2},{4,5},{5,4},{6,7},{7,6},{8,9},{9,8},{10,11... | collective-permute-start | bytes 49160 | tf_op jit(solution)/shard_map/ppermute | solution.py:672
  6.2 10.2 %collective-permute-start.1 = (f32[32,128]{1,0:T(8,128)}, f32[32,128]{1,0:T(8,128)S(1)}, u32[]{:S(2)}, u32[]{:S(2)}) collective-permute-start(f32[32,128]{1,0:T(8,128)} %get-tuple-element.31.far_own), channel_id=1, source_target_pairs={{0,15},{1,2},{2,1},{3,4},{4,3},{5,6},{6,5},{7,8},{8,7},{9,10},{10,... | collective-permute-start | bytes 49160 | tf_op jit(solution)/shard_map/ppermute | solution.py:673
  16.6 9.4 %collective-permute-start.2 = (f32[16,640]{1,0:T(8,128)S(1)}, f32[16,640]{1,0:T(8,128)S(1)}, u32[]{:S(2)}, u32[]{:S(2)}) collective-permute-start(f32[16,640]{1,0:T(8,128)S(1)} %get-tuple-element.34), channel_id=1, source_target_pairs={{0,16},{16,0},{32,48},{48,32},{64,80},{80,64},{96,112},{112,96},{1... | collective-permute-start | bytes 122888 | tf_op jit(solution)/shard_map/ppermute | solution.py:672
  17.4 8.6 %collective-permute-start.3 = (f32[16,640]{1,0:T(8,128)S(1)}, f32[16,640]{1,0:T(8,128)S(1)}, u32[]{:S(2)}, u32[]{:S(2)}) collective-permute-start(f32[16,640]{1,0:T(8,128)S(1)} %get-tuple-element.35), channel_id=1, source_target_pairs={{0,240},{16,32},{32,16},{48,64},{64,48},{80,96},{96,80},{112,128},... | collective-permute-start | bytes 122888 | tf_op jit(solution)/shard_map/ppermute | solution.py:673
  21.5 4.5 %copy-start.5 = (f32[32,128]{1,0:T(8,128)S(1)}, f32[32,128]{1,0:T(8,128)}, u32[]{:S(2)}) copy-start(f32[32,128]{1,0:T(8,128)} %get-tuple-element.30.near_own) | copy-start | bytes 49156
  21.5 4.5 %copy-start.6 = (f32[32,128]{1,0:T(8,128)S(1)}, f32[32,128]{1,0:T(8,128)}, u32[]{:S(2)}) copy-start(f32[32,128]{1,0:T(8,128)} %get-tuple-element.31.far_own) | copy-start | bytes 49156

commit v4 on v3

--- a/solution.py
+++ b/solution.py
@@ -170,8 +170,8 @@
         for lead in itertools.product(*index):
             ref[lead + (pl.ds(start, 8), slice(None))] = jnp.full((8, LANES), value, jnp.float32)
 
-    def run(step):
-        lax.fori_loop(0, chunks, step, 0, unroll=UNROLL)
+    def run(step, count=chunks):
+        lax.fori_loop(0, count, step, 0, unroll=UNROLL)
 
     def add_inflow(step, ref, refresh):
         def one(index, carry):
@@ -181,7 +181,7 @@
             else:
                 old = [ref[j, pl.ds(row, 1), :]]
             here = lax.broadcasted_iota(jnp.int32, (1, LANES), 1) == col
-            height = old[0] + jnp.where(here, INFLOW_GAIN * release_ref[d, step], 0.0)
+            height = old[0] + jnp.where(here, INFLOW_GAIN * release_ref[step, d], 0.0)
             if refresh:
                 terms = (height, old[1], old[2]) + cell_terms(height, old[1], old[2])
                 for k, value in enumerate(terms):
@@ -199,7 +199,7 @@
             d, row, j, col, inside = (listed[k, index] for k in range(5))
             values = ref[j, pl.ds(row, 1), :]
             value = jnp.sum(jnp.where(lane_row == col, values, 0.0), axis=1, keepdims=True)
-            spot = (lane_row == d + step * release_ref.shape[0]) & (inside > 0)
+            spot = (lane_row == d + step * release_ref.shape[1]) & (inside > 0)
             return total + jnp.where(spot, (INFLOW_GAIN / TIME_RATIO) * value, 0.0)
 
         return lax.fori_loop(0, dams, one, gradient)
@@ -414,7 +414,7 @@
                 final[j, pl.ds(start, 8), :] = (1.0 / TIME_RATIO) * lh[j] + of_h
             return carry
 
-        run(first_back)
+        run(first_back, held.get("needed", chunks))
         return gradient
 
     return forward, backward
@@ -519,7 +519,7 @@
     rows, cols = held["adjoint"].shape
     tiles = cols // LANES
     dams = list_dams(held["dams"], held["listed"], rows, cols, inner_spots(rows, cols))
-    shape = jax.ShapeDtypeStruct((held["dams"].shape[1],), jnp.float32)
+    shape = jax.ShapeDtypeStruct((1, held["dams"].shape[1]), jnp.float32)
     _, backward = window(rows // 8, *ring(tiles), None, held["listed"], dams, None, shape, held)
     held["grad"][...] = backward(held["grad_in"][...])
     for j in range(tiles):
@@ -556,7 +556,8 @@
         own = at_end(col, cols) & within(row, REACH, rows - REACH)
         yield near & near_end(col, cols), (chunk_row(col, cols), tile + turned, lane, jnp.where(own, 1, 0))
 
-    held = dict(zip(KEPT + ("listed", "mask", "weight", "last", "back", "lam", "final"), rest))
+    names = KEPT + ("listed", "mask", "weight", "last", "back", "lam", "final")
+    held = dict(zip(names + ("row_patch", "column_patch", "sems"), rest))
     dams = list_dams(dam_ref, held["listed"], rows, cols, spots)
     above, below = beside("gx", near_row, far_row)
     left, right = beside("gy", near_col, far_col)
@@ -610,39 +611,62 @@
         for chunk in range(chunks):
             coded(turned + 1, chunk * EDGE, *(v[chunk * EDGE : (chunk + 1) * EDGE] for v in fields))
 
+    held["needed"] = chunks - 1
     forward, backward = window(chunks, after, before, put, held["listed"], dams, rates_ref, release_ref, held)
-    grad_ref[...] = jnp.broadcast_to(backward(forward() + grad_in[...]), grad_ref.shape)
-    last, final = held["last"], held["final"]
-    blank = jnp.zeros((LANES - 4 * EDGE, LANES), jnp.float32)
-    ends = slice(EDGE, 3 * EDGE)
-    columns = jnp.concatenate((last[turned, ends, :], final[turned, ends, :], blank), axis=0).T
+    row_patch, column_patch, sems = held["row_patch"], held["column_patch"], held["sems"]
     lane = lax.broadcasted_iota(jnp.int32, (rows, LANES), 1)
     row = lax.broadcasted_iota(jnp.int32, (EDGE, LANES), 0)
-    for number, (ref, inner, strip) in enumerate(((depth_ref, depth_in, last), (adjoint_ref, adjoint_in, final))):
+    middle = slice(EDGE, rows - EDGE)
+    blocks = [
+        pltpu.make_async_copy(depth_in, depth_ref, sems.at[0, 0]),
+        pltpu.make_async_copy(adjoint_in, adjoint_ref, sems.at[1, 0]),
+    ]
+    for block in blocks:
+        block.start()
+
+    def send(number, ref, inner, frame, wet_only):
+        blank = jnp.zeros((LANES - 2 * EDGE, LANES), jnp.float32)
+        columns = jnp.concatenate((frame[turned, EDGE : 3 * EDGE, :], blank), axis=0).T
+        columns = {0: columns, tiles - 1: pltpu.roll(columns, LANES - 2 * EDGE, 1)}
+
+        def with_columns(j, part, across):
+            own = (lane < REACH) if j == 0 else (lane >= LANES - REACH)
+            return jnp.where(own[part], wet_only(columns[j][part], part, across), inner[part, across])
+
         for j in range(tiles):
             across = slice(j * LANES, (j + 1) * LANES)
-
-            def wet_only(value, part):
-                if number:
-                    return value
-                return jnp.where(wet_ref[part, across] > 0, value, h_ref[part, across])
-
-            whole = slice(0, rows)
-            block = inner[:, across]
-            if j == 0:
-                moved = (LANES - 2 * EDGE * number) % LANES
-                edge = pltpu.roll(columns, moved, 1) if moved else columns
-                block = jnp.where(lane < REACH, wet_only(edge, whole), block)
-            if j == tiles - 1:
-                edge = pltpu.roll(columns, LANES - 2 * EDGE - 2 * EDGE * number, 1)
-                block = jnp.where(lane >= LANES - REACH, wet_only(edge, whole), block)
-            middle = slice(EDGE, rows - EDGE)
-            ref[middle, across] = block[middle]
-            for part, start, own in (
-                (slice(0, EDGE), EDGE, row < REACH),
-                (slice(rows - EDGE, rows), 2 * EDGE, row >= EDGE - REACH),
-            ):
-                ref[part, across] = jnp.where(own, wet_only(strip[j, start : start + EDGE, :], part), block[part])
+            for end, own in ((0, row < REACH), (1, row >= EDGE - REACH)):
+                part = slice(end * (rows - EDGE), end * (rows - EDGE) + EDGE)
+                value = frame[j, (1 + end) * EDGE : (2 + end) * EDGE, :]
+                base = with_columns(j, part, across) if j in columns else inner[part, across]
+                row_patch[number, end, :, across] = jnp.where(own, wet_only(value, part, across), base)
+            if j in columns:
+                column_patch[number, 0 if j == 0 else 1] = with_columns(j, middle, across)
+        blocks[number].wait()
+        copies = []
+        for end in range(2):
+            part = pl.ds(end * (rows - EDGE), EDGE)
+            across = pl.ds(end * (cols - LANES), LANES)
+            copies += [
+                pltpu.make_async_copy(row_patch.at[number, end], ref.at[part, :], sems.at[number, 1 + end]),
+                pltpu.make_async_copy(
+                    column_patch.at[number, end], ref.at[pl.ds(EDGE, rows - 2 * EDGE), across], sems.at[number, 3 + end]
+                ),
+            ]
+        for copy in copies:
+            copy.start()
+        return copies
+
+    gradient = forward() + grad_in[...]
+    copies = send(
+        0, depth_ref, depth_in, held["last"],
+        lambda value, part, across: jnp.where(wet_ref[part, across] > 0, value, h_ref[part, across]),
+    )
+    gradient = backward(gradient)
+    copies += send(1, adjoint_ref, adjoint_in, held["final"], lambda value, part, across: value)
+    grad_ref[...] = jnp.broadcast_to(gradient, grad_ref.shape)
+    for copy in copies:
+        copy.wait()
 
 
 def total_kernel(parts_ref, out_ref):
@@ -666,7 +690,7 @@
     hbm = pl.BlockSpec(memory_space=pltpu.HBM)
     f32 = jnp.float32
     local = (water_depth, momentum_x, momentum_y, wet_mask, damage_class)
-    given = (damage_rates, dam_cell.reshape(1, -1), releases)
+    given = (damage_rates, dam_cell.reshape(1, -1), releases.T)
 
     def swap(near, far, axis, count):
         near = lax.ppermute(near, axis, [(i, i + 1 - 2 * (i % 2)) for i in range(count)])
@@ -734,10 +758,15 @@
         frame_kernel,
         out_shape=[array(rows, cols), array(rows, cols), array(rows_count * cols_count, LANES)],
         in_specs=[vmem] * 5 + [smem, vmem, smem] + [vmem] * 10,
-        out_specs=[vmem] * 3,
+        out_specs=[hbm, hbm, vmem],
         scratch_shapes=(
             [pltpu.VMEM(v.shape, v.dtype) for v in need(KEPT, tiles + 3, 4)]
             + scratch(("mask", "weight", "last", "back", "lam", "final"), tiles + 3, 4, 2 * dams)
+            + [
+                pltpu.VMEM((2, 2, EDGE, cols), f32),
+                pltpu.VMEM((2, 2, rows - 2 * EDGE, LANES), f32),
+                pltpu.SemaphoreType.DMA((2, 5)),
+            ]
         ),
         compiler_params=inner_params,
         name="frame",

time: 53.4 us -> 53.1 us (level)
  blocking collectives: 21.9 us -> 22.6 us
    all_to_all x1, blocking collectives: 21.9 us -> 22.6 us  [on_device(): gathered = lax.all_to_all(parts, ('gx', 'gy'), 0, 0)]
  transfers between devices with their start and end apart: 4 -> 4, of which waited for: 0 -> 0; matrix products, arithmetic and copies ran while one was open for 0% -> 0% of each run, Pallas kernels for 18% -> 17%
where the time goes in v4:
time: 53.1 us; the launch traced here: 53 us
  blocking collectives  22.6 us (43%)
  Pallas kernels  16.5 us (31%)
  starting transfers between devices  13.1 us (25%)
  between operations  0.82 us (2%)
    all_to_all x1, blocking collectives, on_device(): gathered = lax.all_to_all(parts, ('gx', 'gy'), 0, 0)  22.6 us
    ppermute x2, starting transfers between devices, swap(): lax.ppermute(far, axis, [(i, (i - 1 + 2 * (i % 2)) % count) for i in rang...  9.25 us
    pallas_call x1, Pallas kernels, on_device(): pl.pallas_call(inner_forward_kernel, out_shape=[array(2, STRIP, cols), ar...  4.58 us
    pallas_call x1, Pallas kernels, on_device(): pl.pallas_call(inner_backward_kernel, out_shape=[array(rows, cols), array...  4.47 us
    pallas_call x1, Pallas kernels, on_device(): pl.pallas_call(frame_kernel, out_shape=[array(rows, cols), array(rows, co...  4.41 us
    ppermute x2, starting transfers between devices, swap(): lax.ppermute(near, axis, [(i, i + 1 - 2 * (i % 2)) for i in range(count)])  3.84 us
    pallas_call x1, Pallas kernels, on_device(): pl.pallas_call(edge_kernel, out_shape=[array(FIELDS * EDGE, rows)] * 2, i...  2.14 us
  transfers between devices with their start and end apart: 4, of which 0 were waited for; matrix products, arithmetic and copies ran while one was open for 0% of the time, Pallas kernels for 17%

profile of v4, /device:TPU:1, one launch (start us, length us, event | category | flops | bytes accessed | tf_op | source)
XLA Modules:
  0.0 53.0 jit_solution(9606753528815612658)
XLA Ops:
  0.6 0.0 copy-start.2
  0.6 0.0 copy-start.3
  0.7 0.0 copy-start.4
  0.7 0.0 copy-start
  0.7 0.0 copy-start.1
  0.7 0.0 copy-start.7
  0.7 0.0 copy-start.8
  0.7 0.0 copy-start.9
  0.7 2.1 %edges.1 = (f32[32,128]{1,0:T(8,128)}, f32[32,128]{1,0:T(8,128)}) custom-call(f32[128,512]{1,0:T(8,128)} %h_ref.3, f32[128,512]{1,0:T(8,128)} %x_ref.3, f32[128,512]{1,0:T(8,128)} %y_ref.3, s32[128,512]{1,0:T(8,128)} %wet_ref.3, s32[128,512]{1,0:T(8,128)} %class_ref.3), custom_call_target="tpu_custom_call" | custom-call | flops 1000000000 | bytes 40000000 | tf_op jit(solution)/shard_map/edges/pallas_call | solution.py:710
  2.9 3.3 %collective-permute-start = (f32[32,128]{1,0:T(8,128)}, f32[32,128]{1,0:T(8,128)S(1)}, u32[]{:S(2)}, u32[]{:S(2)}) collective-permute-start(f32[32,128]{1,0:T(8,128)} %get-tuple-element.30.near_own), channel_id=1, source_target_pairs={{0,1},{1,0},{2,3},{3,2},{4,5},{5,4},{6,7},{7,6},{8,9},{9,8},{10,11... | collective-permute-start | bytes 49160 | tf_op jit(solution)/shard_map/ppermute | solution.py:696
  6.2 5.2 %collective-permute-start.1 = (f32[32,128]{1,0:T(8,128)}, f32[32,128]{1,0:T(8,128)S(1)}, u32[]{:S(2)}, u32[]{:S(2)}) collective-permute-start(f32[32,128]{1,0:T(8,128)} %get-tuple-element.31.far_own), channel_id=1, source_target_pairs={{0,15},{1,2},{2,1},{3,4},{4,3},{5,6},{6,5},{7,8},{8,7},{9,10},{10,... | collective-permute-start | bytes 49160 | tf_op jit(solution)/shard_map/ppermute | solution.py:697
  11.4 0.0 copy-done
  11.4 4.6 %inner_forward.1 = (f32[2,16,512]{2,1,0:T(8,128)S(1)}, f32[128,512]{1,0:T(8,128)S(1)}, f32[1,128]{1,0:T(1,128)S(1)}, f32[7,4,136,128]{3,2,1,0:T(8,128)S(1)}, f32...) custom-call(f32[128,512]{1,0:T(8,128)S(1)} %copy-done, ...), custom_call_target="tpu_custom_call" | custom-call | flops 13107200 | bytes 1572864 | tf_op jit(solution)/shard_map/inner_forward/pallas_call | solution.py:728
  16.0 0.0 collective-permute-done.near_in.near_col
  16.0 0.0 collective-permute-done.1.far_in.far_col
  16.0 0.2 corners.1
  16.2 0.5 collective-permute-start.2
  16.7 4.1 %collective-permute-start.3 = (f32[16,640]{1,0:T(8,128)S(1)}, f32[16,640]{1,0:T(8,128)S(1)}, u32[]{:S(2)}, u32[]{:S(2)}) collective-permute-start(f32[16,640]{1,0:T(8,128)S(1)} %get-tuple-element.35), channel_id=1, source_target_pairs={{0,240},{16,32},{32,16},{48,64},{64,48},{80,96},{96,80},{112,128},... | collective-permute-start | bytes 122888 | tf_op jit(solution)/shard_map/ppermute | solution.py:697
  20.8 4.5 %inner_backward.1 = (f32[128,512]{1,0:T(8,128)S(1)}, f32[1,128]{1,0:T(1,128)S(1)}) custom-call(f32[7,4,136,128]{3,2,1,0:T(8,128)S(1)} %get-tuple-element.22.refs_0_, f32[7,4,136,128]{3,2,1,0:T(8,128)S(1)} %get-tuple-element.23.refs_1_, f32[2,4,136,128]{3,2,1,0:T(8,128)S(1)} %get-tuple-element.24.refs_2_, f32[4,4,136,128]{3,2,1,0:T(8,128)S(1)} %get-tuple-element.25.refs_3_, ...), custom_call_target="tpu_custom_call" | custom-call | flops 19660800 | bytes 1572864 | tf_op jit(solution)/shard_map/inner_backward/pallas_call | solution.py:746
  25.3 0.0 collective-permute-done.2.near_row
  25.3 0.0 collective-permute-done.3.far_row
  25.3 4.4 %frame.1 = (f32[128,512]{1,0:T(8,128)}, f32[128,512]{1,0:T(8,128)}, f32[256,128]{1,0:T(8,128)S(1)}) custom-call(f32[128,512]{1,0:T(8,128)S(1)} %copy-done, f32[128,512]{1,0:T(8,128)S(1)} %copy-done.1, f32[128,512]{1,0:T(8,128)S(1)} %copy-done.2, s32[128,512]{1,0:T(8,128)S(1)} %copy-done.3, s32[128,512]{1,0:T(8,128)S(1)} %copy-done.4, f32[8]{0:T(128)S(1)} %copy-done.9, ...), custom_call_target="tpu_custom_call" | custom-call | tf_op jit(solution)/shard_map/frame/pallas_call | solution.py:757
  29.7 22.6 %all_to_all.11 = f32[256,1,128]{2,1,0:T(1,128)S(1)} all-to-all(f32[256,1,128]{2,1,0:T(1,128)S(1)} %bitcast.8), channel_id=1, replica_groups=mesh['gx'=16,'gy'=16] {'gx','gy'}, dimensions={0} | all-to-all | bytes 262144 | tf_op jit(solution)/shard_map/all_to_all | solution.py:774
  52.3 0.7 %total.1 = f32[2,64]{1,0:T(2,128)} custom-call(f32[256,128]{1,0:T(8,128)S(1)} %bitcast.7), custom_call_target="tpu_custom_call" | custom-call | tf_op jit(solution)/shard_map/total/pallas_call | solution.py:775
  (11 shorter events, 0.0 us)
Async XLA Ops:
  0.6 10.7 %copy-start.2 = (f32[128,512]{1,0:T(8,128)S(1)}, f32[128,512]{1,0:T(8,128)}, u32[]{:S(2)}) copy-start(f32[128,512]{1,0:T(8,128)} %y_ref.3) | copy-start | bytes 786436
  0.6 10.7 %copy-start.3 = (s32[128,512]{1,0:T(8,128)S(1)}, s32[128,512]{1,0:T(8,128)}, u32[]{:S(2)}) copy-start(s32[128,512]{1,0:T(8,128)} %wet_ref.3) | copy-start | bytes 786436
  0.7 10.7 %copy-start.4 = (s32[128,512]{1,0:T(8,128)S(1)}, s32[128,512]{1,0:T(8,128)}, u32[]{:S(2)}) copy-start(s32[128,512]{1,0:T(8,128)} %class_ref.3) | copy-start | bytes 786436
  0.7 10.7 %copy-start = (f32[128,512]{1,0:T(8,128)S(1)}, f32[128,512]{1,0:T(8,128)}, u32[]{:S(2)}) copy-start(f32[128,512]{1,0:T(8,128)} %h_ref.3) | copy-start | bytes 786436
  0.7 10.7 %copy-start.1 = (f32[128,512]{1,0:T(8,128)S(1)}, f32[128,512]{1,0:T(8,128)}, u32[]{:S(2)}) copy-start(f32[128,512]{1,0:T(8,128)} %x_ref.3) | copy-start | bytes 786436
  0.7 10.7 %copy-start.7 = (s32[64]{0:T(128)S(1)}, s32[64]{0:T(128)}, u32[]{:S(2)}) copy-start(s32[64]{0:T(128)} %param.14) | copy-start | bytes 772
  0.7 10.7 %copy-start.8 = (f32[64,2]{0,1:T(2,128)S(1)}, f32[64,2]{0,1:T(2,128)}, u32[]{:S(2)}) copy-start(f32[64,2]{0,1:T(2,128)} %param.15) | copy-start | bytes 1540
  0.7 10.7 %copy-start.9 = (f32[8]{0:T(128)S(1)}, f32[8]{0:T(128)}, u32[]{:S(2)}) copy-start(f32[8]{0:T(128)} %rates_ref.3) | copy-start | bytes 100
  2.9 13.1 %collective-permute-start = (f32[32,128]{1,0:T(8,128)}, f32[32,128]{1,0:T(8,128)S(1)}, u32[]{:S(2)}, u32[]{:S(2)}) collective-permute-start(f32[32,128]{1,0:T(8,128)} %get-tuple-element.30.near_own), channel_id=1, source_target_pairs={{0,1},{1,0},{2,3},{3,2},{4,5},{5,4},{6,7},{7,6},{8,9},{9,8},{10,11... | collective-permute-start | bytes 49160 | tf_op jit(solution)/shard_map/ppermute | solution.py:696
  6.2 9.8 %collective-permute-start.1 = (f32[32,128]{1,0:T(8,128)}, f32[32,128]{1,0:T(8,128)S(1)}, u32[]{:S(2)}, u32[]{:S(2)}) collective-permute-start(f32[32,128]{1,0:T(8,128)} %get-tuple-element.31.far_own), channel_id=1, source_target_pairs={{0,15},{1,2},{2,1},{3,4},{4,3},{5,6},{6,5},{7,8},{8,7},{9,10},{10,... | collective-permute-start | bytes 49160 | tf_op jit(solution)/shard_map/ppermute | solution.py:697
  16.2 9.1 %collective-permute-start.2 = (f32[16,640]{1,0:T(8,128)S(1)}, f32[16,640]{1,0:T(8,128)S(1)}, u32[]{:S(2)}, u32[]{:S(2)}) collective-permute-start(f32[16,640]{1,0:T(8,128)S(1)} %get-tuple-element.34), channel_id=1, source_target_pairs={{0,16},{16,0},{32,48},{48,32},{64,80},{80,64},{96,112},{112,96},{1... | collective-permute-start | bytes 122888 | tf_op jit(solution)/shard_map/ppermute | solution.py:696
  16.7 8.6 %collective-permute-start.3 = (f32[16,640]{1,0:T(8,128)S(1)}, f32[16,640]{1,0:T(8,128)S(1)}, u32[]{:S(2)}, u32[]{:S(2)}) collective-permute-start(f32[16,640]{1,0:T(8,128)S(1)} %get-tuple-element.35), channel_id=1, source_target_pairs={{0,240},{16,32},{32,16},{48,64},{64,48},{80,96},{96,80},{112,128},... | collective-permute-start | bytes 122888 | tf_op jit(solution)/shard_map/ppermute | solution.py:697
  20.8 4.5 %copy-start.5 = (f32[32,128]{1,0:T(8,128)S(1)}, f32[32,128]{1,0:T(8,128)}, u32[]{:S(2)}) copy-start(f32[32,128]{1,0:T(8,128)} %get-tuple-element.30.near_own) | copy-start | bytes 49156
  20.8 4.5 %copy-start.6 = (f32[32,128]{1,0:T(8,128)S(1)}, f32[32,128]{1,0:T(8,128)}, u32[]{:S(2)}) copy-start(f32[32,128]{1,0:T(8,128)} %get-tuple-element.31.far_own) | copy-start | bytes 49156

commit v5 on v4

--- a/solution.py
+++ b/solution.py
@@ -135,6 +135,7 @@
     )
     tiles = len(after)
     every = range(tiles)
+    wanted = held.get("wanted", every)
     lane = lax.broadcasted_iota(jnp.int32, (8, LANES), 1)
 
     def at(ref, k, j, start):
@@ -377,8 +378,8 @@
                     slow, fast, of_slow, of_fast, slow_low, fast_low
                 )
 
-            kept = []
-            for j in every:
+            kept = {}
+            for j in wanted:
                 hn, xn, yn, un, cn = (at(state0, k, j, start + 1) for k in (0, 1, 2, 3, 5))
                 nl, tl, nh, th, jump, u_low, c_low, u_high, c_high = face(
                     h[j], x[j], y[j], u[j], c[j], x[j] * u[j] + half[j], cross[j],
@@ -390,7 +391,7 @@
                 across = tl + previous_row(1, j, start, th)
                 of_u = normal * x[j] + across * y[j] + u_low + previous_row(3, j, start, u_high) - shut * jnp.abs(x[j])
                 of_c = c_low + previous_row(4, j, start, c_high) - shut * x[j]
-                kept.append((normal, previous_row(2, j, start, jump) - jump, of_u * u[j], of_c))
+                kept[j] = (normal, previous_row(2, j, start, jump) - jump, of_u * u[j], of_c)
             press = [y[j] * v[j] + half[j] for j in every]
             hn, xn, yn, vn, cn, pn, kn = (next_col(q) for q in (h, x, y, v, c, press, cross))
             lhn, lxn, lyn = (next_col(q) for q in (lh, lx, ly))
@@ -403,7 +404,7 @@
                 for j in every
             ]
             nh, th, jump, u_high, c_high = (previous_col([t[k] for t in terms]) for k in (2, 3, 4, 7, 8))
-            for j in every:
+            for j in wanted:
                 shut = ly[j] * at(walls, 3, j, start)
                 normal = terms[j][0] + nh[j] - ly[j] * at(walls, 2, j, start)
                 across = terms[j][1] + th[j]
@@ -612,6 +613,7 @@
             coded(turned + 1, chunk * EDGE, *(v[chunk * EDGE : (chunk + 1) * EDGE] for v in fields))
 
     held["needed"] = chunks - 1
+    held["wanted"] = [*range(tiles), turned]
     forward, backward = window(chunks, after, before, put, held["listed"], dams, rates_ref, release_ref, held)
     row_patch, column_patch, sems = held["row_patch"], held["column_patch"], held["sems"]
     lane = lax.broadcasted_iota(jnp.int32, (rows, LANES), 1)

time: 53.1 us -> 52.7 us (level)
  no operation moved by 1% of the time
where the time goes in v5:
time: 52.7 us; the launch traced here: 52.6 us
  blocking collectives  22.2 us (42%)
  Pallas kernels  16.5 us (31%)
  starting transfers between devices  13.1 us (25%)
  between operations  0.82 us (2%)
    all_to_all x1, blocking collectives, on_device(): gathered = lax.all_to_all(parts, ('gx', 'gy'), 0, 0)  22.2 us
    ppermute x2, starting transfers between devices, swap(): lax.ppermute(far, axis, [(i, (i - 1 + 2 * (i % 2)) % count) for i in rang...  9.25 us
    pallas_call x1, Pallas kernels, on_device(): pl.pallas_call(inner_forward_kernel, out_shape=[array(2, STRIP, cols), ar...  4.58 us
    pallas_call x1, Pallas kernels, on_device(): pl.pallas_call(inner_backward_kernel, out_shape=[array(rows, cols), array...  4.47 us
    pallas_call x1, Pallas kernels, on_device(): pl.pallas_call(frame_kernel, out_shape=[array(rows, cols), array(rows, co...  4.41 us
    ppermute x2, starting transfers between devices, swap(): lax.ppermute(near, axis, [(i, i + 1 - 2 * (i % 2)) for i in range(count)])  3.84 us
    pallas_call x1, Pallas kernels, on_device(): pl.pallas_call(edge_kernel, out_shape=[array(FIELDS * EDGE, rows)] * 2, i...  2.14 us
  transfers between devices with their start and end apart: 4, of which 0 were waited for; matrix products, arithmetic and copies ran while one was open for 0% of the time, Pallas kernels for 17%

profile of v5, /device:TPU:1, one launch (start us, length us, event | category | flops | bytes accessed | tf_op | source)
XLA Modules:
  0.0 52.6 jit_solution(10574291849904516629)
XLA Ops:
  0.6 0.0 copy-start.2
  0.6 0.0 copy-start.3
  0.7 0.0 copy-start.4
  0.7 0.0 copy-start
  0.7 0.0 copy-start.1
  0.7 0.0 copy-start.7
  0.7 0.0 copy-start.8
  0.7 0.0 copy-start.9
  0.7 2.1 %edges.1 = (f32[32,128]{1,0:T(8,128)}, f32[32,128]{1,0:T(8,128)}) custom-call(f32[128,512]{1,0:T(8,128)} %h_ref.3, f32[128,512]{1,0:T(8,128)} %x_ref.3, f32[128,512]{1,0:T(8,128)} %y_ref.3, s32[128,512]{1,0:T(8,128)} %wet_ref.3, s32[128,512]{1,0:T(8,128)} %class_ref.3), custom_call_target="tpu_custom_call" | custom-call | flops 1000000000 | bytes 40000000 | tf_op jit(solution)/shard_map/edges/pallas_call | solution.py:712
  2.9 3.3 %collective-permute-start = (f32[32,128]{1,0:T(8,128)}, f32[32,128]{1,0:T(8,128)S(1)}, u32[]{:S(2)}, u32[]{:S(2)}) collective-permute-start(f32[32,128]{1,0:T(8,128)} %get-tuple-element.30.near_own), channel_id=1, source_target_pairs={{0,1},{1,0},{2,3},{3,2},{4,5},{5,4},{6,7},{7,6},{8,9},{9,8},{10,11... | collective-permute-start | bytes 49160 | tf_op jit(solution)/shard_map/ppermute | solution.py:698
  6.2 5.2 %collective-permute-start.1 = (f32[32,128]{1,0:T(8,128)}, f32[32,128]{1,0:T(8,128)S(1)}, u32[]{:S(2)}, u32[]{:S(2)}) collective-permute-start(f32[32,128]{1,0:T(8,128)} %get-tuple-element.31.far_own), channel_id=1, source_target_pairs={{0,15},{1,2},{2,1},{3,4},{4,3},{5,6},{6,5},{7,8},{8,7},{9,10},{10,... | collective-permute-start | bytes 49160 | tf_op jit(solution)/shard_map/ppermute | solution.py:699
  11.4 0.0 copy-done
  11.4 4.6 %inner_forward.1 = (f32[2,16,512]{2,1,0:T(8,128)S(1)}, f32[128,512]{1,0:T(8,128)S(1)}, f32[1,128]{1,0:T(1,128)S(1)}, f32[7,4,136,128]{3,2,1,0:T(8,128)S(1)}, f32...) custom-call(f32[128,512]{1,0:T(8,128)S(1)} %copy-done, ...), custom_call_target="tpu_custom_call" | custom-call | flops 13107200 | bytes 1572864 | tf_op jit(solution)/shard_map/inner_forward/pallas_call | solution.py:730
  16.0 0.0 collective-permute-done.near_in.near_col
  16.0 0.0 collective-permute-done.1.far_in.far_col
  16.0 0.2 corners.1
  16.2 0.5 collective-permute-start.2
  16.7 4.1 %collective-permute-start.3 = (f32[16,640]{1,0:T(8,128)S(1)}, f32[16,640]{1,0:T(8,128)S(1)}, u32[]{:S(2)}, u32[]{:S(2)}) collective-permute-start(f32[16,640]{1,0:T(8,128)S(1)} %get-tuple-element.35), channel_id=1, source_target_pairs={{0,240},{16,32},{32,16},{48,64},{64,48},{80,96},{96,80},{112,128},... | collective-permute-start | bytes 122888 | tf_op jit(solution)/shard_map/ppermute | solution.py:699
  20.8 4.5 %inner_backward.1 = (f32[128,512]{1,0:T(8,128)S(1)}, f32[1,128]{1,0:T(1,128)S(1)}) custom-call(f32[7,4,136,128]{3,2,1,0:T(8,128)S(1)} %get-tuple-element.22.refs_0_, f32[7,4,136,128]{3,2,1,0:T(8,128)S(1)} %get-tuple-element.23.refs_1_, f32[2,4,136,128]{3,2,1,0:T(8,128)S(1)} %get-tuple-element.24.refs_2_, f32[4,4,136,128]{3,2,1,0:T(8,128)S(1)} %get-tuple-element.25.refs_3_, ...), custom_call_target="tpu_custom_call" | custom-call | flops 19660800 | bytes 1572864 | tf_op jit(solution)/shard_map/inner_backward/pallas_call | solution.py:748
  25.3 0.0 collective-permute-done.2.near_row
  25.3 0.0 collective-permute-done.3.far_row
  25.3 4.4 %frame.1 = (f32[128,512]{1,0:T(8,128)}, f32[128,512]{1,0:T(8,128)}, f32[256,128]{1,0:T(8,128)S(1)}) custom-call(f32[128,512]{1,0:T(8,128)S(1)} %copy-done, f32[128,512]{1,0:T(8,128)S(1)} %copy-done.1, f32[128,512]{1,0:T(8,128)S(1)} %copy-done.2, s32[128,512]{1,0:T(8,128)S(1)} %copy-done.3, s32[128,512]{1,0:T(8,128)S(1)} %copy-done.4, f32[8]{0:T(128)S(1)} %copy-done.9, ...), custom_call_target="tpu_custom_call" | custom-call | tf_op jit(solution)/shard_map/frame/pallas_call | solution.py:759
  29.7 22.2 %all_to_all.11 = f32[256,1,128]{2,1,0:T(1,128)S(1)} all-to-all(f32[256,1,128]{2,1,0:T(1,128)S(1)} %bitcast.8), channel_id=1, replica_groups=mesh['gx'=16,'gy'=16] {'gx','gy'}, dimensions={0} | all-to-all | bytes 262144 | tf_op jit(solution)/shard_map/all_to_all | solution.py:776
  51.9 0.7 %total.1 = f32[2,64]{1,0:T(2,128)} custom-call(f32[256,128]{1,0:T(8,128)S(1)} %bitcast.7), custom_call_target="tpu_custom_call" | custom-call | tf_op jit(solution)/shard_map/total/pallas_call | solution.py:777
  (11 shorter events, 0.0 us)
Async XLA Ops:
  0.6 10.7 %copy-start.2 = (f32[128,512]{1,0:T(8,128)S(1)}, f32[128,512]{1,0:T(8,128)}, u32[]{:S(2)}) copy-start(f32[128,512]{1,0:T(8,128)} %y_ref.3) | copy-start | bytes 786436
  0.6 10.7 %copy-start.3 = (s32[128,512]{1,0:T(8,128)S(1)}, s32[128,512]{1,0:T(8,128)}, u32[]{:S(2)}) copy-start(s32[128,512]{1,0:T(8,128)} %wet_ref.3) | copy-start | bytes 786436
  0.7 10.7 %copy-start.4 = (s32[128,512]{1,0:T(8,128)S(1)}, s32[128,512]{1,0:T(8,128)}, u32[]{:S(2)}) copy-start(s32[128,512]{1,0:T(8,128)} %class_ref.3) | copy-start | bytes 786436
  0.7 10.7 %copy-start = (f32[128,512]{1,0:T(8,128)S(1)}, f32[128,512]{1,0:T(8,128)}, u32[]{:S(2)}) copy-start(f32[128,512]{1,0:T(8,128)} %h_ref.3) | copy-start | bytes 786436
  0.7 10.7 %copy-start.1 = (f32[128,512]{1,0:T(8,128)S(1)}, f32[128,512]{1,0:T(8,128)}, u32[]{:S(2)}) copy-start(f32[128,512]{1,0:T(8,128)} %x_ref.3) | copy-start | bytes 786436
  0.7 10.7 %copy-start.7 = (s32[64]{0:T(128)S(1)}, s32[64]{0:T(128)}, u32[]{:S(2)}) copy-start(s32[64]{0:T(128)} %param.14) | copy-start | bytes 772
  0.7 10.7 %copy-start.8 = (f32[64,2]{0,1:T(2,128)S(1)}, f32[64,2]{0,1:T(2,128)}, u32[]{:S(2)}) copy-start(f32[64,2]{0,1:T(2,128)} %param.15) | copy-start | bytes 1540
  0.7 10.7 %copy-start.9 = (f32[8]{0:T(128)S(1)}, f32[8]{0:T(128)}, u32[]{:S(2)}) copy-start(f32[8]{0:T(128)} %rates_ref.3) | copy-start | bytes 100
  2.9 13.1 %collective-permute-start = (f32[32,128]{1,0:T(8,128)}, f32[32,128]{1,0:T(8,128)S(1)}, u32[]{:S(2)}, u32[]{:S(2)}) collective-permute-start(f32[32,128]{1,0:T(8,128)} %get-tuple-element.30.near_own), channel_id=1, source_target_pairs={{0,1},{1,0},{2,3},{3,2},{4,5},{5,4},{6,7},{7,6},{8,9},{9,8},{10,11... | collective-permute-start | bytes 49160 | tf_op jit(solution)/shard_map/ppermute | solution.py:698
  6.2 9.8 %collective-permute-start.1 = (f32[32,128]{1,0:T(8,128)}, f32[32,128]{1,0:T(8,128)S(1)}, u32[]{:S(2)}, u32[]{:S(2)}) collective-permute-start(f32[32,128]{1,0:T(8,128)} %get-tuple-element.31.far_own), channel_id=1, source_target_pairs={{0,15},{1,2},{2,1},{3,4},{4,3},{5,6},{6,5},{7,8},{8,7},{9,10},{10,... | collective-permute-start | bytes 49160 | tf_op jit(solution)/shard_map/ppermute | solution.py:699
  16.2 9.1 %collective-permute-start.2 = (f32[16,640]{1,0:T(8,128)S(1)}, f32[16,640]{1,0:T(8,128)S(1)}, u32[]{:S(2)}, u32[]{:S(2)}) collective-permute-start(f32[16,640]{1,0:T(8,128)S(1)} %get-tuple-element.34), channel_id=1, source_target_pairs={{0,16},{16,0},{32,48},{48,32},{64,80},{80,64},{96,112},{112,96},{1... | collective-permute-start | bytes 122888 | tf_op jit(solution)/shard_map/ppermute | solution.py:698
  16.7 8.6 %collective-permute-start.3 = (f32[16,640]{1,0:T(8,128)S(1)}, f32[16,640]{1,0:T(8,128)S(1)}, u32[]{:S(2)}, u32[]{:S(2)}) collective-permute-start(f32[16,640]{1,0:T(8,128)S(1)} %get-tuple-element.35), channel_id=1, source_target_pairs={{0,240},{16,32},{32,16},{48,64},{64,48},{80,96},{96,80},{112,128},... | collective-permute-start | bytes 122888 | tf_op jit(solution)/shard_map/ppermute | solution.py:699
  20.8 4.5 %copy-start.5 = (f32[32,128]{1,0:T(8,128)S(1)}, f32[32,128]{1,0:T(8,128)}, u32[]{:S(2)}) copy-start(f32[32,128]{1,0:T(8,128)} %get-tuple-element.30.near_own) | copy-start | bytes 49156
  20.8 4.5 %copy-start.6 = (f32[32,128]{1,0:T(8,128)S(1)}, f32[32,128]{1,0:T(8,128)}, u32[]{:S(2)}) copy-start(f32[32,128]{1,0:T(8,128)} %get-tuple-element.31.far_own) | copy-start | bytes 49156
